TPU v7x, 32 devices: a whole 2x2x4 slice. The times are simulated.
32 devices in a mesh: seq: 8 (over z, y), batch: 2 (over core), head: 2 (over x).
Axes of the slice: x: 2, y: 2, z: 4, core: 2. Of those that a mesh axis runs over, the one named last changes fastest.
Arguments:
- hidden_in: bfloat16 [2, 1024, 2048], P('batch', 'seq'), may hold values from -6 to 6
- log_decay: float32 [2, 8, 1024], P('batch', 'head', 'seq'), may hold values from -1 to 0, as said below
- out_grad: bfloat16 [2, 1024, 2048], P('batch', 'seq'), may hold values from -6 to 6
- ln1_gain: bfloat16 [2048], P(('seq', 'batch')), may hold values from 0.25 to 1.75
- ln1_bias: bfloat16 [2048], P(('seq', 'batch')), may hold values from -2 to 2
- w_query: bfloat16 [2048, 2048], P(('seq', 'batch'), 'head'), may hold values from -0.125 to 0.125
- w_key: bfloat16 [2048, 2048], P(('seq', 'batch'), 'head'), may hold values from -0.125 to 0.125
- w_value: bfloat16 [2048, 4096], P(('seq', 'batch'), 'head'), may hold values from -0.125 to 0.125
- w_gate: bfloat16 [2048, 4096], P(('seq', 'batch'), 'head'), may hold values from -0.125 to 0.125
- w_out: bfloat16 [4096, 2048], P('head', ('seq', 'batch')), may hold values from -0.1875 to 0.1875
- ln2_gain: bfloat16 [2048], P(('seq', 'batch')), may hold values from 0.25 to 1.75
- ln2_bias: bfloat16 [2048], P(('seq', 'batch')), may hold values from -2 to 2
- mlp_gate: bfloat16 [2048, 4096], P(('seq', 'batch'), 'head'), may hold values from -0.125 to 0.125
- mlp_up: bfloat16 [2048, 4096], P(('seq', 'batch'), 'head'), may hold values from -0.125 to 0.125
- mlp_down: bfloat16 [4096, 2048], P('head', ('seq', 'batch')), may hold values from -0.1875 to 0.1875
Outputs:
- hidden_out: bfloat16 [2, 1024, 2048], P('batch', 'seq')
- grad_in: float32 [2, 1024, 2048], P('batch', 'seq')
- grad_ln1_gain: float32 [2048], P(('seq', 'batch'))
- grad_ln1_bias: float32 [2048], P(('seq', 'batch'))
- grad_query: float32 [2048, 2048], P(('seq', 'batch'), 'head')
- grad_key: float32 [2048, 2048], P(('seq', 'batch'), 'head')
- grad_value: float32 [2048, 4096], P(('seq', 'batch'), 'head')
- grad_gate: float32 [2048, 4096], P(('seq', 'batch'), 'head')
- grad_out: float32 [4096, 2048], P('head', ('seq', 'batch'))
- grad_ln2_gain: float32 [2048], P(('seq', 'batch'))
- grad_ln2_bias: float32 [2048], P(('seq', 'batch'))
- grad_mlp_gate: float32 [2048, 4096], P(('seq', 'batch'), 'head')
- grad_mlp_up: float32 [2048, 4096], P(('seq', 'batch'), 'head')
- grad_mlp_down: float32 [4096, 2048], P('head', ('seq', 'batch'))
Inputs may be any that keep to these rules, and one draw needn't show every extreme that they name: `log_decay`: every entry is negative; each head keeps its own rate per sequence, varied from position to position.
All inputs are finite; a program needn't handle non-finite values.
Results may differ from a plain program's by a relative error of at most 0.015.
Values may be sent and summed in bfloat16 or wider, within the bound.
No kernel may reach another device: no remote copies, remote signals or barrier semaphores. Data moves between devices by JAX's collectives and lax.ppermute only.
A program may use at most 320 MiB of HBM per device.

v0:
```python
import jax
import jax.numpy as jnp
from jax import lax
from jax.experimental import pallas as pl
from jax.experimental.pallas import tpu as pltpu
from jax.sharding import Mesh
from jax.sharding import PartitionSpec as P

DK = 256
DV = 512

epsilon = 1e-05
f32 = jnp.float32
bf16 = jnp.bfloat16
VMEM_LIMIT = 12 * 1024 * 1024

ORDER = (0, 3, 1, 2)


def swap(values, axis, k):
    count = lax.axis_size(axis)
    return lax.ppermute(values, axis, [(i, i ^ k) for i in range(count)])


def pick(values, index, axis):
    return lax.dynamic_index_in_dim(values, index, axis, keepdims=False)


def tie(*values):
    return lax.optimization_barrier(values)


def after(values, *others):
    return tie(values, others)[0]


def matmul(values, weight):
    return jnp.dot(values, weight, preferred_element_type=f32)


def matmul_t(values, weight):
    return lax.dot_general(values, weight, (((1,), (1,)), ((), ())), preferred_element_type=f32)


def outer_sum(values, other):
    return lax.dot_general(values, other, (((0,), (0,)), ((), ())), preferred_element_type=f32)


def normalize(values):
    center = values - jnp.mean(values, axis=-1, keepdims=True)
    rstd = lax.rsqrt(jnp.mean(center * center, axis=-1, keepdims=True) + epsilon)
    return center * rstd, rstd


def norm_back(scaled_grad, scaled, rstd):
    return rstd * (
        scaled_grad
        - jnp.mean(scaled_grad, axis=-1, keepdims=True)
        - scaled * jnp.mean(scaled_grad * scaled, axis=-1, keepdims=True)
    )


def rotate(values, cosines, sines):
    half_dim = values.shape[-1] // 2
    first_half = values[..., :half_dim]
    second_half = values[..., half_dim:]
    return jnp.concatenate(
        [first_half * cosines - second_half * sines, first_half * sines + second_half * cosines],
        axis=-1,
    )


SMEM = pl.BlockSpec(memory_space=pltpu.SMEM)
WHOLE = pl.BlockSpec(memory_space=pltpu.VMEM)
PARAMS = pltpu.CompilerParams(vmem_limit_bytes=VMEM_LIMIT)


def call(kernel, name, shapes, *operands, grid=None, scratch=()):
    many = isinstance(shapes, list)
    return pl.pallas_call(
        kernel,
        grid=() if grid is None else grid,
        out_shape=shapes,
        in_specs=[SMEM] + [WHOLE] * (len(operands) - 1),
        out_specs=[WHOLE] * len(shapes) if many else WHOLE,
        scratch_shapes=list(scratch),
        compiler_params=PARAMS,
        name=name,
    )(*operands)


def shape(dims, dtype):
    return jax.ShapeDtypeStruct(tuple(dims), dtype)


def cut_halves(where, values, heads):
    block, width = values.shape
    part = block // heads

    def kernel(where_ref, ref, own, other):
        for out, half in ((own, where_ref[3]), (other, 1 - where_ref[3])):
            out[...] = ref[pl.ds(pl.multiple_of(half * part, part), part), :]

    return call(kernel, "cut_halves", [shape((part, width), values.dtype)] * 2, where, values)


def join_halves(where, own, other):
    part, width = own.shape

    def kernel(where_ref, own_ref, other_ref, out):
        for ref, half in ((own_ref, where_ref[3]), (other_ref, 1 - where_ref[3])):
            out[pl.ds(pl.multiple_of(half * part, part), part), :] = ref[...]

    return call(kernel, "join_halves", shape((2 * part, width), own.dtype), where, own, other)


def cut_heads(where, totals, first=0):
    nz, rows, _ = totals[0].shape
    width = sum(total.shape[2] for total in totals)

    def kernel(where_ref, *refs):
        ins, outs = refs[: len(totals)], refs[len(totals) :]
        targets = [outs[k] for k in range(nz)] if not first else steps(outs, first)
        for k in range(nz):
            at = 0
            for ref in ins:
                cols = ref.shape[2]
                targets[k][:, at : at + cols] = ref[where_ref[0] ^ k].astype(bf16)
                at += cols

    shapes = [shape((rows, width), bf16)] * nz
    if first:
        shapes = shapes[:2] + [shape((2, rows, width), bf16)]
    return call(kernel, "cut_heads", shapes, where, *totals)


def steps(refs, first):
    stay, second, firsts = refs
    return {0: stay, 4 - first: second, first: firsts.at[0], 2: firsts.at[1]}


def pack_weights(where, weights, nz, rows, extras=None, first=0):
    widths = [w.size // rows // nz for w in weights]
    total = sum(widths)
    count = 0
    if extras:
        gains, decays = extras
        block = decays.shape[1]
        extras = (jnp.pad(gains, ((0, 0), (0, total - gains.shape[1]))), decays)
        count = EXTRA

    def kernel(where_ref, *refs):
        ins, rest = refs[: len(weights)], refs[len(weights) :]
        outs = steps(rest, first) if first else rest[-nz:]
        for k in range(nz):
            target = where_ref[0] ^ k
            at = 0
            for ref, width in zip(ins, widths):
                start = pl.multiple_of(target * width, width)
                if ref.shape[0] == rows:
                    piece = ref[:, pl.ds(start, width)]
                else:
                    piece = ref[pl.ds(start, width), :].astype(f32).T.astype(bf16)
                outs[k][:rows, at : at + width] = piece
                at += width
            if extras:
                line = lax.broadcasted_iota(jnp.int32, (EXTRA, 1), 0)
                gain_rows = jnp.where(line == 0, rest[0][...].astype(f32), 0.0)
                parts = gain_rows[:, :block]
                left = rest[1][pl.ds(target, 1), :]
                for number in range(1, 4):
                    part = left.astype(bf16).astype(f32)
                    parts = jnp.where(line == number, part, parts)
                    left = left - part
                outs[k][rows:, :] = gain_rows.astype(bf16)
                outs[k][rows:, :block] = parts.astype(bf16)

    shapes = [shape((rows + count, total), bf16)] * nz
    if first:
        shapes = shapes[:2] + [shape((2, rows, total), bf16)]
    return call(kernel, "pack_weights", shapes, where, *weights, *(extras or ()))


def unpack_grads(where, pieces, outs):
    nz = len(pieces)
    rows = pieces[0].shape[0]

    def kernel(where_ref, *refs):
        ins, results = refs[:nz], refs[nz:]
        for k in range(nz):
            target = where_ref[0] ^ k
            at = 0
            for ref, (width, turned) in zip(results, outs):
                to = pl.ds(pl.multiple_of(target * width, width), width)
                piece = ins[k][:, at : at + width].astype(f32)
                if turned:
                    ref[to, :] = piece.T
                else:
                    ref[:, to] = piece
                at += width

    shapes = [shape((nz * w, rows) if turned else (rows, nz * w), f32) for w, turned in outs]
    return call(kernel, "unpack_grads", shapes, where, *pieces)


EXTRA = 16


def assemble(where, parts, ny, nb, widths, extra=0, block=0):
    nz, rows, _ = parts[0][0].shape
    rows -= extra
    count = nz * ny * nb
    total = sum(widths)
    sizes = [len(part) for part in parts]
    aligned = rows % 128 == 0

    def kernel(where_ref, *refs):
        ins, outs = refs[: sum(sizes)], refs[sum(sizes) :]
        for ky in range(ny):
            for kb in range(nb):
                pieces, ins = ins[: sizes[ky * nb + kb]], ins[sizes[ky * nb + kb] :]
                for kz in range(nz):
                    place = (where_ref[0] ^ kz) * ny + (where_ref[1] ^ ky)
                    device = place * nb + (where_ref[2] ^ kb)
                    at = pl.multiple_of(device * rows, rows)
                    column = 0
                    for piece in pieces:
                        cols = piece.shape[-1]
                        start = 0
                        for out, width in zip(outs, widths):
                            low, high = max(start, column), min(start + width, column + cols)
                            if low < high:
                                out[pl.ds(at, rows), low - start : high - start] = piece[
                                    kz, :rows, low - column : high - column
                                ]
                            start += width
                        column += cols
                    if extra:
                        tail = pieces[0][kz, rows:, :].astype(f32)
                        if aligned:
                            for number in range(4):
                                gain = tail[:1, number * rows : (number + 1) * rows]
                                outs[-2][number : number + 1, pl.ds(at, rows)] = gain
                        else:
                            outs[-2][pl.ds(device, 1), :] = tail[:1]
                        if kb == 0:
                            decay = (tail[1:2] + tail[2:3]) + tail[3:4]
                            outs[-1][pl.ds(place, 1), :] = decay[:, :block]

    shapes = [shape((count * rows, width), bf16) for width in widths]
    if extra:
        shapes.append(shape((4, count * rows) if aligned else (count, total), f32))
        shapes.append(shape((nz * ny, block), f32))
    outs = list(call(kernel, "assemble", shapes, where, *[p for part in parts for p in part]))
    if extra and not aligned:
        gains = outs[-2][:, : 4 * rows].reshape(count, 4, rows)
        outs[-2] = gains.transpose(1, 0, 2).reshape(4, count * rows)
    return outs


def row_groups(where, left, sizes):
    nz, ny, nb = sizes
    groups = left.reshape(left.shape[0], nz, ny, nb, -1)
    groups = jnp.take(groups, jnp.arange(ny) ^ where[1], axis=2)
    groups = jnp.take(groups, jnp.arange(nb) ^ where[2], axis=3)
    return groups.transpose(0, 3, 2, 1, 4).reshape(left.shape)


def weight_grads(where, lefts, rights, sizes, widths=None, got=None):
    nz, ny, nb = sizes
    width = lefts[0].shape[1]
    rows = width // (nz * ny * nb)
    group = nz * rows
    rights = [right if isinstance(right, tuple) else (right, 0, right.shape[1]) for right in rights]
    ranges = [right[1:] for right in rights]
    rights = [right[0] for right in rights]
    total = sum(high - low for low, high in ranges)
    kb = 1 if got is None else 0
    aligned = rows % 128 == 0
    if not aligned:
        lefts = [row_groups(where, left, sizes) for left in lefts]

    def columns(where_ref, left, step):
        if not aligned:
            return left[:, pl.ds(pl.multiple_of((kb * ny + step) * group, group), group)]
        tiles = []
        for z in range(nz):
            start = ((z * ny + (where_ref[1] ^ step)) * nb + (where_ref[2] ^ kb)) * rows
            tiles.append(left[:, pl.ds(pl.multiple_of(start, rows), rows)])
        return jnp.concatenate(tiles, axis=1)

    def kernel(where_ref, *refs):
        ins, rest = refs[: len(lefts)], refs[len(lefts) :]
        others, rest = rest[: len(rights)], rest[len(rights) :]
        step = pl.program_id(0)
        values = []
        for left, right, (low, high) in zip(ins, others, ranges):
            values.append(dot(columns(where_ref, left, step), right[:, low:high], TN))
        if got is None:
            at = 0
            for value in values:
                rest[0][:, at : at + value.shape[1]] = value.astype(bf16)
                at += value.shape[1]
            return
        value = jnp.concatenate(values, axis=1) + rest[0][...].astype(f32)
        keeps, sends = rest[1 : 1 + len(widths)], rest[1 + len(widths) :]
        at = 0
        for keep, send, cols in zip(keeps, sends, widths):
            part = value[:, at : at + cols]
            send[...] = part.astype(bf16)

            @pl.when(step == 0)
            def _():
                keep[...] = part

            at += cols

    moving = lambda cols: pl.BlockSpec((group, cols), lambda i: (i, 0))
    if got is None:
        specs = moving(total)
        shapes = shape((ny * group, total), bf16)
    else:
        specs = [pl.BlockSpec((group, cols), lambda i: (0, 0)) for cols in widths]
        specs += [moving(cols) for cols in widths]
        shapes = [shape((group, cols), f32) for cols in widths]
        shapes += [shape((ny * group, cols), bf16) for cols in widths]
    outs = pl.pallas_call(
        kernel,
        grid=(ny,),
        out_shape=shapes,
        in_specs=[SMEM]
        + [WHOLE] * (len(lefts) + len(rights))
        + ([] if got is None else [moving(total)]),
        out_specs=specs,
        compiler_params=PARAMS,
        name="weight_grads",
    )(where, *lefts, *rights, *(() if got is None else (got,)))
    return outs if got is None else (outs[: len(widths)], outs[len(widths) :])


def place_rows(where, pieces, gains=None):
    width = pieces[0].shape[-1]
    tokens = sum(piece.shape[0] for piece in pieces)

    def kernel(where_ref, *refs):
        ins, full = refs[: len(pieces)], refs[-1]
        at = 0
        for ref in ins:
            values = ref[...]
            if gains is not None:
                values, _ = normalize(values.astype(f32))
                params = refs[-2]
                values = (values * params[0:1, :] + params[1:2, :]).astype(bf16)
            full[at : at + ref.shape[0], :] = values
            at += ref.shape[0]

    more = () if gains is None else (gains,)
    return call(kernel, "place_rows", shape((tokens, width), bf16), where, *pieces, *more)


LOW = 16


def write_message(ref, values, part, columns=slice(None)):
    count = values.shape[0]
    high = values.astype(bf16)
    ref[:count, columns] = high
    low = values - high.astype(f32)
    line = lax.broadcasted_iota(jnp.int32, (LOW, 1), 0)
    rows = jnp.zeros((LOW, values.shape[1]), f32)
    for number in range(count // part):
        rows = jnp.where(line == number, low[number * part : number * part + 1], rows)
    ref[count:, columns] = rows.astype(bf16)


def read_message(ref, part):
    count = ref.shape[0] - LOW
    values = ref[:count, :].astype(f32)
    low = ref[count:, :].astype(f32)
    line = lax.broadcasted_iota(jnp.int32, (count, 1), 0)
    for number in range(count // part):
        values = values + jnp.where(line == number * part, low[number : number + 1], 0.0)
    return values


def far_messages(where, values, weight, part):
    half = values.shape[0] // 2
    quarter = half // 2
    width, depth = weight.shape
    step = width // 4

    def kernel(where_ref, value_ref, weight_ref, second, first):
        out = dot(value_ref[half:, :], weight_ref[...], NT)
        write_message(second, out[quarter:], part)
        write_message(first, out[:quarter], part)

    return pl.pallas_call(
        kernel,
        grid=(4,),
        out_shape=[shape((quarter + LOW, width), bf16)] * 2,
        in_specs=[SMEM, WHOLE, pl.BlockSpec((step, depth), lambda i: (i, 0))],
        out_specs=[pl.BlockSpec((quarter + LOW, step), lambda i: (0, i))] * 2,
        compiler_params=PARAMS,
        name="far_messages",
    )(where, values, weight)


def pass_message(where, near, got, part):
    def kernel(where_ref, near_ref, got_ref, out):
        write_message(out, near_ref[...] + read_message(got_ref, part), part)

    return call(kernel, "pass_message", shape(got.shape, bf16), where, near, got)


def keep_message(where, near, got_far, got, part):
    width = near.shape[1]

    def kernel(where_ref, near_ref, far_ref, got_ref, keep, out):
        total = near_ref[...] + read_message(far_ref, part) + read_message(got_ref, part)
        keep[...] = total[:part]
        write_message(out, total[part:], part)

    shapes = [shape((part, width), f32), shape((part + LOW, width), bf16)]
    return call(kernel, "keep_message", shapes, where, near, got_far, got)


def second_norm(where, inputs, keep, got, gains, part):
    width = keep.shape[1]

    def kernel(where_ref, in_ref, keep_ref, got_ref, gain_ref, middle, scaled, rstd, out):
        total = in_ref[...].astype(f32) + (keep_ref[...] + read_message(got_ref, part))
        middle[...] = total
        normed, factor = normalize(total)
        scaled[...] = normed
        rstd[...] = factor
        out[...] = (normed * gain_ref[2:3, :] + gain_ref[3:4, :]).astype(bf16)

    full = shape((part, width), f32)
    shapes = [full, full, shape((part, 1), f32), shape((part, width), bf16)]
    return call(kernel, "second_norm", shapes, where, inputs, keep, got, gains)


def second_norm_back(where, grad, keep, got, gains, scaled, rstd, part):
    width = keep.shape[1]

    def kernel(where_ref, g_ref, keep_ref, got_ref, gain_ref, scaled_ref, rstd_ref, two, mid, out):
        total = keep_ref[...] + read_message(got_ref, part)
        two[...] = total
        back = norm_back(total * gain_ref[2:3, :], scaled_ref[...], rstd_ref[...])
        back = g_ref[...].astype(f32) + back
        mid[...] = back
        out[...] = back.astype(bf16)

    full = shape((part, width), f32)
    shapes = [full, full, shape((part, width), bf16)]
    operands = (where, grad, keep, got, gains, scaled, rstd)
    return call(kernel, "second_norm_back", shapes, *operands)


def slot_of(k):
    return (((k & 1) ^ (k >> 1)) << 1) | (k >> 1)


def natural(ref, slot, flip, columns=slice(None)):
    first = ref[flip, slot, :, columns]
    second = ref[1 - flip, slot, :, columns]
    return jnp.concatenate([first, second], axis=0)


def choose(refs, ky, slot, flip, columns=slice(None)):
    values = natural(refs[0], slot, flip, columns)
    for k in range(1, len(refs)):
        values = jnp.where(ky == k, natural(refs[k], slot, flip, columns), values)
    return values


def dot(left, right, dims):
    return lax.dot_general(left, right, (dims, ((), ())), preferred_element_type=f32)


NN, NT, TN = ((1,), (0,)), ((1,), (1,)), ((0,), (0,))


def decays_of(row):
    block = row.shape[-1]
    at = lax.broadcasted_iota(jnp.int32, (block, block), 0)
    to = lax.broadcasted_iota(jnp.int32, (block, block), 1)
    turned = jnp.sum(jnp.where(at == to, row, 0.0), axis=1, keepdims=True)
    running = jnp.sum(jnp.where(at <= to, turned, 0.0), axis=0, keepdims=True)
    col = jnp.sum(jnp.where(at == to, running, 0.0), axis=1, keepdims=True)
    matrix = jnp.where(at >= to, jnp.exp(jnp.minimum(col - running, 0.0)), 0.0)
    return col, running[:, block - 1 :], matrix


def retention_forward(where, decays, keyvals, query_gate):
    ny = len(keyvals)
    halves, nz, part, _ = query_gate.shape

    def kernel(where_ref, decay_ref, *refs):
        kv_refs, (qg_ref, y_ref, n_ref, r_ref, s_ref, q_ref, state) = refs[:ny], refs[ny:]
        j = pl.program_id(0)

        @pl.when(j == 0)
        def _():
            state[...] = jnp.zeros_like(state)

        slot = slot_of((j // ny) ^ where_ref[0])
        ky = (j % ny) ^ where_ref[1]
        flip = where_ref[3]
        col, last, matrix = decays_of(decay_ref[pl.ds(j, 1), :])
        key = choose(kv_refs, ky, slot, flip, slice(0, DK))
        value = choose(kv_refs, ky, slot, flip, slice(DK, DK + DV))

        @pl.when(ky == 0)
        def _():
            q = natural(qg_ref, slot, flip, slice(0, DK)).astype(bf16)
            state_bf = state[...].astype(bf16)
            s_ref[slot] = state_bf
            weights = (dot(q, key, NT) * matrix).astype(bf16)
            out = dot(weights, value, NN) + jnp.exp(col) * dot(q, state_bf, NN)
            normed, rstd = normalize(out)
            g = natural(qg_ref, slot, flip, slice(DK, DK + DV))
            mixed = (g * jax.nn.sigmoid(g) * normed).astype(bf16)
            for half in range(2):
                rows = slice(half * part, (half + 1) * part)
                to = (1 - flip) if half else flip
                y_ref[to, slot] = mixed[rows]
                n_ref[to, slot] = normed[rows]
                r_ref[to, slot] = rstd[rows]
                q_ref[to, slot] = q[rows]

        key_tail = (key.astype(f32) * jnp.exp(last - col)).astype(bf16)
        state[...] = jnp.exp(last) * state[...] + dot(key_tail, value, TN)

    return call(
        kernel,
        "retention_forward",
        [
            shape((halves, nz, part, DV), bf16),
            shape((halves, nz, part, DV), f32),
            shape((halves, nz, part, 1), f32),
            shape((nz, DK, DV), bf16),
            shape((halves, nz, part, DK), bf16),
        ],
        where,
        decays,
        *keyvals,
        query_gate,
        grid=(nz * ny,),
        scratch=[pltpu.VMEM((DK, DV), f32)],
    )


def retention_backward(where, decays, keyval, queries, grads, states, cosines, sines, gate):
    ny = len(queries)
    halves, nz, part, _ = keyval.shape
    key_scale = DK ** (-0.5)

    def kernel(where_ref, decay_ref, *refs):
        q_refs, d_refs, rest = refs[:ny], refs[ny : 2 * ny], refs[2 * ny :]
        kv_ref, s_ref, cos_ref, sin_ref, gate_ref, kv_out, qg_out, state = rest
        step = pl.program_id(0)
        j = nz * ny - 1 - step

        @pl.when(step == 0)
        def _():
            state[...] = jnp.zeros_like(state)
            qg_out[:, :, :, DK:] = gate_ref[...]

        slot = slot_of((j // ny) ^ where_ref[0])
        ky = (j % ny) ^ where_ref[1]
        flip = where_ref[3]
        col, last, matrix = decays_of(decay_ref[pl.ds(j, 1), :])
        q = choose(q_refs, ky, slot, flip)
        grad = choose(d_refs, ky, slot, flip)
        entry = jnp.exp(col)

        @pl.when(ky == 0)
        def _():
            key = natural(kv_ref, slot, flip, slice(0, DK))
            value = natural(kv_ref, slot, flip, slice(DK, DK + DV))
            cos = natural(cos_ref, slot, flip)
            sin = natural(sin_ref, slot, flip)
            tail = jnp.exp(last - col)
            state_bf = state[...].astype(bf16)
            weights = (dot(q, key, NT) * matrix).astype(bf16)
            scores = (dot(grad, value, NT) * matrix).astype(bf16)
            grad_q = dot(scores, key, NN) + entry * dot(grad, s_ref[slot], NT)
            grad_k = dot(scores, q, TN) + tail * dot(value, state_bf, NT)
            grad_v = dot(weights, grad, TN) + tail * dot(key, state_bf, NN)
            grad_q = rotate(grad_q, cos, -sin).astype(bf16)
            grad_k = (rotate(grad_k, cos, -sin) * key_scale).astype(bf16)
            grad_v = grad_v.astype(bf16)
            for half in range(2):
                rows = slice(half * part, (half + 1) * part)
                to = (1 - flip) if half else flip
                kv_out[to, slot, :, :DK] = grad_k[rows]
                kv_out[to, slot, :, DK:] = grad_v[rows]
                qg_out[to, slot, :, :DK] = grad_q[rows]

        query_entry = (q.astype(f32) * entry).astype(bf16)
        state[...] = jnp.exp(last) * state[...] + dot(query_entry, grad, TN)

    return call(
        kernel,
        "retention_backward",
        [shape((halves, nz, part, DK + DV), bf16)] * 2,
        where,
        decays,
        *queries,
        *grads,
        keyval,
        states,
        cosines,
        sines,
        gate,
        grid=(nz * ny,),
        scratch=[pltpu.VMEM((DK, DV), f32)],
    )


def shards(
    hidden_in,
    log_decay,
    out_grad,
    ln1_gain,
    ln1_bias,
    w_query,
    w_key,
    w_value,
    w_gate,
    w_out,
    ln2_gain,
    ln2_bias,
    mlp_gate,
    mlp_up,
    mlp_down,
):
    nz, ny = lax.axis_size("row"), lax.axis_size("col")
    nb, nh = lax.axis_size("batch"), lax.axis_size("head")
    block, width = hidden_in.shape[1:]
    rows = ln1_gain.shape[0]
    part = block // nh
    tokens = nz * block
    half, quarter = tokens // 2, tokens // 4
    group = nz * rows
    sizes = (nz, ny, nb)
    where = jnp.stack([lax.axis_index(name) for name in ("row", "col", "batch", "head")])
    (where,) = tie(where.astype(jnp.int32))

    def trade(pieces, k):
        return swap(pieces[k], "row", k) if k else pieces[k]

    def over_col(own):
        return [own] + [swap(own, "col", k) for k in range(1, ny)]

    def over_batch(values):
        return [swap(value, "batch", 1) for value in values]

    def mirror(values):
        return swap(values, "head", 1)

    def pairs(own, other):
        return [(part,) for both in zip(own, other) for part in both]

    def split(values):
        return values.reshape(nh, nz, part, -1)

    def add(values, got):
        return values + got.astype(f32)

    def sum_col(keep, send):
        for k in range(1, ny):
            keep = add(keep, swap(send[k * group : (k + 1) * group], "col", k))
        return keep.reshape(nz, rows, -1)

    def reduce_far(*terms):
        far = sum(matmul_t(values[half:], weight) for values, weight in terms).astype(bf16)
        return far[quarter:], far[:quarter]

    def reduce_near(*terms):
        near = sum(matmul_t(values[:half], weight) for values, weight in terms)
        return near[quarter:], near[:quarter]

    def step_one(packed, first):
        return swap(packed[2], "row", first)

    def step_two(packed, got, first):
        return swap(jnp.stack([packed[1], got[1]]), "row", 4 - first)

    def in_order(packed, got, last, first):
        pieces = {0: packed[0], first: got[0], 4 - first: last[0], 2: last[1]}
        return [pieces[k] for k in range(4)]

    gains = jnp.concatenate([ln1_gain, ln1_bias, ln2_gain, ln2_bias])[None]
    own_in, other_in = cut_halves(where, hidden_in[0], nh)
    two_in = swap(own_in, "row", 3)
    kv = pack_weights(where, (w_key, w_value), nz, rows, (gains, log_decay[0]))
    kv = [trade(kv, k) for k in range(nz)]
    qg = pack_weights(where, (w_query, w_gate), nz, rows, first=1)
    qg_got = step_one(qg, 1)
    kv, two_in, qg_got, late_grad = tie(kv, two_in, qg_got, out_grad[0])
    kv = jnp.stack(kv)
    kv_cols, kv_mate = over_col(kv), swap(kv, "batch", 1)
    one_in = swap(jnp.concatenate([own_in, two_in]), "row", 1)
    qg_last = step_two(qg, qg_got, 1)
    own_grad, other_grad = cut_halves(where, late_grad, nh)
    half_dim = DK // 2
    freqs = 10000.0 ** (-jnp.arange(half_dim, dtype=f32) / half_dim)
    block_at = (jnp.array(ORDER, jnp.int32) ^ where[0:1]) * ny + where[1:2]
    half_at = jnp.arange(nh, dtype=jnp.int32) ^ where[3:4]
    positions = (
        block_at[None, :, None] * block + half_at[:, None, None] * part + jnp.arange(part)
    )
    angles = positions.astype(f32)[..., None] * freqs
    cosines, sines = jnp.cos(angles), jnp.sin(angles)
    out = pack_weights(where, (w_out,), nz, rows, first=3)
    kv_cols, kv_mate, one_in, qg_last, own_grad, out, cosines, sines = tie(
        kv_cols, kv_mate, one_in, qg_last, own_grad, out, cosines, sines
    )
    kv_mates = [kv_mate] + over_batch(kv_cols[1:])
    mirror_in = mirror(jnp.concatenate([two_in, one_in]))
    qg_cols = over_col(jnp.stack(in_order(qg, qg_got, qg_last, 1)))
    two_grad = swap(own_grad, "row", 3)
    out_got = step_one(out, 3)
    feed = pack_weights(where, (mlp_gate, mlp_up, mlp_down), nz, rows)
    kv_mates, mirror_in, qg_cols, two_grad, out_got, feed = tie(
        kv_mates, mirror_in, qg_cols, two_grad, out_got, feed
    )
    kv_w, gains, decays = assemble(
        where, pairs(kv_cols, kv_mates), ny, nb, (DK + DV,), EXTRA, block
    )

    first_bf = place_rows(where, (own_in, two_in, one_in, other_in, mirror_in), gains)
    key_scale = DK ** (-0.5)
    projected = split(matmul(first_bf, kv_w))
    key_bf = (rotate(projected[..., :DK], cosines, sines) * key_scale).astype(bf16)
    keyval = jnp.concatenate([key_bf, projected[..., DK:].astype(bf16)], axis=-1)

    keyval, qg_cols, out_got, feed = tie(keyval, qg_cols, out_got, feed)
    keyvals = over_col(keyval)
    out_last = step_two(out, out_got, 3)
    feed_two = trade(feed, 2)
    (qg_w,) = assemble(where, pairs(qg_cols, over_batch(qg_cols)), ny, nb, (DK + DV,))
    projected = split(matmul(first_bf, qg_w))
    query_gate = jnp.concatenate(
        [rotate(projected[..., :DK], cosines, sines), projected[..., DK:]], axis=-1
    )
    keyvals, query_gate, out_last, feed_two = tie(keyvals, query_gate, out_last, feed_two)
    out_cols = over_col(jnp.stack(in_order(out, out_got, out_last, 3)))
    late_grad, late_two = after((own_grad, two_grad), keyvals)
    one_grad = swap(jnp.concatenate([late_grad, late_two]), "row", 1)
    mixed, normed, rstd, states, query = retention_forward(where, decays, keyvals, query_gate)
    mixed, out_cols, one_grad = tie(mixed, out_cols, one_grad)
    (out_w,) = assemble(where, pairs(out_cols, over_batch(out_cols)), ny, nb, (DV,))
    mixed_bf = mixed.reshape(tokens, DV)

    far = far_messages(where, mixed_bf, out_w, part)
    got = mirror(far[0])
    near = reduce_near((mixed_bf, out_w))
    late_feed = after(feed, far)
    feed_three, feed_one = trade(late_feed, 3), trade(late_feed, 1)
    got, near, feed_three, feed_one = tie(got, near, feed_three, feed_one)
    got_far = mirror(after(far[1], got))
    got = swap(pass_message(where, near[0], got, part), "row", 1)
    feed = jnp.stack([feed[0], feed_one, feed_two, feed_three])
    units = feed.shape[-1] // 3
    feed_gates = over_col(feed[..., :units])[1:]
    feed_mate = swap(feed, "batch", 1)
    got, got_far, feed_gates, feed_mate, feed = tie(got, got_far, feed_gates, feed_mate, feed)
    keep, send = keep_message(where, near[1], got_far, got, part)
    got = swap(send, "row", 3)
    late_feed, late_two, late_gates = after((feed, two_grad, feed_gates), keep)
    feed_ups = over_col(late_feed[..., units : 2 * units])[1:]
    mirror_two = mirror(late_two)
    gate_mates = over_batch(late_gates)
    got, feed_ups, mirror_two, gate_mates = tie(got, feed_ups, mirror_two, gate_mates)
    middle, scaled_two, rstd_two, own = second_norm(where, own_in, keep, got, gains, part)
    two = swap(own, "row", 3)
    late_feed, late_one, late_ups = after((feed, one_grad, feed_ups), own)
    feed_downs = over_col(late_feed[..., 2 * units :])[1:]
    mirror_one = mirror(late_one)
    up_mates = over_batch(late_ups)
    two, feed_downs, mirror_one, up_mates, query = tie(
        two, feed_downs, mirror_one, up_mates, query
    )
    pair = jnp.concatenate([own, two])
    one, mirror_pair = swap(pair, "row", 1), mirror(pair)
    down_mates = over_batch(after(feed_downs, pair))
    one, mirror_pair, down_mates, query = tie(one, mirror_pair, down_mates, query)
    mirror_last = mirror(one)
    queries = over_col(query)
    parts = [(feed,), (feed_mate,)]
    for three in zip(feed_gates, feed_ups, feed_downs, gate_mates, up_mates, down_mates):
        parts += [three[:3], three[3:]]
    up_w, down_w = assemble(where, after(parts, one), ny, nb, (2 * units, units))
    down_bf = place_rows(
        where, after((own_grad, two_grad, one_grad, other_grad, mirror_two, mirror_one), one)
    )
    mirror_last, up_w, down_w, down_bf, queries = tie(mirror_last, up_w, down_w, down_bf, queries)
    second_bf = place_rows(where, (pair, one, mirror_pair, mirror_last))

    up = matmul(second_bf, up_w)
    up_gate, up_lin = up[:, :units], up[:, units:]
    gelu_cdf = 0.5 * (1.0 + lax.erf(up_gate * (0.5**0.5)))
    gelu_val = up_gate * gelu_cdf
    gelu_slope = gelu_cdf + up_gate * jnp.exp(-0.5 * up_gate * up_gate) * (2.0 * jnp.pi) ** -0.5
    hidden_bf = (gelu_val * up_lin).astype(bf16)
    grad_hidden = matmul(down_bf, down_w)
    grad_upgate = (grad_hidden * up_lin * gelu_slope).astype(bf16)
    grad_uplin = (grad_hidden * gelu_val).astype(bf16)
    grad_up = jnp.concatenate([grad_upgate, grad_uplin], axis=-1)
    far = far_messages(where, grad_up, up_w, part)
    got = mirror(far[0])
    near = reduce_near((grad_up, up_w))
    lefts, rights = (second_bf, down_bf), (grad_up, hidden_bf)
    feed_far = weight_grads(where, lefts, rights, sizes)
    got, near, feed_far, hidden_bf = tie(got, near, feed_far, hidden_bf)
    got_far = mirror(after(far[1], got))
    got = swap(pass_message(where, near[0], got, part), "row", 1)
    feed_got = swap(feed_far, "batch", 1)
    feed_keeps, feed_sends = weight_grads(where, lefts, rights, sizes, (units,) * 3, feed_got)
    result_far = reduce_far((hidden_bf, down_w))
    got, got_far, feed_sends, result_far, hidden_bf = tie(
        got, got_far, feed_sends, result_far, hidden_bf
    )
    keep, send = keep_message(where, near[1], got_far, got, part)
    got = swap(send, "row", 3)
    result_got = mirror(result_far[0])
    result_near = reduce_near((hidden_bf, down_w))
    sums = [sum_col(feed_keeps[0], feed_sends[0])]
    got, result_got, result_near, sums, feed_sends = tie(
        got, result_got, result_near, sums, feed_sends
    )
    grad_two, grad_middle, own = second_norm_back(
        where, own_grad, keep, got, gains, scaled_two, rstd_two, part
    )
    own, feed_sends, result_got = tie(own, feed_sends, result_got)
    two = swap(own, "row", 3)
    sums.append(sum_col(feed_keeps[1], feed_sends[1]))
    result_got_far = mirror(after(result_far[1], own))
    result_got = swap(add(result_near[0], result_got).astype(bf16), "row", 1)
    two, sums, feed_sends, result_got_far, result_got = tie(
        two, sums, feed_sends, result_got_far, result_got
    )
    pair = jnp.concatenate([own, two])
    one, mirror_pair = swap(pair, "row", 1), mirror(pair)
    down_sum = sum_col(feed_keeps[2], feed_sends[2])
    wide_grads = cut_heads(where, sums)
    result_keep = add(add(result_near[1], result_got_far), result_got)
    result_send = result_keep[part:].astype(bf16)
    one, mirror_pair, down_sum, wide_grads, result_send = tie(
        one, mirror_pair, down_sum, wide_grads, result_send
    )
    mirror_last = mirror(one)
    wide_two, wide_one = trade(wide_grads, 2), trade(wide_grads, 1)
    down_grads = cut_heads(where, (down_sum,))
    mirror_last, wide_two, wide_one, down_grads = tie(mirror_last, wide_two, wide_one, down_grads)
    attn_bf = place_rows(where, (pair, one, mirror_pair, mirror_last))

    grp_norm, grp_rstd = normed.reshape(tokens, DV), rstd.reshape(tokens, 1)
    gate = query_gate.reshape(tokens, -1)[:, DK:]
    gate_sig = jax.nn.sigmoid(gate)
    gate_act = gate * gate_sig
    grad_mixed = matmul(attn_bf, out_w)
    grad_gate = (grad_mixed * grp_norm * (gate_sig * (1.0 + gate * (1.0 - gate_sig)))).astype(bf16)
    ret_bf = norm_back(grad_mixed * gate_act, grp_norm, grp_rstd).astype(bf16)
    ret_bf, wide_grads, down_grads = tie(split(ret_bf), wide_grads, down_grads)
    ret_all = over_col(ret_bf)
    wide_three, down_one = trade(wide_grads, 3), trade(down_grads, 1)
    lefts, rights = (first_bf, attn_bf), (grad_gate, mixed_bf)
    both_got = swap(weight_grads(where, lefts, rights, sizes), "batch", 1)
    both_keeps, both_sends = weight_grads(where, lefts, rights, sizes, (DV, DV), both_got)
    ret_all, wide_three, down_one, both_sends = tie(ret_all, wide_three, down_one, both_sends)
    grad_kv, grad_qg = retention_backward(
        where, decays, keyval, queries, ret_all, states, cosines, sines, split(grad_gate)
    )
    grad_kv, grad_qg = grad_kv.reshape(tokens, -1), grad_qg.reshape(tokens, -1)
    terms = ((grad_kv, kv_w), (grad_qg, qg_w))
    far = reduce_far(*terms)
    got = mirror(far[0])
    late_kv, late_qg, late_send, late_down = after((grad_kv, grad_qg, both_sends, down_grads), far)
    kvq = ((first_bf, first_bf), (late_kv, (late_qg, 0, DK)))
    kvq_got = swap(weight_grads(where, *kvq, sizes), "batch", 1)
    down_two, down_three = trade(late_down, 2), trade(late_down, 3)
    out_sum = sum_col(both_keeps[1], late_send[1])
    near = reduce_near(*terms)
    kvq_keeps, kvq_sends = weight_grads(where, *kvq, sizes, (DV, 2 * DK), kvq_got)
    got, near, down_two, down_three, kvq_sends, out_sum, both_sends, result_send = tie(
        got, near, down_two, down_three, kvq_sends, out_sum, both_sends, result_send
    )
    got_far = mirror(after(far[1], got))
    got = swap(add(near[0], got).astype(bf16), "row", 1)
    gate_sum = sum_col(both_keeps[0], both_sends[0])
    result_got = swap(result_send, "row", 3)
    got, got_far, gate_sum, result_got, kvq_sends = tie(
        got, got_far, gate_sum, result_got, kvq_sends
    )
    keep = add(add(near[1], got_far), got)
    got = swap(keep[part:].astype(bf16), "row", 3)
    result = (middle + add(result_keep[:part], result_got)).astype(bf16)
    result_other = mirror(result)
    kvq_first = sum_col(kvq_keeps[0], kvq_sends[0])
    both_pieces = cut_heads(where, (gate_sum, out_sum))
    got, result_other, kvq_first, kvq_sends, both_pieces = tie(
        got, result_other, kvq_first, kvq_sends, both_pieces
    )
    both_pieces = [trade(both_pieces, k) for k in range(nz)]
    kvq_second = sum_col(kvq_keeps[1], kvq_sends[1])
    grad_one = add(keep[:part], got)
    scaled_own, rstd_own = normalize(own_in.astype(f32))
    grad_in = grad_middle + norm_back(grad_one * gains[0:1], scaled_own, rstd_own)
    grad_in_other = mirror(grad_in)
    wide_pieces = (wide_grads[0], wide_one, wide_two, wide_three)
    grad_gates, grad_ups = unpack_grads(where, wide_pieces, ((units, False), (units, False)))
    down_pieces = (down_grads[0], down_one, down_two, down_three)
    (grad_downs,) = unpack_grads(where, down_pieces, ((units, True),))
    kvq_pieces = cut_heads(where, (kvq_first, kvq_second))
    norm_sums = jnp.stack(
        [
            jnp.sum(grad_one * scaled_own, axis=0),
            jnp.sum(grad_one, axis=0),
            jnp.sum(grad_two * scaled_two, axis=0),
            jnp.sum(grad_two, axis=0),
        ]
    )
    norm_sums = norm_sums + mirror(norm_sums)
    norm_sums = norm_sums.reshape(4, nz, ny, nb, rows)

    def sum_over(values, name, axis):
        me = lax.axis_index(name)
        summed = pick(values, me, axis)
        for k in range(1, lax.axis_size(name)):
            summed = summed + swap(pick(values, me ^ k, axis), name, k)
        return summed

    norm_sums = sum_over(sum_over(norm_sums, "batch", 3), "col", 2)
    both_pieces, kvq_pieces, grad_in_other, norm_sums, grad_gates, grad_ups, grad_downs = tie(
        both_pieces, kvq_pieces, grad_in_other, norm_sums, grad_gates, grad_ups, grad_downs
    )
    norm_sums = sum_over(norm_sums, "row", 1)
    kvq_pieces = [trade(kvq_pieces, k) for k in range(nz)]
    grad_g, grad_outs = unpack_grads(where, both_pieces, ((DV, False), (DV, True)))
    grad_k, grad_v, grad_q = unpack_grads(
        where, kvq_pieces, ((DK, False), (DV, False), (DK, False))
    )

    def join(own, other):
        return join_halves(where, own, other).reshape(1, block, width)

    return (
        join(result, result_other),
        join(grad_in, grad_in_other),
        norm_sums[0],
        norm_sums[1],
        grad_q,
        grad_k,
        grad_v,
        grad_g,
        grad_outs,
        norm_sums[2],
        norm_sums[3],
        grad_gates,
        grad_ups,
        grad_downs,
    )


def solution(mesh):
    seq = ("row", "col")
    tokens = P("batch", seq, None)
    params = P((*seq, "batch"))
    by_rows = P((*seq, "batch"), "head")
    by_cols = P("head", (*seq, "batch"))

    def run(*arrays):
        rows = arrays[1].shape[1] // mesh.shape["head"]
        sizes = (rows, mesh.shape["seq"] // rows, mesh.shape["batch"], mesh.shape["head"])
        order = [mesh.axis_names.index(n) for n in ("seq", "batch", "head")]
        fine = Mesh(
            mesh.devices.transpose(order).reshape(sizes), ("row", "col", "batch", "head")
        )
        weights = (by_rows, by_rows, by_rows, by_rows, by_cols)
        feeds = (by_rows, by_rows, by_cols)
        return jax.shard_map(
            shards,
            mesh=fine,
            in_specs=(
                tokens,
                P("batch", "head", seq),
                tokens,
                params,
                params,
                *weights,
                params,
                params,
                *feeds,
            ),
            out_specs=(tokens, tokens, params, params, *weights, params, params, *feeds),
            check_vma=False,
        )(*arrays)

    return run
```

profile of v0, /device:TPU:0, one launch (start us, length us, event | category | flops | bytes accessed | tf_op | source)
XLA Modules:
  0.0 510.7 jit_solution(4158359297406596191)
XLA Ops:
  4.8 3.1 collective-permute-start
  7.9 2.6 collective-permute-start.1
  12.1 3.9 collective-permute-start.3
  21.3 11.0 %collective-permute-done.1 = bf16[144,768]{1,0:T(8,128)(2,1)S(1)} collective-permute-done((bf16[144,768]{1,0:T(8,128)(2,1)S(1)}, bf16[144,768]{1,0:T(8,128)(2,1)S(1)}, u32[]{:S(2)}, u32[]{:S(2)}) %collective-permute-start.1) | collective-permute-done | bytes 221216 | tf_op jit(solution)/shard_map/ppermute | solution.py:22
  32.3 6.9 %collective-permute-done.4 = bf16[2,128,768]{2,1,0:T(8,128)(2,1)S(1)} collective-permute-done((bf16[2,128,768]{2,1,0:T(8,128)(2,1)S(1)}, bf16[2,128,768]{2,1,0:T(8,128)(2,1)S(1)}, u32[]{:S(2)}, u32[]{:S(2)}) %collective-permute-start.4) | collective-permute-done | bytes 393248 | tf_op jit(solution)/shard_map/ppermute | solution.py:22
  40.9 2.7 collective-permute-start.7
  43.7 2.5 collective-permute-start.8
  48.7 18.1 %collective-permute-done.8 = bf16[2,128,768]{2,1,0:T(8,128)(2,1)S(1)} collective-permute-done((bf16[2,128,768]{2,1,0:T(8,128)(2,1)S(1)}, bf16[2,128,768]{2,1,0:T(8,128)(2,1)S(1)}, u32[]{:S(2)}, u32[]{:S(2)}) %collective-permute-start.8) | collective-permute-done | bytes 393248 | tf_op jit(solution)/shard_map/ppermute | solution.py:22
  73.9 6.4 %collective-permute-done.12.refs_1_ = bf16[64,2048]{1,0:T(8,128)(2,1)S(1)} collective-permute-done((bf16[64,2048]{1,0:T(8,128)(2,1)S(1)}, bf16[64,2048]{1,0:T(8,128)(2,1)S(1)}, u32[]{:S(2)}, u32[]{:S(2)}) %collective-permute-start.12) | collective-permute-done | bytes 262176 | tf_op jit(solution)/shard_map/ppermute | solution.py:22
  80.3 4.6 collective-permute-done.13
  100.8 7.7 %collective-permute-done.17 = bf16[2,128,512]{2,1,0:T(8,128)(2,1)S(1)} collective-permute-done((bf16[2,128,512]{2,1,0:T(8,128)(2,1)S(1)}, bf16[2,128,512]{2,1,0:T(8,128)(2,1)S(1)}, u32[]{:S(2)}, u32[]{:S(2)}) %collective-permute-start.17) | collective-permute-done | bytes 262176 | tf_op jit(solution)/shard_map/ppermute | solution.py:22
  108.5 8.1 %collective-permute-done.18 = bf16[128,1536]{1,0:T(8,128)(2,1)S(1)} collective-permute-done((bf16[128,1536]{1,0:T(8,128)(2,1)S(1)}, bf16[128,1536]{1,0:T(8,128)(2,1)S(1)}, u32[]{:S(2)}, u32[]{:S(2)}) %collective-permute-start.18) | collective-permute-done | bytes 393248 | tf_op jit(solution)/shard_map/ppermute | solution.py:22
  118.4 7.1 %retention_forward.1 = (bf16[2,4,64,512]{3,2,1,0:T(8,128)(2,1)S(1)}, f32[2,4,64,512]{3,2,1,0:T(8,128)S(1)}, f32[2,4,64,1]{3,2,1,0:T(8,128)S(1)}, bf16[4,256,512]...) custom-call(s32[4]{0:T(128)S(1)} %pad_add_fusion.where_ref, f32[8,128]{1,0:T(8,128)S(1)} %get-tuple-element.332.decay_ref, ...), custom_call_target="tpu_custom_call" | custom-call | tf_op jit(solution)/shard_map/retention_forward/pallas_call | solution.py:80
  125.6 3.6 collective-permute-done.19.refs_2_
  140.2 11.4 %collective-permute-done.24 = bf16[128,1536]{1,0:T(8,128)(2,1)S(1)} collective-permute-done((bf16[128,1536]{1,0:T(8,128)(2,1)S(1)}, bf16[128,1536]{1,0:T(8,128)(2,1)S(1)}, u32[]{:S(2)}, u32[]{:S(2)}) %collective-permute-start.24) | collective-permute-done | bytes 393248 | tf_op jit(solution)/shard_map/ppermute | solution.py:22
  151.5 7.4 %collective-permute-done.25 = bf16[128,1536]{1,0:T(8,128)(2,1)S(1)} collective-permute-done((bf16[128,1536]{1,0:T(8,128)(2,1)S(1)}, bf16[128,1536]{1,0:T(8,128)(2,1)S(1)}, u32[]{:S(2)}, u32[]{:S(2)}) %collective-permute-start.25) | collective-permute-done | bytes 393248 | tf_op jit(solution)/shard_map/ppermute | solution.py:22
  162.4 13.3 %collective-permute-done.28.refs_2_ = bf16[4,128,512]{2,1,0:T(8,128)(2,1)S(1)} collective-permute-done((bf16[4,128,512]{2,1,0:T(8,128)(2,1)S(1)}, bf16[4,128,512]{2,1,0:T(8,128)(2,1)S(1)}, u32[]{:S(2)}, u32[]{:S(2)}) %collective-permute-start.28) | collective-permute-done | bytes 524320 | tf_op jit(solution)/shard_map/ppermute | solution.py:22
  180.0 7.2 %collective-permute-done.32.refs_4_ = bf16[64,2048]{1,0:T(8,128)(2,1)S(1)} collective-permute-done((bf16[64,2048]{1,0:T(8,128)(2,1)S(1)}, bf16[64,2048]{1,0:T(8,128)(2,1)S(1)}, u32[]{:S(2)}, u32[]{:S(2)}) %collective-permute-start.32) | collective-permute-done | bytes 262176 | tf_op jit(solution)/shard_map/ppermute | solution.py:22
  194.6 9.2 %collective-permute-done.34 = bf16[64,2048]{1,0:T(8,128)(2,1)S(1)} collective-permute-done((bf16[64,2048]{1,0:T(8,128)(2,1)S(1)}, bf16[64,2048]{1,0:T(8,128)(2,1)S(1)}, u32[]{:S(2)}, u32[]{:S(2)}) %collective-permute-start.34) | collective-permute-done | bytes 262176 | tf_op jit(solution)/shard_map/ppermute | solution.py:22
  204.9 6.9 %collective-permute-start.38 = (bf16[128,2048]{1,0:T(8,128)(2,1)S(1)}, bf16[128,2048]{1,0:T(8,128)(2,1)S(1)}, u32[]{:S(2)}, u32[]{:S(2)}) collective-permute-start(bf16[128,2048]{1,0:T(8,128)(2,1)S(1)} %constant_dynamic-update-slice_fusion.refs_0_), channel_id=1, source_target_pairs={{0,8},{8,0},{16,24},{24,16},{1,9},{9,1},{17,25},{25,17},{2,10},{10... | collective-permute-start | bytes 1572872 | tf_op jit(solution)/shard_map/ppermute | solution.py:22
  213.0 9.3 %collective-permute-done.38.refs_1_ = bf16[128,2048]{1,0:T(8,128)(2,1)S(1)} collective-permute-done((bf16[128,2048]{1,0:T(8,128)(2,1)S(1)}, bf16[128,2048]{1,0:T(8,128)(2,1)S(1)}, u32[]{:S(2)}, u32[]{:S(2)}) %collective-permute-start.38) | collective-permute-done | bytes 524320 | tf_op jit(solution)/shard_map/ppermute | solution.py:22
  227.4 4.1 collective-permute-done.42.refs_1_
  232.2 2.9 collective-permute-done.41.refs_3_
  239.9 2.6 far_messages.3
  245.2 2.7 weight_grads.6
  248.1 6.2 %collective-permute-done.43.got_ref = bf16[144,2048]{1,0:T(8,128)(2,1)S(1)} collective-permute-done((bf16[144,2048]{1,0:T(8,128)(2,1)S(1)}, bf16[144,2048]{1,0:T(8,128)(2,1)S(1)}, u32[]{:S(2)}, u32[]{:S(2)}) %collective-permute-start.43) | collective-permute-done | bytes 589856 | tf_op jit(solution)/shard_map/ppermute | solution.py:22
  260.0 3.3 weight_grads.7
  263.3 7.6 %collective-permute-done.44.got_ref = bf16[144,2048]{1,0:T(8,128)(2,1)S(1)} collective-permute-done((bf16[144,2048]{1,0:T(8,128)(2,1)S(1)}, bf16[144,2048]{1,0:T(8,128)(2,1)S(1)}, u32[]{:S(2)}, u32[]{:S(2)}) %collective-permute-start.44) | collective-permute-done | bytes 589856 | tf_op jit(solution)/shard_map/ppermute | solution.py:22
  276.9 11.7 %collective-permute-done.49 = bf16[512,512]{1,0:T(8,128)(2,1)S(1)} collective-permute-done((bf16[512,512]{1,0:T(8,128)(2,1)S(1)}, bf16[512,512]{1,0:T(8,128)(2,1)S(1)}, u32[]{:S(2)}, u32[]{:S(2)}) %collective-permute-start.49) | collective-permute-done | bytes 524320 | tf_op jit(solution)/shard_map/ppermute | solution.py:22
  296.4 6.7 %collective-permute-done.51 = bf16[512,512]{1,0:T(8,128)(2,1)S(1)} collective-permute-done((bf16[512,512]{1,0:T(8,128)(2,1)S(1)}, bf16[512,512]{1,0:T(8,128)(2,1)S(1)}, u32[]{:S(2)}, u32[]{:S(2)}) %collective-permute-start.51) | collective-permute-done | bytes 524320 | tf_op jit(solution)/shard_map/ppermute | solution.py:22
  303.3 8.1 %collective-permute-done.50 = bf16[64,2048]{1,0:T(8,128)(2,1)S(1)} collective-permute-done((bf16[64,2048]{1,0:T(8,128)(2,1)S(1)}, bf16[64,2048]{1,0:T(8,128)(2,1)S(1)}, u32[]{:S(2)}, u32[]{:S(2)}) %collective-permute-start.50) | collective-permute-done | bytes 262176 | tf_op jit(solution)/shard_map/ppermute | solution.py:22
  316.5 7.2 %collective-permute-done.56 = bf16[512,512]{1,0:T(8,128)(2,1)S(1)} collective-permute-done((bf16[512,512]{1,0:T(8,128)(2,1)S(1)}, bf16[512,512]{1,0:T(8,128)(2,1)S(1)}, u32[]{:S(2)}, u32[]{:S(2)}) %collective-permute-start.56) | collective-permute-done | bytes 524320 | tf_op jit(solution)/shard_map/ppermute | solution.py:22
  324.6 3.4 collective-permute-start.58
  328.6 6.6 %collective-permute-done.58.refs_2_ = bf16[128,1024]{1,0:T(8,128)(2,1)S(1)} collective-permute-done((bf16[128,1024]{1,0:T(8,128)(2,1)S(1)}, bf16[128,1024]{1,0:T(8,128)(2,1)S(1)}, u32[]{:S(2)}, u32[]{:S(2)}) %collective-permute-start.58) | collective-permute-done | bytes 262176 | tf_op jit(solution)/shard_map/ppermute | solution.py:22
  336.7 2.6 fusion.36
  339.4 3.1 weight_grads.8
  349.9 3.2 weight_grads.9
  353.1 6.9 %collective-permute-done.62.refs_1_ = bf16[128,512]{1,0:T(8,128)(2,1)S(1)} collective-permute-done((bf16[128,512]{1,0:T(8,128)(2,1)}, bf16[128,512]{1,0:T(8,128)(2,1)S(1)}, u32[]{:S(2)}, u32[]{:S(2)}) %collective-permute-start.62) | collective-permute-done | bytes 131104 | tf_op jit(solution)/shard_map/ppermute | solution.py:22
  360.1 6.8 %retention_backward.1 = (bf16[2,4,64,768]{3,2,1,0:T(8,128)(2,1)S(1)}, bf16[2,4,64,768]{3,2,1,0:T(8,128)(2,1)S(1)}) custom-call(s32[4]{0:T(128)S(1)} %pad_add_fusion.where_ref, f32[8,128]{1,0:T(8,128)S(1)} %get-tuple-element.332.decay_ref, bf16[2,4,64,256]{3,2,1,0:T(8,128)(2,1)S(1)} %copy-done.60, bf16[2,4,64,256]{3,2,1,0:T(8,128)(2,1)S(1)} %copy-done.62, ...), custom_call_target="tpu_custom_call" | custom-call | tf_op jit(solution)/shard_map/retention_backward/pallas_call | solution.py:80
  383.0 5.3 %collective-permute-done.68 = bf16[512,512]{1,0:T(8,128)(2,1)S(1)} collective-permute-done((bf16[512,512]{1,0:T(8,128)(2,1)S(1)}, bf16[512,512]{1,0:T(8,128)(2,1)S(1)}, u32[]{:S(2)}, u32[]{:S(2)}) %collective-permute-start.68) | collective-permute-done | bytes 524320 | tf_op jit(solution)/shard_map/ppermute | solution.py:22
  402.9 6.6 %collective-permute-done.71 = bf16[512,512]{1,0:T(8,128)(2,1)} collective-permute-done((bf16[512,512]{1,0:T(8,128)(2,1)}, bf16[512,512]{1,0:T(8,128)(2,1)}, u32[]{:S(2)}, u32[]{:S(2)}) %collective-permute-start.71) | collective-permute-done | bytes 524320 | tf_op jit(solution)/shard_map/ppermute | solution.py:22
  410.7 7.8 %collective-permute-done.72 = bf16[64,2048]{1,0:T(8,128)(2,1)S(1)} collective-permute-done((bf16[64,2048]{1,0:T(8,128)(2,1)}, bf16[64,2048]{1,0:T(8,128)(2,1)S(1)}, u32[]{:S(2)}, u32[]{:S(2)}) %collective-permute-start.72) | collective-permute-done | bytes 262176 | tf_op jit(solution)/shard_map/ppermute | solution.py:22
  454.1 2.8 collective-permute-start.77
  461.1 5.9 %collective-permute-done.76.refs_1_ = bf16[128,1024]{1,0:T(8,128)(2,1)S(1)} collective-permute-done((bf16[128,1024]{1,0:T(8,128)(2,1)S(1)}, bf16[128,1024]{1,0:T(8,128)(2,1)S(1)}, u32[]{:S(2)}, u32[]{:S(2)}) %collective-permute-start.76) | collective-permute-done | bytes 262176 | tf_op jit(solution)/shard_map/ppermute | solution.py:22
  467.1 8.4 %collective-permute-done.77.refs_2_ = bf16[128,1024]{1,0:T(8,128)(2,1)S(1)} collective-permute-done((bf16[128,1024]{1,0:T(8,128)(2,1)S(1)}, bf16[128,1024]{1,0:T(8,128)(2,1)S(1)}, u32[]{:S(2)}, u32[]{:S(2)}) %collective-permute-start.77) | collective-permute-done | bytes 262176 | tf_op jit(solution)/shard_map/ppermute | solution.py:22
  477.8 4.4 collective-permute-start.85
  492.2 3.5 collective-permute-done.87.refs_1_
  495.7 12.6 %collective-permute-done.88.refs_2_ = bf16[128,1024]{1,0:T(8,128)(2,1)S(1)} collective-permute-done((bf16[128,1024]{1,0:T(8,128)(2,1)S(1)}, bf16[128,1024]{1,0:T(8,128)(2,1)S(1)}, u32[]{:S(2)}, u32[]{:S(2)}) %collective-permute-start.88) | collective-permute-done | bytes 262176 | tf_op jit(solution)/shard_map/ppermute | solution.py:22
  (453 shorter events, 202.2 us)
Async XLA Ops:
  4.8 16.5 %collective-permute-start = (bf16[144,768]{1,0:T(8,128)(2,1)S(1)}, bf16[144,768]{1,0:T(8,128)(2,1)S(1)}, u32[]{:S(2)}, u32[]{:S(2)}) collective-permute-start(bf16[144,768]{1,0:T(8,128)(2,1)S(1)} %get-tuple-element.302), channel_id=1, source_target_pairs={{0,8},{8,0},{16,24},{24,16},{1,9},{9,1},{17,25},{25,17},{2,10},{10... | collective-permute-start | bytes 663560 | tf_op jit(solution)/shard_map/ppermute | solution.py:22
  7.9 24.4 %collective-permute-start.1 = (bf16[144,768]{1,0:T(8,128)(2,1)S(1)}, bf16[144,768]{1,0:T(8,128)(2,1)S(1)}, u32[]{:S(2)}, u32[]{:S(2)}) collective-permute-start(bf16[144,768]{1,0:T(8,128)(2,1)S(1)} %get-tuple-element.303), channel_id=1, source_target_pairs={{0,16},{8,24},{16,0},{24,8},{1,17},{9,25},{17,1},{25,9},{2,18},{10... | collective-permute-start | bytes 663560 | tf_op jit(solution)/shard_map/ppermute | solution.py:22
  10.5 21.8 %collective-permute-start.2 = (bf16[144,768]{1,0:T(8,128)(2,1)S(1)}, bf16[144,768]{1,0:T(8,128)(2,1)S(1)}, u32[]{:S(2)}, u32[]{:S(2)}) collective-permute-start(bf16[144,768]{1,0:T(8,128)(2,1)S(1)} %get-tuple-element.304), channel_id=1, source_target_pairs={{0,24},{8,16},{16,8},{24,0},{1,25},{9,17},{17,9},{25,1},{2,26},{10... | collective-permute-start | bytes 663560 | tf_op jit(solution)/shard_map/ppermute | solution.py:22
  12.1 20.2 %collective-permute-start.3 = (bf16[64,2048]{1,0:T(8,128)(2,1)S(1)}, bf16[64,2048]{1,0:T(8,128)(2,1)S(1)}, u32[]{:S(2)}, u32[]{:S(2)}) collective-permute-start(bf16[64,2048]{1,0:T(8,128)(2,1)S(1)} %get-tuple-element.300.refs_0_.in_ref), channel_id=1, source_target_pairs={{0,24},{8,16},{16,8},{24,0},{1,25},{9,17},{17,9},{25,1},{2,26},{10... | collective-permute-start | bytes 786440 | tf_op jit(solution)/shard_map/ppermute | solution.py:22
  18.6 20.5 %collective-permute-start.4 = (bf16[2,128,768]{2,1,0:T(8,128)(2,1)S(1)}, bf16[2,128,768]{2,1,0:T(8,128)(2,1)S(1)}, u32[]{:S(2)}, u32[]{:S(2)}) collective-permute-start(bf16[2,128,768]{2,1,0:T(8,128)(2,1)S(1)} %get-tuple-element.305), channel_id=1, source_target_pairs={{0,8},{8,0},{16,24},{24,16},{1,9},{9,1},{17,25},{25,17},{2,10},{10... | collective-permute-start | bytes 1179656 | tf_op jit(solution)/shard_map/ppermute | solution.py:22
  39.3 27.6 %collective-permute-start.5 = (bf16[4,144,768]{2,1,0:T(8,128)(2,1)S(1)}, bf16[4,144,768]{2,1,0:T(8,128)(2,1)S(1)}, u32[]{:S(2)}, u32[]{:S(2)}) collective-permute-start(bf16[4,144,768]{2,1,0:T(8,128)(2,1)S(1)} %pad_maximum_fusion.3.refs_0_), channel_id=1, source_target_pairs={{0,4},{4,0},{1,5},{5,1},{2,6},{6,2},{3,7},{7,3},{8,12},{12,8},{9,1... | collective-permute-start | bytes 2654216 | tf_op jit(solution)/shard_map/ppermute | solution.py:22
  40.8 26.0 %collective-permute-start.6 = (bf16[4,144,768]{2,1,0:T(8,128)(2,1)S(1)}, bf16[4,144,768]{2,1,0:T(8,128)(2,1)S(1)}, u32[]{:S(2)}, u32[]{:S(2)}) collective-permute-start(bf16[4,144,768]{2,1,0:T(8,128)(2,1)S(1)} %pad_maximum_fusion.3.refs_0_), channel_id=1, source_target_pairs={{0,2},{2,0},{1,3},{3,1},{4,6},{6,4},{5,7},{7,5},{8,10},{10,8},{9,1... | collective-permute-start | bytes 2654216 | tf_op jit(solution)/shard_map/ppermute | solution.py:22
  40.9 25.9 %collective-permute-start.7 = (bf16[128,2048]{1,0:T(8,128)(2,1)S(1)}, bf16[128,2048]{1,0:T(8,128)(2,1)S(1)}, u32[]{:S(2)}, u32[]{:S(2)}) collective-permute-start(bf16[128,2048]{1,0:T(8,128)(2,1)S(1)} %pad_maximum_fusion.7), channel_id=1, source_target_pairs={{0,8},{8,0},{16,24},{24,16},{1,9},{9,1},{17,25},{25,17},{2,10},{10... | collective-permute-start | bytes 1572872 | tf_op jit(solution)/shard_map/ppermute | solution.py:22
  43.7 23.1 %collective-permute-start.8 = (bf16[2,128,768]{2,1,0:T(8,128)(2,1)S(1)}, bf16[2,128,768]{2,1,0:T(8,128)(2,1)S(1)}, u32[]{:S(2)}, u32[]{:S(2)}) collective-permute-start(bf16[2,128,768]{2,1,0:T(8,128)(2,1)S(1)} %pad_maximum_fusion.10), channel_id=1, source_target_pairs={{0,24},{8,16},{16,8},{24,0},{1,25},{9,17},{17,9},{25,1},{2,26},{10... | collective-permute-start | bytes 1179656 | tf_op jit(solution)/shard_map/ppermute | solution.py:22
  66.8 21.6 %collective-permute-start.9 = (bf16[4,144,768]{2,1,0:T(8,128)(2,1)S(1)}, bf16[4,144,768]{2,1,0:T(8,128)(2,1)S(1)}, u32[]{:S(2)}, u32[]{:S(2)}) collective-permute-start(bf16[4,144,768]{2,1,0:T(8,128)(2,1)S(1)} %collective-permute-done.5.refs_2_), channel_id=1, source_target_pairs={{0,2},{2,0},{1,3},{3,1},{4,6},{6,4},{5,7},{7,5},{8,10},{10,8},{9,1... | collective-permute-start | bytes 2654216 | tf_op jit(solution)/shard_map/ppermute | solution.py:22
  67.0 20.0 %collective-permute-start.10 = (bf16[192,2048]{1,0:T(8,128)(2,1)S(1)}, bf16[192,2048]{1,0:T(8,128)(2,1)S(1)}, u32[]{:S(2)}, u32[]{:S(2)}) collective-permute-start(bf16[192,2048]{1,0:T(8,128)(2,1)S(1)} %pad_maximum_fusion.4), channel_id=1, source_target_pairs={{0,1},{1,0},{2,3},{3,2},{4,5},{5,4},{6,7},{7,6},{8,9},{9,8},{10,11... | collective-permute-start | bytes 2359304 | tf_op jit(solution)/shard_map/ppermute | solution.py:22
  68.7 19.7 %collective-permute-start.11 = (bf16[4,128,768]{2,1,0:T(8,128)(2,1)S(1)}, bf16[4,128,768]{2,1,0:T(8,128)(2,1)S(1)}, u32[]{:S(2)}, u32[]{:S(2)}) collective-permute-start(bf16[4,128,768]{2,1,0:T(8,128)(2,1)S(1)} %pad_maximum_fusion.5.refs_0_), channel_id=1, source_target_pairs={{0,4},{4,0},{1,5},{5,1},{2,6},{6,2},{3,7},{7,3},{8,12},{12,8},{9,1... | collective-permute-start | bytes 2359304 | tf_op jit(solution)/shard_map/ppermute | solution.py:22
  70.6 14.3 %collective-permute-start.13 = (bf16[2,128,512]{2,1,0:T(8,128)(2,1)S(1)}, bf16[2,128,512]{2,1,0:T(8,128)(2,1)S(1)}, u32[]{:S(2)}, u32[]{:S(2)}) collective-permute-start(bf16[2,128,512]{2,1,0:T(8,128)(2,1)S(1)} %get-tuple-element.325), channel_id=1, source_target_pairs={{0,24},{8,16},{16,8},{24,0},{1,25},{9,17},{17,9},{25,1},{2,26},{10... | collective-permute-start | bytes 786440 | tf_op jit(solution)/shard_map/ppermute | solution.py:22
  93.9 22.7 %collective-permute-start.14 = (bf16[2,4,64,768]{3,2,1,0:T(8,128)(2,1)S(1)}, bf16[2,4,64,768]{3,2,1,0:T(8,128)(2,1)S(1)}, u32[]{:S(2)}, u32[]{:S(2)}) collective-permute-start(bf16[2,4,64,768]{3,2,1,0:T(8,128)(2,1)S(1)} %pad_maximum_fusion.6.refs_0_.refs_4_), channel_id=1, source_target_pairs={{0,4},{4,0},{1,5},{5,1},{2,6},{6,2},{3,7},{7,3},{8,12},{12,8},{9,1... | collective-permute-start | bytes 2359304 | tf_op jit(solution)/shard_map/ppermute | solution.py:22
  94.5 14.0 %collective-permute-start.17 = (bf16[2,128,512]{2,1,0:T(8,128)(2,1)S(1)}, bf16[2,128,512]{2,1,0:T(8,128)(2,1)S(1)}, u32[]{:S(2)}, u32[]{:S(2)}) collective-permute-start(bf16[2,128,512]{2,1,0:T(8,128)(2,1)S(1)} %pad_maximum_fusion.11), channel_id=1, source_target_pairs={{0,8},{8,0},{16,24},{24,16},{1,9},{9,1},{17,25},{25,17},{2,10},{10... | collective-permute-start | bytes 786440 | tf_op jit(solution)/shard_map/ppermute | solution.py:22
  96.7 19.9 %collective-permute-start.18 = (bf16[128,1536]{1,0:T(8,128)(2,1)S(1)}, bf16[128,1536]{1,0:T(8,128)(2,1)S(1)}, u32[]{:S(2)}, u32[]{:S(2)}) collective-permute-start(bf16[128,1536]{1,0:T(8,128)(2,1)S(1)} %get-tuple-element.351), channel_id=1, source_target_pairs={{0,16},{8,24},{16,0},{24,8},{1,17},{9,25},{17,1},{25,9},{2,18},{10... | collective-permute-start | bytes 1179656 | tf_op jit(solution)/shard_map/ppermute | solution.py:22
  136.0 22.8 %collective-permute-start.23 = (bf16[144,2048]{1,0:T(8,128)(2,1)S(1)}, bf16[144,2048]{1,0:T(8,128)(2,1)S(1)}, u32[]{:S(2)}, u32[]{:S(2)}) collective-permute-start(bf16[144,2048]{1,0:T(8,128)(2,1)S(1)} %get-tuple-element.364), channel_id=1, source_target_pairs={{0,1},{1,0},{2,3},{3,2},{4,5},{5,4},{6,7},{7,6},{8,9},{9,8},{10,11... | collective-permute-start | bytes 1769480 | tf_op jit(solution)/shard_map/ppermute | solution.py:22
  137.6 13.9 %collective-permute-start.24 = (bf16[128,1536]{1,0:T(8,128)(2,1)S(1)}, bf16[128,1536]{1,0:T(8,128)(2,1)S(1)}, u32[]{:S(2)}, u32[]{:S(2)}) collective-permute-start(bf16[128,1536]{1,0:T(8,128)(2,1)S(1)} %get-tuple-element.369), channel_id=1, source_target_pairs={{0,24},{8,16},{16,8},{24,0},{1,25},{9,17},{17,9},{25,1},{2,26},{10... | collective-permute-start | bytes 1179656 | tf_op jit(solution)/shard_map/ppermute | solution.py:22
  139.9 19.0 %collective-permute-start.25 = (bf16[128,1536]{1,0:T(8,128)(2,1)S(1)}, bf16[128,1536]{1,0:T(8,128)(2,1)S(1)}, u32[]{:S(2)}, u32[]{:S(2)}) collective-permute-start(bf16[128,1536]{1,0:T(8,128)(2,1)S(1)} %get-tuple-element.370), channel_id=1, source_target_pairs={{0,8},{8,0},{16,24},{24,16},{1,9},{9,1},{17,25},{25,17},{2,10},{10... | collective-permute-start | bytes 1179656 | tf_op jit(solution)/shard_map/ppermute | solution.py:22
  159.1 16.7 %collective-permute-start.29 = (bf16[4,128,1536]{2,1,0:T(8,128)(2,1)S(1)}, bf16[4,128,1536]{2,1,0:T(8,128)(2,1)S(1)}, u32[]{:S(2)}, u32[]{:S(2)}) collective-permute-start(bf16[4,128,1536]{2,1,0:T(8,128)(2,1)S(1)} %pad_maximum_fusion.1.refs_0_), channel_id=1, source_target_pairs={{0,2},{2,0},{1,3},{3,1},{4,6},{6,4},{5,7},{7,5},{8,10},{10,8},{9,1... | collective-permute-start | bytes 4718600 | tf_op jit(solution)/shard_map/ppermute | solution.py:22
  159.8 15.8 %collective-permute-start.26 = (bf16[144,2048]{1,0:T(8,128)(2,1)S(1)}, bf16[144,2048]{1,0:T(8,128)(2,1)S(1)}, u32[]{:S(2)}, u32[]{:S(2)}) collective-permute-start(bf16[144,2048]{1,0:T(8,128)(2,1)S(1)} %pass_message.2), channel_id=1, source_target_pairs={{0,8},{8,0},{16,24},{24,16},{1,9},{9,1},{17,25},{25,17},{2,10},{10... | collective-permute-start | bytes 1769480 | tf_op jit(solution)/shard_map/ppermute | solution.py:22
  160.3 15.4 %collective-permute-start.27 = (bf16[144,2048]{1,0:T(8,128)(2,1)S(1)}, bf16[144,2048]{1,0:T(8,128)(2,1)S(1)}, u32[]{:S(2)}, u32[]{:S(2)}) collective-permute-start(bf16[144,2048]{1,0:T(8,128)(2,1)S(1)} %get-tuple-element.374), channel_id=1, source_target_pairs={{0,1},{1,0},{2,3},{3,2},{4,5},{5,4},{6,7},{7,6},{8,9},{9,8},{10,11... | collective-permute-start | bytes 1769480 | tf_op jit(solution)/shard_map/ppermute | solution.py:22
  161.8 13.8 %collective-permute-start.28 = (bf16[4,128,512]{2,1,0:T(8,128)(2,1)S(1)}, bf16[4,128,512]{2,1,0:T(8,128)(2,1)S(1)}, u32[]{:S(2)}, u32[]{:S(2)}) collective-permute-start(bf16[4,128,512]{2,1,0:T(8,128)(2,1)S(1)} %slice.268), channel_id=1, source_target_pairs={{0,4},{4,0},{1,5},{5,1},{2,6},{6,2},{3,7},{7,3},{8,12},{12,8},{9,1... | collective-permute-start | bytes 1572872 | tf_op jit(solution)/shard_map/ppermute | solution.py:22
  204.9 17.5 %collective-permute-start.38 = (bf16[128,2048]{1,0:T(8,128)(2,1)S(1)}, bf16[128,2048]{1,0:T(8,128)(2,1)S(1)}, u32[]{:S(2)}, u32[]{:S(2)}) collective-permute-start(bf16[128,2048]{1,0:T(8,128)(2,1)S(1)} %constant_dynamic-update-slice_fusion.refs_0_), channel_id=1, source_target_pairs={{0,8},{8,0},{16,24},{24,16},{1,9},{9,1},{17,25},{25,17},{2,10},{10... | collective-permute-start | bytes 1572872 | tf_op jit(solution)/shard_map/ppermute | solution.py:22
  255.0 15.8 %collective-permute-start.44 = (bf16[144,2048]{1,0:T(8,128)(2,1)S(1)}, bf16[144,2048]{1,0:T(8,128)(2,1)S(1)}, u32[]{:S(2)}, u32[]{:S(2)}) collective-permute-start(bf16[144,2048]{1,0:T(8,128)(2,1)S(1)} %pass_message.3), channel_id=1, source_target_pairs={{0,8},{8,0},{16,24},{24,16},{1,9},{9,1},{17,25},{25,17},{2,10},{10... | collective-permute-start | bytes 1769480 | tf_op jit(solution)/shard_map/ppermute | solution.py:22
  255.9 15.5 %collective-permute-start.45 = (bf16[144,2048]{1,0:T(8,128)(2,1)S(1)}, bf16[144,2048]{1,0:T(8,128)(2,1)S(1)}, u32[]{:S(2)}, u32[]{:S(2)}) collective-permute-start(bf16[144,2048]{1,0:T(8,128)(2,1)S(1)} %get-tuple-element.435), channel_id=1, source_target_pairs={{0,1},{1,0},{2,3},{3,2},{4,5},{5,4},{6,7},{7,6},{8,9},{9,8},{10,11... | collective-permute-start | bytes 1769480 | tf_op jit(solution)/shard_map/ppermute | solution.py:22
  272.0 16.7 %collective-permute-start.47 = (bf16[80,2048]{1,0:T(8,128)(2,1)S(1)}, bf16[80,2048]{1,0:T(8,128)(2,1)S(1)}, u32[]{:S(2)}, u32[]{:S(2)}) collective-permute-start(bf16[80,2048]{1,0:T(8,128)(2,1)S(1)} %get-tuple-element.443), channel_id=1, source_target_pairs={{0,24},{8,16},{16,8},{24,0},{1,25},{9,17},{17,9},{25,1},{2,26},{10... | collective-permute-start | bytes 983048 | tf_op jit(solution)/shard_map/ppermute | solution.py:22
  273.8 15.0 %collective-permute-start.48 = (bf16[128,2048]{1,0:T(8,128)(2,1)S(1)}, bf16[128,2048]{1,0:T(8,128)(2,1)S(1)}, u32[]{:S(2)}, u32[]{:S(2)}) collective-permute-start(bf16[128,2048]{1,0:T(8,128)(2,1)S(1)} %get-tuple-element.444), channel_id=1, source_target_pairs={{0,1},{1,0},{2,3},{3,2},{4,5},{5,4},{6,7},{7,6},{8,9},{9,8},{10,11... | collective-permute-start | bytes 1572872 | tf_op jit(solution)/shard_map/ppermute | solution.py:22
  292.1 19.3 %collective-permute-start.52 = (bf16[128,2048]{1,0:T(8,128)(2,1)S(1)}, bf16[128,2048]{1,0:T(8,128)(2,1)S(1)}, u32[]{:S(2)}, u32[]{:S(2)}) collective-permute-start(bf16[128,2048]{1,0:T(8,128)(2,1)S(1)} %get-tuple-element.465), channel_id=1, source_target_pairs={{0,1},{1,0},{2,3},{3,2},{4,5},{5,4},{6,7},{7,6},{8,9},{9,8},{10,11... | collective-permute-start | bytes 1572872 | tf_op jit(solution)/shard_map/ppermute | solution.py:22
  293.9 17.5 %collective-permute-start.53 = (bf16[128,2048]{1,0:T(8,128)(2,1)S(1)}, bf16[128,2048]{1,0:T(8,128)(2,1)S(1)}, u32[]{:S(2)}, u32[]{:S(2)}) collective-permute-start(bf16[128,2048]{1,0:T(8,128)(2,1)S(1)} %add_convert_fusion.1), channel_id=1, source_target_pairs={{0,8},{8,0},{16,24},{24,16},{1,9},{9,1},{17,25},{25,17},{2,10},{10... | collective-permute-start | bytes 1572872 | tf_op jit(solution)/shard_map/ppermute | solution.py:22
  294.2 17.2 %collective-permute-start.50 = (bf16[64,2048]{1,0:T(8,128)(2,1)S(1)}, bf16[64,2048]{1,0:T(8,128)(2,1)S(1)}, u32[]{:S(2)}, u32[]{:S(2)}) collective-permute-start(bf16[64,2048]{1,0:T(8,128)(2,1)S(1)} %get-tuple-element.459), channel_id=1, source_target_pairs={{0,24},{8,16},{16,8},{24,0},{1,25},{9,17},{17,9},{25,1},{2,26},{10... | collective-permute-start | bytes 786440 | tf_op jit(solution)/shard_map/ppermute | solution.py:22
  345.7 14.4 %collective-permute-start.60 = (bf16[2,4,64,512]{3,2,1,0:T(8,128)(2,1)S(1)}, bf16[2,4,64,512]{3,2,1,0:T(8,128)(2,1)S(1)}, u32[]{:S(2)}, u32[]{:S(2)}) collective-permute-start(bf16[2,4,64,512]{3,2,1,0:T(8,128)(2,1)S(1)} %bitcast.120), channel_id=1, source_target_pairs={{0,4},{4,0},{1,5},{5,1},{2,6},{6,2},{3,7},{7,3},{8,12},{12,8},{9,1... | collective-permute-start | bytes 1572872 | tf_op jit(solution)/shard_map/ppermute | solution.py:22
  373.1 15.3 %collective-permute-start.67 = (bf16[1024,1024]{1,0:T(8,128)(2,1)S(1)}, bf16[1024,1024]{1,0:T(8,128)(2,1)S(1)}, u32[]{:S(2)}, u32[]{:S(2)}) collective-permute-start(bf16[1024,1024]{1,0:T(8,128)(2,1)S(1)} %weight_grads.10), channel_id=1, source_target_pairs={{0,2},{2,0},{1,3},{3,1},{4,6},{6,4},{5,7},{7,5},{8,10},{10,8},{9,1... | collective-permute-start | bytes 6291464 | tf_op jit(solution)/shard_map/ppermute | solution.py:22
  373.6 21.4 %collective-permute-start.64 = (bf16[128,2048]{1,0:T(8,128)(2,1)S(1)}, bf16[128,2048]{1,0:T(8,128)(2,1)S(1)}, u32[]{:S(2)}, u32[]{:S(2)}) collective-permute-start(bf16[128,2048]{1,0:T(8,128)(2,1)S(1)} %get-tuple-element.612), channel_id=1, source_target_pairs={{0,1},{1,0},{2,3},{3,2},{4,5},{5,4},{6,7},{7,6},{8,9},{9,8},{10,11... | collective-permute-start | bytes 1572872 | tf_op jit(solution)/shard_map/ppermute | solution.py:22
  374.2 14.1 %collective-permute-start.68 = (bf16[512,512]{1,0:T(8,128)(2,1)S(1)}, bf16[512,512]{1,0:T(8,128)(2,1)S(1)}, u32[]{:S(2)}, u32[]{:S(2)}) collective-permute-start(bf16[512,512]{1,0:T(8,128)(2,1)S(1)} %slice.249), channel_id=1, source_target_pairs={{0,4},{4,0},{1,5},{5,1},{2,6},{6,2},{3,7},{7,3},{8,12},{12,8},{9,1... | collective-permute-start | bytes 1572872 | tf_op jit(solution)/shard_map/ppermute | solution.py:22
  378.6 15.2 %collective-permute-start.65 = (bf16[128,512]{1,0:T(8,128)(2,1)S(1)}, bf16[128,512]{1,0:T(8,128)(2,1)S(1)}, u32[]{:S(2)}, u32[]{:S(2)}) collective-permute-start(bf16[128,512]{1,0:T(8,128)(2,1)S(1)} %copy-done.82), channel_id=1, source_target_pairs={{0,16},{8,24},{16,0},{24,8},{1,17},{9,25},{17,1},{25,9},{2,18},{10... | collective-permute-start | bytes 393224 | tf_op jit(solution)/shard_map/ppermute | solution.py:22
  380.8 13.6 %collective-permute-start.66 = (bf16[128,512]{1,0:T(8,128)(2,1)S(1)}, bf16[128,512]{1,0:T(8,128)(2,1)S(1)}, u32[]{:S(2)}, u32[]{:S(2)}) collective-permute-start(bf16[128,512]{1,0:T(8,128)(2,1)S(1)} %copy-done.80), channel_id=1, source_target_pairs={{0,24},{8,16},{16,8},{24,0},{1,25},{9,17},{17,9},{25,1},{2,26},{10... | collective-permute-start | bytes 393224 | tf_op jit(solution)/shard_map/ppermute | solution.py:22
  397.9 20.6 %collective-permute-start.69 = (bf16[128,2048]{1,0:T(8,128)(2,1)}, bf16[128,2048]{1,0:T(8,128)(2,1)}, u32[]{:S(2)}, u32[]{:S(2)}) collective-permute-start(bf16[128,2048]{1,0:T(8,128)(2,1)} %add_convert_fusion), channel_id=1, source_target_pairs={{0,8},{8,0},{16,24},{24,16},{1,9},{9,1},{17,25},{25,17},{2,10},{10... | collective-permute-start | bytes 1572872 | tf_op jit(solution)/shard_map/ppermute | solution.py:22
  400.0 18.5 %collective-permute-start.70 = (bf16[128,2048]{1,0:T(8,128)(2,1)}, bf16[128,2048]{1,0:T(8,128)(2,1)}, u32[]{:S(2)}, u32[]{:S(2)}) collective-permute-start(bf16[128,2048]{1,0:T(8,128)(2,1)} %get-tuple-element.525), channel_id=1, source_target_pairs={{0,1},{1,0},{2,3},{3,2},{4,5},{5,4},{6,7},{7,6},{8,9},{9,8},{10,11... | collective-permute-start | bytes 1572872 | tf_op jit(solution)/shard_map/ppermute | solution.py:22
  401.7 16.8 %collective-permute-start.72 = (bf16[64,2048]{1,0:T(8,128)(2,1)}, bf16[64,2048]{1,0:T(8,128)(2,1)S(1)}, u32[]{:S(2)}, u32[]{:S(2)}) collective-permute-start(bf16[64,2048]{1,0:T(8,128)(2,1)} %slice.350), channel_id=1, source_target_pairs={{0,24},{8,16},{16,8},{24,0},{1,25},{9,17},{17,9},{25,1},{2,26},{10... | collective-permute-start | bytes 786440 | tf_op jit(solution)/shard_map/ppermute | solution.py:22
  431.9 27.3 %collective-permute-start.79 = (bf16[512,512]{1,0:T(8,128)(2,1)}, bf16[512,512]{1,0:T(8,128)(2,1)}, u32[]{:S(2)}, u32[]{:S(2)}) collective-permute-start(bf16[512,512]{1,0:T(8,128)(2,1)} %slice.255), channel_id=1, source_target_pairs={{0,4},{4,0},{1,5},{5,1},{2,6},{6,2},{3,7},{7,3},{8,12},{12,8},{9,1... | collective-permute-start | bytes 1572872 | tf_op jit(solution)/shard_map/ppermute | solution.py:22
  435.0 40.5 %collective-permute-start.80 = (f32[64,2048]{1,0:T(8,128)S(1)}, f32[64,2048]{1,0:T(8,128)S(1)}, u32[]{:S(2)}, u32[]{:S(2)}) collective-permute-start(f32[64,2048]{1,0:T(8,128)S(1)} %fusion.21.own_ref), channel_id=1, source_target_pairs={{0,1},{1,0},{2,3},{3,2},{4,5},{5,4},{6,7},{7,6},{8,9},{9,8},{10,11... | collective-permute-start | bytes 1572872 | tf_op jit(solution)/shard_map/ppermute | solution.py:22
  454.1 21.4 %collective-permute-start.77 = (bf16[128,1024]{1,0:T(8,128)(2,1)S(1)}, bf16[128,1024]{1,0:T(8,128)(2,1)S(1)}, u32[]{:S(2)}, u32[]{:S(2)}) collective-permute-start(bf16[128,1024]{1,0:T(8,128)(2,1)S(1)} %copy-done.75), channel_id=1, source_target_pairs={{0,16},{8,24},{16,0},{24,8},{1,17},{9,25},{17,1},{25,9},{2,18},{10... | collective-permute-start | bytes 786440 | tf_op jit(solution)/shard_map/ppermute | solution.py:22
  456.9 18.6 %collective-permute-start.78 = (bf16[128,1024]{1,0:T(8,128)(2,1)S(1)}, bf16[128,1024]{1,0:T(8,128)(2,1)S(1)}, u32[]{:S(2)}, u32[]{:S(2)}) collective-permute-start(bf16[128,1024]{1,0:T(8,128)(2,1)S(1)} %copy-done.73), channel_id=1, source_target_pairs={{0,24},{8,16},{16,8},{24,0},{1,25},{9,17},{17,9},{25,1},{2,26},{10... | collective-permute-start | bytes 786440 | tf_op jit(solution)/shard_map/ppermute | solution.py:22
  475.5 14.5 %collective-permute-start.86 = (f32[4,128]{1,0:T(4,128)S(1)}, f32[4,128]{1,0:T(4,128)S(1)}, u32[]{:S(2)}, u32[]{:S(2)}) collective-permute-start(f32[4,128]{1,0:T(4,128)S(1)} %bitcast.163), channel_id=1, source_target_pairs={{0,24},{8,16},{16,8},{24,0},{1,25},{9,17},{17,9},{25,1},{2,26},{10... | collective-permute-start | bytes 6152 | tf_op jit(solution)/shard_map/ppermute | solution.py:22
  477.8 13.8 %collective-permute-start.85 = (f32[4,128]{1,0:T(4,128)S(1)}, f32[4,128]{1,0:T(4,128)S(1)}, u32[]{:S(2)}, u32[]{:S(2)}) collective-permute-start(f32[4,128]{1,0:T(4,128)S(1)} %bitcast.162), channel_id=1, source_target_pairs={{0,16},{8,24},{16,0},{24,8},{1,17},{9,25},{17,1},{25,9},{2,18},{10... | collective-permute-start | bytes 6152 | tf_op jit(solution)/shard_map/ppermute | solution.py:22
  487.2 21.1 %collective-permute-start.88 = (bf16[128,1024]{1,0:T(8,128)(2,1)S(1)}, bf16[128,1024]{1,0:T(8,128)(2,1)S(1)}, u32[]{:S(2)}, u32[]{:S(2)}) collective-permute-start(bf16[128,1024]{1,0:T(8,128)(2,1)S(1)} %get-tuple-element.572), channel_id=1, source_target_pairs={{0,16},{8,24},{16,0},{24,8},{1,17},{9,25},{17,1},{25,9},{2,18},{10... | collective-permute-start | bytes 786440 | tf_op jit(solution)/shard_map/ppermute | solution.py:22
  490.0 18.2 %collective-permute-start.89 = (bf16[128,1024]{1,0:T(8,128)(2,1)S(1)}, bf16[128,1024]{1,0:T(8,128)(2,1)S(1)}, u32[]{:S(2)}, u32[]{:S(2)}) collective-permute-start(bf16[128,1024]{1,0:T(8,128)(2,1)S(1)} %get-tuple-element.573), channel_id=1, source_target_pairs={{0,24},{8,16},{16,8},{24,0},{1,25},{9,17},{17,9},{25,1},{2,26},{10... | collective-permute-start | bytes 786440 | tf_op jit(solution)/shard_map/ppermute | solution.py:22
  (130 other events, 1714.6 us)
where the time goes:
time: 519 us; the launch traced here: 511 us
  waiting for transfers between devices  264 us (51%)
  starting transfers between devices  111 us (21%)
  Pallas kernels  64.4 us (12%)
  local copies, waits for them, and re-layouts  34.3 us (7%)
  matrix products  17.8 us (3%)
  other arithmetic  17.2 us (3%)
    ppermute x90, waiting for transfers between devices, swap(): return lax.ppermute(values, axis, [(i, i ^ k) for i in range(count)])  264 us
    ppermute x90, starting transfers between devices, swap(): return lax.ppermute(values, axis, [(i, i ^ k) for i in range(count)])  111 us
    pallas_call x32, Pallas kernels, call(): pl.pallas_call(kernel, grid=() if grid is None else grid, out_shape=shape...  42.8 us
    unnamed x178, local copies, waits for them, and re-layouts  23.7 us
    pallas_call x6, Pallas kernels, weight_grads(): pl.pallas_call(kernel, grid=(ny,), out_shape=shapes, in_specs=[SMEM] + [W...  16.9 us
  transfers between devices with their start and end apart: 90, of which 47 were waited for; matrix products, arithmetic and copies ran while one was open for 6% of the time, Pallas kernels for 7%

commit v1 on v0

--- a/solution.py
+++ b/solution.py
@@ -748,10 +748,12 @@
     )
     keyvals, query_gate, out_last, feed_two = tie(keyvals, query_gate, out_last, feed_two)
     out_cols = over_col(jnp.stack(in_order(out, out_got, out_last, 3)))
-    late_grad, late_two = after((own_grad, two_grad), keyvals)
+    late_grad, late_two, late_three = after((own_grad, two_grad, feed[3]), keyvals)
+    middle_col = late_three.shape[1] // 2
+    feed_left = swap(late_three[:, :middle_col], "row", 3)
     one_grad = swap(jnp.concatenate([late_grad, late_two]), "row", 1)
     mixed, normed, rstd, states, query = retention_forward(where, decays, keyvals, query_gate)
-    mixed, out_cols, one_grad = tie(mixed, out_cols, one_grad)
+    mixed, out_cols, one_grad, feed_left = tie(mixed, out_cols, one_grad, feed_left)
     (out_w,) = assemble(where, pairs(out_cols, over_batch(out_cols)), ny, nb, (DV,))
     mixed_bf = mixed.reshape(tokens, DV)
 
@@ -759,8 +761,10 @@
     got = mirror(far[0])
     near = reduce_near((mixed_bf, out_w))
     late_feed = after(feed, far)
-    feed_three, feed_one = trade(late_feed, 3), trade(late_feed, 1)
-    got, near, feed_three, feed_one = tie(got, near, feed_three, feed_one)
+    feed_right = swap(late_feed[3][:, middle_col:], "row", 3)
+    feed_one = trade(late_feed, 1)
+    got, near, feed_right, feed_one = tie(got, near, feed_right, feed_one)
+    feed_three = jnp.concatenate([feed_left, feed_right], axis=-1)
     got_far = mirror(after(far[1], got))
     got = swap(pass_message(where, near[0], got, part), "row", 1)
     feed = jnp.stack([feed[0], feed_one, feed_two, feed_three])
@@ -885,16 +889,18 @@
     down_two, down_three = trade(late_down, 2), trade(late_down, 3)
     out_sum = sum_col(both_keeps[1], late_send[1])
     near = reduce_near(*terms)
-    kvq_keeps, kvq_sends = weight_grads(where, *kvq, sizes, (DV, 2 * DK), kvq_got)
-    got, near, down_two, down_three, kvq_sends, out_sum, both_sends, result_send = tie(
-        got, near, down_two, down_three, kvq_sends, out_sum, both_sends, result_send
+    got, near, down_two, down_three, kvq_got, out_sum, both_sends, result_send = tie(
+        got, near, down_two, down_three, kvq_got, out_sum, both_sends, result_send
     )
     got_far = mirror(after(far[1], got))
     got = swap(add(near[0], got).astype(bf16), "row", 1)
     gate_sum = sum_col(both_keeps[0], both_sends[0])
     result_got = swap(result_send, "row", 3)
-    got, got_far, gate_sum, result_got, kvq_sends = tie(
-        got, got_far, gate_sum, result_got, kvq_sends
+    kvq_keeps, kvq_sends = weight_grads(where, *kvq, sizes, (DV, 2 * DK), kvq_got)
+    wide_pieces = (wide_grads[0], wide_one, wide_two, wide_three)
+    grad_gates, grad_ups = unpack_grads(where, wide_pieces, ((units, False), (units, False)))
+    got, got_far, gate_sum, result_got, kvq_sends, grad_gates, grad_ups = tie(
+        got, got_far, gate_sum, result_got, kvq_sends, grad_gates, grad_ups
     )
     keep = add(add(near[1], got_far), got)
     got = swap(keep[part:].astype(bf16), "row", 3)
@@ -902,8 +908,10 @@
     result_other = mirror(result)
     kvq_first = sum_col(kvq_keeps[0], kvq_sends[0])
     both_pieces = cut_heads(where, (gate_sum, out_sum))
-    got, result_other, kvq_first, kvq_sends, both_pieces = tie(
-        got, result_other, kvq_first, kvq_sends, both_pieces
+    down_pieces = (down_grads[0], down_one, down_two, down_three)
+    (grad_downs,) = unpack_grads(where, down_pieces, ((units, True),))
+    got, result_other, kvq_first, kvq_sends, both_pieces, grad_downs = tie(
+        got, result_other, kvq_first, kvq_sends, both_pieces, grad_downs
     )
     both_pieces = [trade(both_pieces, k) for k in range(nz)]
     kvq_second = sum_col(kvq_keeps[1], kvq_sends[1])
@@ -911,11 +919,11 @@
     scaled_own, rstd_own = normalize(own_in.astype(f32))
     grad_in = grad_middle + norm_back(grad_one * gains[0:1], scaled_own, rstd_own)
     grad_in_other = mirror(grad_in)
-    wide_pieces = (wide_grads[0], wide_one, wide_two, wide_three)
-    grad_gates, grad_ups = unpack_grads(where, wide_pieces, ((units, False), (units, False)))
-    down_pieces = (down_grads[0], down_one, down_two, down_three)
-    (grad_downs,) = unpack_grads(where, down_pieces, ((units, True),))
     kvq_pieces = cut_heads(where, (kvq_first, kvq_second))
+    both_pieces, kvq_pieces, grad_in_other, grad_one = tie(
+        both_pieces, kvq_pieces, grad_in_other, grad_one
+    )
+    kvq_pieces = [trade(kvq_pieces, k) for k in range(nz)]
     norm_sums = jnp.stack(
         [
             jnp.sum(grad_one * scaled_own, axis=0),
@@ -924,6 +932,7 @@
             jnp.sum(grad_two, axis=0),
         ]
     )
+    norm_sums = after(norm_sums, kvq_pieces[1])
     norm_sums = norm_sums + mirror(norm_sums)
     norm_sums = norm_sums.reshape(4, nz, ny, nb, rows)
 
@@ -934,12 +943,8 @@
             summed = summed + swap(pick(values, me ^ k, axis), name, k)
         return summed
 
-    norm_sums = sum_over(sum_over(norm_sums, "batch", 3), "col", 2)
-    both_pieces, kvq_pieces, grad_in_other, norm_sums, grad_gates, grad_ups, grad_downs = tie(
-        both_pieces, kvq_pieces, grad_in_other, norm_sums, grad_gates, grad_ups, grad_downs
-    )
-    norm_sums = sum_over(norm_sums, "row", 1)
-    kvq_pieces = [trade(kvq_pieces, k) for k in range(nz)]
+    for name, axis in (("batch", 3), ("col", 2), ("row", 1)):
+        norm_sums = sum_over(norm_sums, name, axis)
     grad_g, grad_outs = unpack_grads(where, both_pieces, ((DV, False), (DV, True)))
     grad_k, grad_v, grad_q = unpack_grads(
         where, kvq_pieces, ((DK, False), (DV, False), (DK, False))

time: 519 us -> 489 us (0.942)
  local copies, waits for them, and re-layouts: 34.3 us -> 18.7 us
  waiting for transfers between devices: 264 us -> 250 us
  other arithmetic: 17.2 us -> 11.3 us
    ppermute x90 -> x91, waiting for transfers between devices: 264 us -> 250 us  [swap(): return lax.ppermute(values, axis, [(i, i ^ k) for i in range(count)])]
    unnamed x178 -> x134, local copies, waits for them, and re-layouts: 23.7 us -> 14.9 us
    ppermute x90 -> x91, starting transfers between devices: 111 us -> 116 us  [swap(): return lax.ppermute(values, axis, [(i, i ^ k) for i in range(count)])]
  transfers between devices with their start and end apart: 90 -> 91, of which waited for: 47 -> 46; matrix products, arithmetic and copies ran while one was open for 6% -> 4% of each run, Pallas kernels for 7% -> 8%
where the time goes in v1:
time: 489 us; the launch traced here: 481 us
  waiting for transfers between devices  250 us (51%)
  starting transfers between devices  116 us (24%)
  Pallas kernels  64.8 us (13%)
  local copies, waits for them, and re-layouts  18.7 us (4%)
  matrix products  17.8 us (4%)
  other arithmetic  11.3 us (2%)
    ppermute x91, waiting for transfers between devices, swap(): return lax.ppermute(values, axis, [(i, i ^ k) for i in range(count)])  250 us
    ppermute x91, starting transfers between devices, swap(): return lax.ppermute(values, axis, [(i, i ^ k) for i in range(count)])  116 us
    pallas_call x32, Pallas kernels, call(): pl.pallas_call(kernel, grid=() if grid is None else grid, out_shape=shape...  43.3 us
    pallas_call x6, Pallas kernels, weight_grads(): pl.pallas_call(kernel, grid=(ny,), out_shape=shapes, in_specs=[SMEM] + [W...  16.9 us
    unnamed x134, local copies, waits for them, and re-layouts  14.9 us
    dot_general x5, matrix products, matmul(): return jnp.dot(values, weight, preferred_element_type=f32)  10.3 us
  transfers between devices with their start and end apart: 91, of which 46 were waited for; matrix products, arithmetic and copies ran while one was open for 4% of the time, Pallas kernels for 8%

profile of v1, /device:TPU:0, one launch (start us, length us, event | category | flops | bytes accessed | tf_op | source)
XLA Modules:
  0.0 481.1 jit_solution(8322502857667158484)
XLA Ops:
  4.8 3.1 collective-permute-start
  12.1 3.9 collective-permute-start.3
  21.3 10.9 %collective-permute-done.1 = bf16[144,768]{1,0:T(8,128)(2,1)S(1)} collective-permute-done((bf16[144,768]{1,0:T(8,128)(2,1)S(1)}, bf16[144,768]{1,0:T(8,128)(2,1)S(1)}, u32[]{:S(2)}, u32[]{:S(2)}) %collective-permute-start.1) | collective-permute-done | bytes 221216 | tf_op jit(solution)/shard_map/ppermute | solution.py:22
  32.3 6.9 %collective-permute-done.4 = bf16[2,128,768]{2,1,0:T(8,128)(2,1)S(1)} collective-permute-done((bf16[2,128,768]{2,1,0:T(8,128)(2,1)S(1)}, bf16[2,128,768]{2,1,0:T(8,128)(2,1)S(1)}, u32[]{:S(2)}, u32[]{:S(2)}) %collective-permute-start.4) | collective-permute-done | bytes 393248 | tf_op jit(solution)/shard_map/ppermute | solution.py:22
  40.9 2.7 collective-permute-start.7
  48.7 18.1 %collective-permute-done.8 = bf16[2,128,768]{2,1,0:T(8,128)(2,1)S(1)} collective-permute-done((bf16[2,128,768]{2,1,0:T(8,128)(2,1)S(1)}, bf16[2,128,768]{2,1,0:T(8,128)(2,1)S(1)}, u32[]{:S(2)}, u32[]{:S(2)}) %collective-permute-start.8) | collective-permute-done | bytes 393248 | tf_op jit(solution)/shard_map/ppermute | solution.py:22
  73.9 6.4 %collective-permute-done.12.refs_1_ = bf16[64,2048]{1,0:T(8,128)(2,1)S(1)} collective-permute-done((bf16[64,2048]{1,0:T(8,128)(2,1)S(1)}, bf16[64,2048]{1,0:T(8,128)(2,1)S(1)}, u32[]{:S(2)}, u32[]{:S(2)}) %collective-permute-start.12) | collective-permute-done | bytes 262176 | tf_op jit(solution)/shard_map/ppermute | solution.py:22
  80.3 4.6 collective-permute-done.13
  100.7 7.7 %collective-permute-done.17 = bf16[2,128,512]{2,1,0:T(8,128)(2,1)S(1)} collective-permute-done((bf16[2,128,512]{2,1,0:T(8,128)(2,1)S(1)}, bf16[2,128,512]{2,1,0:T(8,128)(2,1)S(1)}, u32[]{:S(2)}, u32[]{:S(2)}) %collective-permute-start.17) | collective-permute-done | bytes 262176 | tf_op jit(solution)/shard_map/ppermute | solution.py:22
  108.5 8.1 %collective-permute-done.18 = bf16[128,1536]{1,0:T(8,128)(2,1)S(1)} collective-permute-done((bf16[128,1536]{1,0:T(8,128)(2,1)S(1)}, bf16[128,1536]{1,0:T(8,128)(2,1)S(1)}, u32[]{:S(2)}, u32[]{:S(2)}) %collective-permute-start.18) | collective-permute-done | bytes 393248 | tf_op jit(solution)/shard_map/ppermute | solution.py:22
  121.0 7.1 %retention_forward.1 = (bf16[2,4,64,512]{3,2,1,0:T(8,128)(2,1)S(1)}, f32[2,4,64,512]{3,2,1,0:T(8,128)S(1)}, f32[2,4,64,1]{3,2,1,0:T(8,128)S(1)}, bf16[4,256,512]...) custom-call(s32[4]{0:T(128)S(1)} %pad_add_fusion.where_ref, f32[8,128]{1,0:T(8,128)S(1)} %get-tuple-element.334.decay_ref, ...), custom_call_target="tpu_custom_call" | custom-call | tf_op jit(solution)/shard_map/retention_forward/pallas_call | solution.py:80
  129.7 5.8 %collective-permute-done.21 = bf16[128,768]{1,0:T(8,128)(2,1)S(1)} collective-permute-done((bf16[128,768]{1,0:T(8,128)(2,1)S(1)}, bf16[128,768]{1,0:T(8,128)(2,1)S(1)}, u32[]{:S(2)}, u32[]{:S(2)}) %collective-permute-start.21) | collective-permute-done | bytes 196640 | tf_op jit(solution)/shard_map/ppermute | solution.py:22
  144.4 7.6 %collective-permute-done.25 = bf16[128,768]{1,0:T(8,128)(2,1)S(1)} collective-permute-done((bf16[128,768]{1,0:T(8,128)(2,1)S(1)}, bf16[128,768]{1,0:T(8,128)(2,1)S(1)}, u32[]{:S(2)}, u32[]{:S(2)}) %collective-permute-start.25) | collective-permute-done | bytes 196640 | tf_op jit(solution)/shard_map/ppermute | solution.py:22
  152.0 7.0 %collective-permute-done.26 = bf16[128,1536]{1,0:T(8,128)(2,1)S(1)} collective-permute-done((bf16[128,1536]{1,0:T(8,128)(2,1)S(1)}, bf16[128,1536]{1,0:T(8,128)(2,1)S(1)}, u32[]{:S(2)}, u32[]{:S(2)}) %collective-permute-start.26) | collective-permute-done | bytes 393248 | tf_op jit(solution)/shard_map/ppermute | solution.py:22
  162.5 13.3 %collective-permute-done.29.refs_2_ = bf16[4,128,512]{2,1,0:T(8,128)(2,1)S(1)} collective-permute-done((bf16[4,128,512]{2,1,0:T(8,128)(2,1)S(1)}, bf16[4,128,512]{2,1,0:T(8,128)(2,1)S(1)}, u32[]{:S(2)}, u32[]{:S(2)}) %collective-permute-start.29) | collective-permute-done | bytes 524320 | tf_op jit(solution)/shard_map/ppermute | solution.py:22
  180.8 6.9 %collective-permute-done.33.refs_4_ = bf16[64,2048]{1,0:T(8,128)(2,1)S(1)} collective-permute-done((bf16[64,2048]{1,0:T(8,128)(2,1)S(1)}, bf16[64,2048]{1,0:T(8,128)(2,1)S(1)}, u32[]{:S(2)}, u32[]{:S(2)}) %collective-permute-start.33) | collective-permute-done | bytes 262176 | tf_op jit(solution)/shard_map/ppermute | solution.py:22
  195.4 8.5 %collective-permute-done.35 = bf16[64,2048]{1,0:T(8,128)(2,1)S(1)} collective-permute-done((bf16[64,2048]{1,0:T(8,128)(2,1)S(1)}, bf16[64,2048]{1,0:T(8,128)(2,1)S(1)}, u32[]{:S(2)}, u32[]{:S(2)}) %collective-permute-start.35) | collective-permute-done | bytes 262176 | tf_op jit(solution)/shard_map/ppermute | solution.py:22
  205.0 6.9 %collective-permute-start.39 = (bf16[128,2048]{1,0:T(8,128)(2,1)S(1)}, bf16[128,2048]{1,0:T(8,128)(2,1)S(1)}, u32[]{:S(2)}, u32[]{:S(2)}) collective-permute-start(bf16[128,2048]{1,0:T(8,128)(2,1)S(1)} %constant_dynamic-update-slice_fusion.refs_0_), channel_id=1, source_target_pairs={{0,8},{8,0},{16,24},{24,16},{1,9},{9,1},{17,25},{25,17},{2,10},{10... | collective-permute-start | bytes 1572872 | tf_op jit(solution)/shard_map/ppermute | solution.py:22
  213.4 9.1 %collective-permute-done.39.refs_1_ = bf16[128,2048]{1,0:T(8,128)(2,1)S(1)} collective-permute-done((bf16[128,2048]{1,0:T(8,128)(2,1)S(1)}, bf16[128,2048]{1,0:T(8,128)(2,1)S(1)}, u32[]{:S(2)}, u32[]{:S(2)}) %collective-permute-start.39) | collective-permute-done | bytes 524320 | tf_op jit(solution)/shard_map/ppermute | solution.py:22
  227.7 4.1 collective-permute-done.43.refs_1_
  232.6 2.6 collective-permute-done.42.refs_3_
  240.1 2.6 far_messages.3
  245.6 2.7 weight_grads.6
  248.5 6.0 %collective-permute-done.44.got_ref = bf16[144,2048]{1,0:T(8,128)(2,1)S(1)} collective-permute-done((bf16[144,2048]{1,0:T(8,128)(2,1)S(1)}, bf16[144,2048]{1,0:T(8,128)(2,1)S(1)}, u32[]{:S(2)}, u32[]{:S(2)}) %collective-permute-start.44) | collective-permute-done | bytes 589856 | tf_op jit(solution)/shard_map/ppermute | solution.py:22
  260.1 3.3 weight_grads.7
  263.4 7.6 %collective-permute-done.45.got_ref = bf16[144,2048]{1,0:T(8,128)(2,1)S(1)} collective-permute-done((bf16[144,2048]{1,0:T(8,128)(2,1)S(1)}, bf16[144,2048]{1,0:T(8,128)(2,1)S(1)}, u32[]{:S(2)}, u32[]{:S(2)}) %collective-permute-start.45) | collective-permute-done | bytes 589856 | tf_op jit(solution)/shard_map/ppermute | solution.py:22
  278.1 11.3 %collective-permute-done.50 = bf16[512,512]{1,0:T(8,128)(2,1)S(1)} collective-permute-done((bf16[512,512]{1,0:T(8,128)(2,1)S(1)}, bf16[512,512]{1,0:T(8,128)(2,1)S(1)}, u32[]{:S(2)}, u32[]{:S(2)}) %collective-permute-start.50) | collective-permute-done | bytes 524320 | tf_op jit(solution)/shard_map/ppermute | solution.py:22
  297.2 6.7 %collective-permute-done.52 = bf16[512,512]{1,0:T(8,128)(2,1)S(1)} collective-permute-done((bf16[512,512]{1,0:T(8,128)(2,1)S(1)}, bf16[512,512]{1,0:T(8,128)(2,1)S(1)}, u32[]{:S(2)}, u32[]{:S(2)}) %collective-permute-start.52) | collective-permute-done | bytes 524320 | tf_op jit(solution)/shard_map/ppermute | solution.py:22
  304.1 9.3 %collective-permute-done.51 = bf16[64,2048]{1,0:T(8,128)(2,1)S(1)} collective-permute-done((bf16[64,2048]{1,0:T(8,128)(2,1)S(1)}, bf16[64,2048]{1,0:T(8,128)(2,1)S(1)}, u32[]{:S(2)}, u32[]{:S(2)}) %collective-permute-start.51) | collective-permute-done | bytes 262176 | tf_op jit(solution)/shard_map/ppermute | solution.py:22
  317.4 7.6 %collective-permute-done.57 = bf16[512,512]{1,0:T(8,128)(2,1)S(1)} collective-permute-done((bf16[512,512]{1,0:T(8,128)(2,1)S(1)}, bf16[512,512]{1,0:T(8,128)(2,1)S(1)}, u32[]{:S(2)}, u32[]{:S(2)}) %collective-permute-start.57) | collective-permute-done | bytes 524320 | tf_op jit(solution)/shard_map/ppermute | solution.py:22
  329.3 6.9 %collective-permute-done.59.refs_2_ = bf16[128,1024]{1,0:T(8,128)(2,1)S(1)} collective-permute-done((bf16[128,1024]{1,0:T(8,128)(2,1)S(1)}, bf16[128,1024]{1,0:T(8,128)(2,1)S(1)}, u32[]{:S(2)}, u32[]{:S(2)}) %collective-permute-start.59) | collective-permute-done | bytes 262176 | tf_op jit(solution)/shard_map/ppermute | solution.py:22
  337.0 2.6 fusion.34
  339.6 3.1 weight_grads.8
  350.6 3.2 weight_grads.9
  353.8 6.7 %collective-permute-done.63.refs_1_ = bf16[128,512]{1,0:T(8,128)(2,1)S(1)} collective-permute-done((bf16[128,512]{1,0:T(8,128)(2,1)}, bf16[128,512]{1,0:T(8,128)(2,1)S(1)}, u32[]{:S(2)}, u32[]{:S(2)}) %collective-permute-start.63) | collective-permute-done | bytes 131104 | tf_op jit(solution)/shard_map/ppermute | solution.py:22
  360.6 6.8 %retention_backward.1 = (bf16[2,4,64,768]{3,2,1,0:T(8,128)(2,1)S(1)}, bf16[2,4,64,768]{3,2,1,0:T(8,128)(2,1)S(1)}) custom-call(s32[4]{0:T(128)S(1)} %pad_add_fusion.where_ref, f32[8,128]{1,0:T(8,128)S(1)} %get-tuple-element.334.decay_ref, bf16[2,4,64,256]{3,2,1,0:T(8,128)(2,1)S(1)} %copy-done.48, bf16[2,4,64,256]{3,2,1,0:T(8,128)(2,1)S(1)} %copy-done.50, ...), custom_call_target="tpu_custom_call" | custom-call | tf_op jit(solution)/shard_map/retention_backward/pallas_call | solution.py:80
  382.5 5.9 %collective-permute-done.69 = bf16[512,512]{1,0:T(8,128)(2,1)S(1)} collective-permute-done((bf16[512,512]{1,0:T(8,128)(2,1)S(1)}, bf16[512,512]{1,0:T(8,128)(2,1)S(1)}, u32[]{:S(2)}, u32[]{:S(2)}) %collective-permute-start.69) | collective-permute-done | bytes 524320 | tf_op jit(solution)/shard_map/ppermute | solution.py:22
  388.5 3.0 collective-permute-done.66.refs_2_
  404.4 8.8 %collective-permute-done.73 = bf16[64,2048]{1,0:T(8,128)(2,1)S(1)} collective-permute-done((bf16[64,2048]{1,0:T(8,128)(2,1)S(1)}, bf16[64,2048]{1,0:T(8,128)(2,1)S(1)}, u32[]{:S(2)}, u32[]{:S(2)}) %collective-permute-start.73) | collective-permute-done | bytes 262176 | tf_op jit(solution)/shard_map/ppermute | solution.py:22
  419.1 5.9 %collective-permute-done.76 = bf16[512,512]{1,0:T(8,128)(2,1)S(1)} collective-permute-done((bf16[512,512]{1,0:T(8,128)(2,1)S(1)}, bf16[512,512]{1,0:T(8,128)(2,1)S(1)}, u32[]{:S(2)}, u32[]{:S(2)}) %collective-permute-start.76) | collective-permute-done | bytes 524320 | tf_op jit(solution)/shard_map/ppermute | solution.py:22
  428.1 3.5 collective-permute-start.78
  432.5 3.8 collective-permute-done.80
  438.5 10.1 %collective-permute-done.78.refs_2_ = bf16[128,1024]{1,0:T(8,128)(2,1)S(1)} collective-permute-done((bf16[128,1024]{1,0:T(8,128)(2,1)S(1)}, bf16[128,1024]{1,0:T(8,128)(2,1)S(1)}, u32[]{:S(2)}, u32[]{:S(2)}) %collective-permute-start.78) | collective-permute-done | bytes 262176 | tf_op jit(solution)/shard_map/ppermute | solution.py:22
  448.6 3.4 collective-permute-start.82
  452.3 4.1 collective-permute-done.82.refs_1_
  456.7 4.0 collective-permute-start.89
  463.5 2.7 collective-permute-done.85
  466.2 3.5 collective-permute-start.88
  (415 shorter events, 182.2 us)
Async XLA Ops:
  4.8 16.5 %collective-permute-start = (bf16[144,768]{1,0:T(8,128)(2,1)S(1)}, bf16[144,768]{1,0:T(8,128)(2,1)S(1)}, u32[]{:S(2)}, u32[]{:S(2)}) collective-permute-start(bf16[144,768]{1,0:T(8,128)(2,1)S(1)} %get-tuple-element.304), channel_id=1, source_target_pairs={{0,8},{8,0},{16,24},{24,16},{1,9},{9,1},{17,25},{25,17},{2,10},{10... | collective-permute-start | bytes 663560 | tf_op jit(solution)/shard_map/ppermute | solution.py:22
  7.9 24.4 %collective-permute-start.1 = (bf16[144,768]{1,0:T(8,128)(2,1)S(1)}, bf16[144,768]{1,0:T(8,128)(2,1)S(1)}, u32[]{:S(2)}, u32[]{:S(2)}) collective-permute-start(bf16[144,768]{1,0:T(8,128)(2,1)S(1)} %get-tuple-element.305), channel_id=1, source_target_pairs={{0,16},{8,24},{16,0},{24,8},{1,17},{9,25},{17,1},{25,9},{2,18},{10... | collective-permute-start | bytes 663560 | tf_op jit(solution)/shard_map/ppermute | solution.py:22
  10.5 21.8 %collective-permute-start.2 = (bf16[144,768]{1,0:T(8,128)(2,1)S(1)}, bf16[144,768]{1,0:T(8,128)(2,1)S(1)}, u32[]{:S(2)}, u32[]{:S(2)}) collective-permute-start(bf16[144,768]{1,0:T(8,128)(2,1)S(1)} %get-tuple-element.306), channel_id=1, source_target_pairs={{0,24},{8,16},{16,8},{24,0},{1,25},{9,17},{17,9},{25,1},{2,26},{10... | collective-permute-start | bytes 663560 | tf_op jit(solution)/shard_map/ppermute | solution.py:22
  12.1 20.2 %collective-permute-start.3 = (bf16[64,2048]{1,0:T(8,128)(2,1)S(1)}, bf16[64,2048]{1,0:T(8,128)(2,1)S(1)}, u32[]{:S(2)}, u32[]{:S(2)}) collective-permute-start(bf16[64,2048]{1,0:T(8,128)(2,1)S(1)} %get-tuple-element.302.refs_0_.in_ref), channel_id=1, source_target_pairs={{0,24},{8,16},{16,8},{24,0},{1,25},{9,17},{17,9},{25,1},{2,26},{10... | collective-permute-start | bytes 786440 | tf_op jit(solution)/shard_map/ppermute | solution.py:22
  18.6 20.5 %collective-permute-start.4 = (bf16[2,128,768]{2,1,0:T(8,128)(2,1)S(1)}, bf16[2,128,768]{2,1,0:T(8,128)(2,1)S(1)}, u32[]{:S(2)}, u32[]{:S(2)}) collective-permute-start(bf16[2,128,768]{2,1,0:T(8,128)(2,1)S(1)} %get-tuple-element.307), channel_id=1, source_target_pairs={{0,8},{8,0},{16,24},{24,16},{1,9},{9,1},{17,25},{25,17},{2,10},{10... | collective-permute-start | bytes 1179656 | tf_op jit(solution)/shard_map/ppermute | solution.py:22
  39.3 27.6 %collective-permute-start.5 = (bf16[4,144,768]{2,1,0:T(8,128)(2,1)S(1)}, bf16[4,144,768]{2,1,0:T(8,128)(2,1)S(1)}, u32[]{:S(2)}, u32[]{:S(2)}) collective-permute-start(bf16[4,144,768]{2,1,0:T(8,128)(2,1)S(1)} %pad_maximum_fusion.3.refs_0_), channel_id=1, source_target_pairs={{0,4},{4,0},{1,5},{5,1},{2,6},{6,2},{3,7},{7,3},{8,12},{12,8},{9,1... | collective-permute-start | bytes 2654216 | tf_op jit(solution)/shard_map/ppermute | solution.py:22
  40.8 26.0 %collective-permute-start.6 = (bf16[4,144,768]{2,1,0:T(8,128)(2,1)S(1)}, bf16[4,144,768]{2,1,0:T(8,128)(2,1)S(1)}, u32[]{:S(2)}, u32[]{:S(2)}) collective-permute-start(bf16[4,144,768]{2,1,0:T(8,128)(2,1)S(1)} %pad_maximum_fusion.3.refs_0_), channel_id=1, source_target_pairs={{0,2},{2,0},{1,3},{3,1},{4,6},{6,4},{5,7},{7,5},{8,10},{10,8},{9,1... | collective-permute-start | bytes 2654216 | tf_op jit(solution)/shard_map/ppermute | solution.py:22
  40.9 25.9 %collective-permute-start.7 = (bf16[128,2048]{1,0:T(8,128)(2,1)S(1)}, bf16[128,2048]{1,0:T(8,128)(2,1)S(1)}, u32[]{:S(2)}, u32[]{:S(2)}) collective-permute-start(bf16[128,2048]{1,0:T(8,128)(2,1)S(1)} %pad_maximum_fusion.7), channel_id=1, source_target_pairs={{0,8},{8,0},{16,24},{24,16},{1,9},{9,1},{17,25},{25,17},{2,10},{10... | collective-permute-start | bytes 1572872 | tf_op jit(solution)/shard_map/ppermute | solution.py:22
  43.7 23.1 %collective-permute-start.8 = (bf16[2,128,768]{2,1,0:T(8,128)(2,1)S(1)}, bf16[2,128,768]{2,1,0:T(8,128)(2,1)S(1)}, u32[]{:S(2)}, u32[]{:S(2)}) collective-permute-start(bf16[2,128,768]{2,1,0:T(8,128)(2,1)S(1)} %pad_maximum_fusion.10), channel_id=1, source_target_pairs={{0,24},{8,16},{16,8},{24,0},{1,25},{9,17},{17,9},{25,1},{2,26},{10... | collective-permute-start | bytes 1179656 | tf_op jit(solution)/shard_map/ppermute | solution.py:22
  66.8 21.6 %collective-permute-start.9 = (bf16[4,144,768]{2,1,0:T(8,128)(2,1)S(1)}, bf16[4,144,768]{2,1,0:T(8,128)(2,1)S(1)}, u32[]{:S(2)}, u32[]{:S(2)}) collective-permute-start(bf16[4,144,768]{2,1,0:T(8,128)(2,1)S(1)} %collective-permute-done.5.refs_2_), channel_id=1, source_target_pairs={{0,2},{2,0},{1,3},{3,1},{4,6},{6,4},{5,7},{7,5},{8,10},{10,8},{9,1... | collective-permute-start | bytes 2654216 | tf_op jit(solution)/shard_map/ppermute | solution.py:22
  67.0 20.0 %collective-permute-start.10 = (bf16[192,2048]{1,0:T(8,128)(2,1)S(1)}, bf16[192,2048]{1,0:T(8,128)(2,1)S(1)}, u32[]{:S(2)}, u32[]{:S(2)}) collective-permute-start(bf16[192,2048]{1,0:T(8,128)(2,1)S(1)} %pad_maximum_fusion.4), channel_id=1, source_target_pairs={{0,1},{1,0},{2,3},{3,2},{4,5},{5,4},{6,7},{7,6},{8,9},{9,8},{10,11... | collective-permute-start | bytes 2359304 | tf_op jit(solution)/shard_map/ppermute | solution.py:22
  68.7 19.7 %collective-permute-start.11 = (bf16[4,128,768]{2,1,0:T(8,128)(2,1)S(1)}, bf16[4,128,768]{2,1,0:T(8,128)(2,1)S(1)}, u32[]{:S(2)}, u32[]{:S(2)}) collective-permute-start(bf16[4,128,768]{2,1,0:T(8,128)(2,1)S(1)} %pad_maximum_fusion.5.refs_0_), channel_id=1, source_target_pairs={{0,4},{4,0},{1,5},{5,1},{2,6},{6,2},{3,7},{7,3},{8,12},{12,8},{9,1... | collective-permute-start | bytes 2359304 | tf_op jit(solution)/shard_map/ppermute | solution.py:22
  70.6 14.3 %collective-permute-start.13 = (bf16[2,128,512]{2,1,0:T(8,128)(2,1)S(1)}, bf16[2,128,512]{2,1,0:T(8,128)(2,1)S(1)}, u32[]{:S(2)}, u32[]{:S(2)}) collective-permute-start(bf16[2,128,512]{2,1,0:T(8,128)(2,1)S(1)} %get-tuple-element.327), channel_id=1, source_target_pairs={{0,24},{8,16},{16,8},{24,0},{1,25},{9,17},{17,9},{25,1},{2,26},{10... | collective-permute-start | bytes 786440 | tf_op jit(solution)/shard_map/ppermute | solution.py:22
  93.9 22.7 %collective-permute-start.14 = (bf16[2,4,64,768]{3,2,1,0:T(8,128)(2,1)S(1)}, bf16[2,4,64,768]{3,2,1,0:T(8,128)(2,1)S(1)}, u32[]{:S(2)}, u32[]{:S(2)}) collective-permute-start(bf16[2,4,64,768]{3,2,1,0:T(8,128)(2,1)S(1)} %pad_maximum_fusion.6.refs_0_.refs_4_), channel_id=1, source_target_pairs={{0,4},{4,0},{1,5},{5,1},{2,6},{6,2},{3,7},{7,3},{8,12},{12,8},{9,1... | collective-permute-start | bytes 2359304 | tf_op jit(solution)/shard_map/ppermute | solution.py:22
  94.5 14.0 %collective-permute-start.17 = (bf16[2,128,512]{2,1,0:T(8,128)(2,1)S(1)}, bf16[2,128,512]{2,1,0:T(8,128)(2,1)S(1)}, u32[]{:S(2)}, u32[]{:S(2)}) collective-permute-start(bf16[2,128,512]{2,1,0:T(8,128)(2,1)S(1)} %pad_maximum_fusion.11), channel_id=1, source_target_pairs={{0,8},{8,0},{16,24},{24,16},{1,9},{9,1},{17,25},{25,17},{2,10},{10... | collective-permute-start | bytes 786440 | tf_op jit(solution)/shard_map/ppermute | solution.py:22
  96.7 19.9 %collective-permute-start.18 = (bf16[128,1536]{1,0:T(8,128)(2,1)S(1)}, bf16[128,1536]{1,0:T(8,128)(2,1)S(1)}, u32[]{:S(2)}, u32[]{:S(2)}) collective-permute-start(bf16[128,1536]{1,0:T(8,128)(2,1)S(1)} %get-tuple-element.353), channel_id=1, source_target_pairs={{0,16},{8,24},{16,0},{24,8},{1,17},{9,25},{17,1},{25,9},{2,18},{10... | collective-permute-start | bytes 1179656 | tf_op jit(solution)/shard_map/ppermute | solution.py:22
  116.7 18.9 %collective-permute-start.19 = (bf16[4,128,512]{2,1,0:T(8,128)(2,1)S(1)}, bf16[4,128,512]{2,1,0:T(8,128)(2,1)S(1)}, u32[]{:S(2)}, u32[]{:S(2)}) collective-permute-start(bf16[4,128,512]{2,1,0:T(8,128)(2,1)S(1)} %pad_maximum_fusion.8.refs_0_), channel_id=1, source_target_pairs={{0,4},{4,0},{1,5},{5,1},{2,6},{6,2},{3,7},{7,3},{8,12},{12,8},{9,1... | collective-permute-start | bytes 1572872 | tf_op jit(solution)/shard_map/ppermute | solution.py:22
  118.3 17.2 %collective-permute-start.20 = (bf16[128,2048]{1,0:T(8,128)(2,1)S(1)}, bf16[128,2048]{1,0:T(8,128)(2,1)S(1)}, u32[]{:S(2)}, u32[]{:S(2)}) collective-permute-start(bf16[128,2048]{1,0:T(8,128)(2,1)S(1)} %pad_maximum_fusion.9), channel_id=1, source_target_pairs={{0,8},{8,0},{16,24},{24,16},{1,9},{9,1},{17,25},{25,17},{2,10},{10... | collective-permute-start | bytes 1572872 | tf_op jit(solution)/shard_map/ppermute | solution.py:22
  118.4 17.1 %collective-permute-start.21 = (bf16[128,768]{1,0:T(8,128)(2,1)S(1)}, bf16[128,768]{1,0:T(8,128)(2,1)S(1)}, u32[]{:S(2)}, u32[]{:S(2)}) collective-permute-start(bf16[128,768]{1,0:T(8,128)(2,1)S(1)} %slice.219), channel_id=1, source_target_pairs={{0,24},{8,16},{16,8},{24,0},{1,25},{9,17},{17,9},{25,1},{2,26},{10... | collective-permute-start | bytes 589832 | tf_op jit(solution)/shard_map/ppermute | solution.py:22
  141.0 18.0 %collective-permute-start.24 = (bf16[144,2048]{1,0:T(8,128)(2,1)S(1)}, bf16[144,2048]{1,0:T(8,128)(2,1)S(1)}, u32[]{:S(2)}, u32[]{:S(2)}) collective-permute-start(bf16[144,2048]{1,0:T(8,128)(2,1)S(1)} %get-tuple-element.368), channel_id=1, source_target_pairs={{0,1},{1,0},{2,3},{3,2},{4,5},{5,4},{6,7},{7,6},{8,9},{9,8},{10,11... | collective-permute-start | bytes 1769480 | tf_op jit(solution)/shard_map/ppermute | solution.py:22
  144.1 14.8 %collective-permute-start.26 = (bf16[128,1536]{1,0:T(8,128)(2,1)S(1)}, bf16[128,1536]{1,0:T(8,128)(2,1)S(1)}, u32[]{:S(2)}, u32[]{:S(2)}) collective-permute-start(bf16[128,1536]{1,0:T(8,128)(2,1)S(1)} %get-tuple-element.373), channel_id=1, source_target_pairs={{0,8},{8,0},{16,24},{24,16},{1,9},{9,1},{17,25},{25,17},{2,10},{10... | collective-permute-start | bytes 1179656 | tf_op jit(solution)/shard_map/ppermute | solution.py:22
  159.2 16.7 %collective-permute-start.30 = (bf16[4,128,1536]{2,1,0:T(8,128)(2,1)S(1)}, bf16[4,128,1536]{2,1,0:T(8,128)(2,1)S(1)}, u32[]{:S(2)}, u32[]{:S(2)}) collective-permute-start(bf16[4,128,1536]{2,1,0:T(8,128)(2,1)S(1)} %pad_maximum_fusion.1.refs_0_), channel_id=1, source_target_pairs={{0,2},{2,0},{1,3},{3,1},{4,6},{6,4},{5,7},{7,5},{8,10},{10,8},{9,1... | collective-permute-start | bytes 4718600 | tf_op jit(solution)/shard_map/ppermute | solution.py:22
  160.0 15.8 %collective-permute-start.27 = (bf16[144,2048]{1,0:T(8,128)(2,1)S(1)}, bf16[144,2048]{1,0:T(8,128)(2,1)S(1)}, u32[]{:S(2)}, u32[]{:S(2)}) collective-permute-start(bf16[144,2048]{1,0:T(8,128)(2,1)S(1)} %pass_message.2), channel_id=1, source_target_pairs={{0,8},{8,0},{16,24},{24,16},{1,9},{9,1},{17,25},{25,17},{2,10},{10... | collective-permute-start | bytes 1769480 | tf_op jit(solution)/shard_map/ppermute | solution.py:22
  160.4 15.4 %collective-permute-start.28 = (bf16[144,2048]{1,0:T(8,128)(2,1)S(1)}, bf16[144,2048]{1,0:T(8,128)(2,1)S(1)}, u32[]{:S(2)}, u32[]{:S(2)}) collective-permute-start(bf16[144,2048]{1,0:T(8,128)(2,1)S(1)} %get-tuple-element.377), channel_id=1, source_target_pairs={{0,1},{1,0},{2,3},{3,2},{4,5},{5,4},{6,7},{7,6},{8,9},{9,8},{10,11... | collective-permute-start | bytes 1769480 | tf_op jit(solution)/shard_map/ppermute | solution.py:22
  161.9 13.8 %collective-permute-start.29 = (bf16[4,128,512]{2,1,0:T(8,128)(2,1)S(1)}, bf16[4,128,512]{2,1,0:T(8,128)(2,1)S(1)}, u32[]{:S(2)}, u32[]{:S(2)}) collective-permute-start(bf16[4,128,512]{2,1,0:T(8,128)(2,1)S(1)} %slice.276), channel_id=1, source_target_pairs={{0,4},{4,0},{1,5},{5,1},{2,6},{6,2},{3,7},{7,3},{8,12},{12,8},{9,1... | collective-permute-start | bytes 1572872 | tf_op jit(solution)/shard_map/ppermute | solution.py:22
  176.7 13.5 %collective-permute-start.32 = (bf16[4,128,512]{2,1,0:T(8,128)(2,1)S(1)}, bf16[4,128,512]{2,1,0:T(8,128)(2,1)S(1)}, u32[]{:S(2)}, u32[]{:S(2)}) collective-permute-start(bf16[4,128,512]{2,1,0:T(8,128)(2,1)S(1)} %slice.226), channel_id=1, source_target_pairs={{0,4},{4,0},{1,5},{5,1},{2,6},{6,2},{3,7},{7,3},{8,12},{12,8},{9,1... | collective-permute-start | bytes 1572872 | tf_op jit(solution)/shard_map/ppermute | solution.py:22
  191.8 13.2 %collective-permute-start.37 = (bf16[128,2048]{1,0:T(8,128)(2,1)S(1)}, bf16[128,2048]{1,0:T(8,128)(2,1)S(1)}, u32[]{:S(2)}, u32[]{:S(2)}) collective-permute-start(bf16[128,2048]{1,0:T(8,128)(2,1)S(1)} %collective-permute-done.20.refs_2_), channel_id=1, source_target_pairs={{0,1},{1,0},{2,3},{3,2},{4,5},{5,4},{6,7},{7,6},{8,9},{9,8},{10,11... | collective-permute-start | bytes 1572872 | tf_op jit(solution)/shard_map/ppermute | solution.py:22
  205.0 17.5 %collective-permute-start.39 = (bf16[128,2048]{1,0:T(8,128)(2,1)S(1)}, bf16[128,2048]{1,0:T(8,128)(2,1)S(1)}, u32[]{:S(2)}, u32[]{:S(2)}) collective-permute-start(bf16[128,2048]{1,0:T(8,128)(2,1)S(1)} %constant_dynamic-update-slice_fusion.refs_0_), channel_id=1, source_target_pairs={{0,8},{8,0},{16,24},{24,16},{1,9},{9,1},{17,25},{25,17},{2,10},{10... | collective-permute-start | bytes 1572872 | tf_op jit(solution)/shard_map/ppermute | solution.py:22
  255.2 15.8 %collective-permute-start.45 = (bf16[144,2048]{1,0:T(8,128)(2,1)S(1)}, bf16[144,2048]{1,0:T(8,128)(2,1)S(1)}, u32[]{:S(2)}, u32[]{:S(2)}) collective-permute-start(bf16[144,2048]{1,0:T(8,128)(2,1)S(1)} %pass_message.3), channel_id=1, source_target_pairs={{0,8},{8,0},{16,24},{24,16},{1,9},{9,1},{17,25},{25,17},{2,10},{10... | collective-permute-start | bytes 1769480 | tf_op jit(solution)/shard_map/ppermute | solution.py:22
  256.0 15.5 %collective-permute-start.46 = (bf16[144,2048]{1,0:T(8,128)(2,1)S(1)}, bf16[144,2048]{1,0:T(8,128)(2,1)S(1)}, u32[]{:S(2)}, u32[]{:S(2)}) collective-permute-start(bf16[144,2048]{1,0:T(8,128)(2,1)S(1)} %get-tuple-element.439), channel_id=1, source_target_pairs={{0,1},{1,0},{2,3},{3,2},{4,5},{5,4},{6,7},{7,6},{8,9},{9,8},{10,11... | collective-permute-start | bytes 1769480 | tf_op jit(solution)/shard_map/ppermute | solution.py:22
  272.2 17.4 %collective-permute-start.48 = (bf16[80,2048]{1,0:T(8,128)(2,1)S(1)}, bf16[80,2048]{1,0:T(8,128)(2,1)S(1)}, u32[]{:S(2)}, u32[]{:S(2)}) collective-permute-start(bf16[80,2048]{1,0:T(8,128)(2,1)S(1)} %get-tuple-element.447), channel_id=1, source_target_pairs={{0,24},{8,16},{16,8},{24,0},{1,25},{9,17},{17,9},{25,1},{2,26},{10... | collective-permute-start | bytes 983048 | tf_op jit(solution)/shard_map/ppermute | solution.py:22
  274.4 15.2 %collective-permute-start.49 = (bf16[128,2048]{1,0:T(8,128)(2,1)S(1)}, bf16[128,2048]{1,0:T(8,128)(2,1)S(1)}, u32[]{:S(2)}, u32[]{:S(2)}) collective-permute-start(bf16[128,2048]{1,0:T(8,128)(2,1)S(1)} %get-tuple-element.448), channel_id=1, source_target_pairs={{0,1},{1,0},{2,3},{3,2},{4,5},{5,4},{6,7},{7,6},{8,9},{9,8},{10,11... | collective-permute-start | bytes 1572872 | tf_op jit(solution)/shard_map/ppermute | solution.py:22
  293.3 20.1 %collective-permute-start.53 = (bf16[128,2048]{1,0:T(8,128)(2,1)S(1)}, bf16[128,2048]{1,0:T(8,128)(2,1)S(1)}, u32[]{:S(2)}, u32[]{:S(2)}) collective-permute-start(bf16[128,2048]{1,0:T(8,128)(2,1)S(1)} %get-tuple-element.469), channel_id=1, source_target_pairs={{0,1},{1,0},{2,3},{3,2},{4,5},{5,4},{6,7},{7,6},{8,9},{9,8},{10,11... | collective-permute-start | bytes 1572872 | tf_op jit(solution)/shard_map/ppermute | solution.py:22
  295.2 18.2 %collective-permute-start.54 = (bf16[128,2048]{1,0:T(8,128)(2,1)S(1)}, bf16[128,2048]{1,0:T(8,128)(2,1)S(1)}, u32[]{:S(2)}, u32[]{:S(2)}) collective-permute-start(bf16[128,2048]{1,0:T(8,128)(2,1)S(1)} %add_convert_fusion.1), channel_id=1, source_target_pairs={{0,8},{8,0},{16,24},{24,16},{1,9},{9,1},{17,25},{25,17},{2,10},{10... | collective-permute-start | bytes 1572872 | tf_op jit(solution)/shard_map/ppermute | solution.py:22
  295.5 17.9 %collective-permute-start.51 = (bf16[64,2048]{1,0:T(8,128)(2,1)S(1)}, bf16[64,2048]{1,0:T(8,128)(2,1)S(1)}, u32[]{:S(2)}, u32[]{:S(2)}) collective-permute-start(bf16[64,2048]{1,0:T(8,128)(2,1)S(1)} %get-tuple-element.463), channel_id=1, source_target_pairs={{0,24},{8,16},{16,8},{24,0},{1,25},{9,17},{17,9},{25,1},{2,26},{10... | collective-permute-start | bytes 786440 | tf_op jit(solution)/shard_map/ppermute | solution.py:22
  345.9 14.6 %collective-permute-start.61 = (bf16[2,4,64,512]{3,2,1,0:T(8,128)(2,1)S(1)}, bf16[2,4,64,512]{3,2,1,0:T(8,128)(2,1)S(1)}, u32[]{:S(2)}, u32[]{:S(2)}) collective-permute-start(bf16[2,4,64,512]{3,2,1,0:T(8,128)(2,1)S(1)} %bitcast.121), channel_id=1, source_target_pairs={{0,4},{4,0},{1,5},{5,1},{2,6},{6,2},{3,7},{7,3},{8,12},{12,8},{9,1... | collective-permute-start | bytes 1572872 | tf_op jit(solution)/shard_map/ppermute | solution.py:22
  347.5 13.0 %collective-permute-start.62 = (bf16[128,1024]{1,0:T(8,128)(2,1)}, bf16[128,1024]{1,0:T(8,128)(2,1)S(1)}, u32[]{:S(2)}, u32[]{:S(2)}) collective-permute-start(bf16[128,1024]{1,0:T(8,128)(2,1)} %copy-done.56), channel_id=1, source_target_pairs={{0,24},{8,16},{16,8},{24,0},{1,25},{9,17},{17,9},{25,1},{2,26},{10... | collective-permute-start | bytes 786440 | tf_op jit(solution)/shard_map/ppermute | solution.py:22
  372.8 18.7 %collective-permute-start.68 = (bf16[1024,1024]{1,0:T(8,128)(2,1)S(1)}, bf16[1024,1024]{1,0:T(8,128)(2,1)S(1)}, u32[]{:S(2)}, u32[]{:S(2)}) collective-permute-start(bf16[1024,1024]{1,0:T(8,128)(2,1)S(1)} %weight_grads.10), channel_id=1, source_target_pairs={{0,2},{2,0},{1,3},{3,1},{4,6},{6,4},{5,7},{7,5},{8,10},{10,8},{9,1... | collective-permute-start | bytes 6291464 | tf_op jit(solution)/shard_map/ppermute | solution.py:22
  373.0 18.5 %collective-permute-start.65 = (bf16[128,2048]{1,0:T(8,128)(2,1)S(1)}, bf16[128,2048]{1,0:T(8,128)(2,1)S(1)}, u32[]{:S(2)}, u32[]{:S(2)}) collective-permute-start(bf16[128,2048]{1,0:T(8,128)(2,1)S(1)} %get-tuple-element.617), channel_id=1, source_target_pairs={{0,1},{1,0},{2,3},{3,2},{4,5},{5,4},{6,7},{7,6},{8,9},{9,8},{10,11... | collective-permute-start | bytes 1572872 | tf_op jit(solution)/shard_map/ppermute | solution.py:22
  374.2 14.1 %collective-permute-start.69 = (bf16[512,512]{1,0:T(8,128)(2,1)S(1)}, bf16[512,512]{1,0:T(8,128)(2,1)S(1)}, u32[]{:S(2)}, u32[]{:S(2)}) collective-permute-start(bf16[512,512]{1,0:T(8,128)(2,1)S(1)} %slice.257), channel_id=1, source_target_pairs={{0,4},{4,0},{1,5},{5,1},{2,6},{6,2},{3,7},{7,3},{8,12},{12,8},{9,1... | collective-permute-start | bytes 1572872 | tf_op jit(solution)/shard_map/ppermute | solution.py:22
  392.4 20.8 %collective-permute-start.70 = (bf16[128,2048]{1,0:T(8,128)(2,1)S(1)}, bf16[128,2048]{1,0:T(8,128)(2,1)S(1)}, u32[]{:S(2)}, u32[]{:S(2)}) collective-permute-start(bf16[128,2048]{1,0:T(8,128)(2,1)S(1)} %add_convert_fusion), channel_id=1, source_target_pairs={{0,8},{8,0},{16,24},{24,16},{1,9},{9,1},{17,25},{25,17},{2,10},{10... | collective-permute-start | bytes 1572872 | tf_op jit(solution)/shard_map/ppermute | solution.py:22
  395.0 18.2 %collective-permute-start.71 = (bf16[128,2048]{1,0:T(8,128)(2,1)S(1)}, bf16[128,2048]{1,0:T(8,128)(2,1)S(1)}, u32[]{:S(2)}, u32[]{:S(2)}) collective-permute-start(bf16[128,2048]{1,0:T(8,128)(2,1)S(1)} %get-tuple-element.527), channel_id=1, source_target_pairs={{0,1},{1,0},{2,3},{3,2},{4,5},{5,4},{6,7},{7,6},{8,9},{9,8},{10,11... | collective-permute-start | bytes 1572872 | tf_op jit(solution)/shard_map/ppermute | solution.py:22
  398.1 15.1 %collective-permute-start.73 = (bf16[64,2048]{1,0:T(8,128)(2,1)S(1)}, bf16[64,2048]{1,0:T(8,128)(2,1)S(1)}, u32[]{:S(2)}, u32[]{:S(2)}) collective-permute-start(bf16[64,2048]{1,0:T(8,128)(2,1)S(1)} %copy-done.64), channel_id=1, source_target_pairs={{0,24},{8,16},{16,8},{24,0},{1,25},{9,17},{17,9},{25,1},{2,26},{10... | collective-permute-start | bytes 786440 | tf_op jit(solution)/shard_map/ppermute | solution.py:22
  427.0 21.7 %collective-permute-start.81 = (f32[64,2048]{1,0:T(8,128)S(1)}, f32[64,2048]{1,0:T(8,128)S(1)}, u32[]{:S(2)}, u32[]{:S(2)}) collective-permute-start(f32[64,2048]{1,0:T(8,128)S(1)} %fusion.21.own_ref), channel_id=1, source_target_pairs={{0,1},{1,0},{2,3},{3,2},{4,5},{5,4},{6,7},{7,6},{8,9},{9,8},{10,11... | collective-permute-start | bytes 1572872 | tf_op jit(solution)/shard_map/ppermute | solution.py:22
  428.1 20.5 %collective-permute-start.78 = (bf16[128,1024]{1,0:T(8,128)(2,1)S(1)}, bf16[128,1024]{1,0:T(8,128)(2,1)S(1)}, u32[]{:S(2)}, u32[]{:S(2)}) collective-permute-start(bf16[128,1024]{1,0:T(8,128)(2,1)S(1)} %get-tuple-element.561), channel_id=1, source_target_pairs={{0,16},{8,24},{16,0},{24,8},{1,17},{9,25},{17,1},{25,9},{2,18},{10... | collective-permute-start | bytes 786440 | tf_op jit(solution)/shard_map/ppermute | solution.py:22
  431.7 16.9 %collective-permute-start.79 = (bf16[128,1024]{1,0:T(8,128)(2,1)S(1)}, bf16[128,1024]{1,0:T(8,128)(2,1)S(1)}, u32[]{:S(2)}, u32[]{:S(2)}) collective-permute-start(bf16[128,1024]{1,0:T(8,128)(2,1)S(1)} %get-tuple-element.562), channel_id=1, source_target_pairs={{0,24},{8,16},{16,8},{24,0},{1,25},{9,17},{17,9},{25,1},{2,26},{10... | collective-permute-start | bytes 786440 | tf_op jit(solution)/shard_map/ppermute | solution.py:22
  456.7 19.3 %collective-permute-start.89 = (bf16[128,1024]{1,0:T(8,128)(2,1)}, bf16[128,1024]{1,0:T(8,128)(2,1)S(1)}, u32[]{:S(2)}, u32[]{:S(2)}) collective-permute-start(bf16[128,1024]{1,0:T(8,128)(2,1)} %copy-done.55), channel_id=1, source_target_pairs={{0,16},{8,24},{16,0},{24,8},{1,17},{9,25},{17,1},{25,9},{2,18},{10... | collective-permute-start | bytes 786440 | tf_op jit(solution)/shard_map/ppermute | solution.py:22
  460.6 15.3 %collective-permute-start.90 = (bf16[128,1024]{1,0:T(8,128)(2,1)}, bf16[128,1024]{1,0:T(8,128)(2,1)}, u32[]{:S(2)}, u32[]{:S(2)}) collective-permute-start(bf16[128,1024]{1,0:T(8,128)(2,1)} %copy-done.54), channel_id=1, source_target_pairs={{0,24},{8,16},{16,8},{24,0},{1,25},{9,17},{17,9},{25,1},{2,26},{10... | collective-permute-start | bytes 786440 | tf_op jit(solution)/shard_map/ppermute | solution.py:22
  (109 other events, 1499.5 us)

commit v2 on v1

--- a/solution.py
+++ b/solution.py
@@ -748,22 +748,22 @@
     )
     keyvals, query_gate, out_last, feed_two = tie(keyvals, query_gate, out_last, feed_two)
     out_cols = over_col(jnp.stack(in_order(out, out_got, out_last, 3)))
-    late_grad, late_two, late_three = after((own_grad, two_grad, feed[3]), keyvals)
+    late_one, late_three = after((feed[1], feed[3]), keyvals)
     middle_col = late_three.shape[1] // 2
     feed_left = swap(late_three[:, :middle_col], "row", 3)
-    one_grad = swap(jnp.concatenate([late_grad, late_two]), "row", 1)
+    feed_one = swap(late_one, "row", 1)
     mixed, normed, rstd, states, query = retention_forward(where, decays, keyvals, query_gate)
-    mixed, out_cols, one_grad, feed_left = tie(mixed, out_cols, one_grad, feed_left)
+    mixed, out_cols, feed_one, feed_left = tie(mixed, out_cols, feed_one, feed_left)
     (out_w,) = assemble(where, pairs(out_cols, over_batch(out_cols)), ny, nb, (DV,))
     mixed_bf = mixed.reshape(tokens, DV)
 
     far = far_messages(where, mixed_bf, out_w, part)
     got = mirror(far[0])
     near = reduce_near((mixed_bf, out_w))
-    late_feed = after(feed, far)
-    feed_right = swap(late_feed[3][:, middle_col:], "row", 3)
-    feed_one = trade(late_feed, 1)
-    got, near, feed_right, feed_one = tie(got, near, feed_right, feed_one)
+    late_three, late_grad, late_two = after((feed[3], own_grad, two_grad), far)
+    feed_right = swap(late_three[:, middle_col:], "row", 3)
+    one_grad = swap(jnp.concatenate([late_grad, late_two]), "row", 1)
+    got, near, feed_right, one_grad = tie(got, near, feed_right, one_grad)
     feed_three = jnp.concatenate([feed_left, feed_right], axis=-1)
     got_far = mirror(after(far[1], got))
     got = swap(pass_message(where, near[0], got, part), "row", 1)
@@ -869,10 +869,12 @@
     grad_mixed = matmul(attn_bf, out_w)
     grad_gate = (grad_mixed * grp_norm * (gate_sig * (1.0 + gate * (1.0 - gate_sig)))).astype(bf16)
     ret_bf = norm_back(grad_mixed * gate_act, grp_norm, grp_rstd).astype(bf16)
-    ret_bf, wide_grads, down_grads = tie(split(ret_bf), wide_grads, down_grads)
+    ret_bf, wide_grads, down_grads, late_gate, late_mixed = tie(
+        split(ret_bf), wide_grads, down_grads, grad_gate, mixed_bf
+    )
     ret_all = over_col(ret_bf)
     wide_three, down_one = trade(wide_grads, 3), trade(down_grads, 1)
-    lefts, rights = (first_bf, attn_bf), (grad_gate, mixed_bf)
+    lefts, rights = (first_bf, attn_bf), (late_gate, late_mixed)
     both_got = swap(weight_grads(where, lefts, rights, sizes), "batch", 1)
     both_keeps, both_sends = weight_grads(where, lefts, rights, sizes, (DV, DV), both_got)
     ret_all, wide_three, down_one, both_sends = tie(ret_all, wide_three, down_one, both_sends)
@@ -932,7 +934,7 @@
             jnp.sum(grad_two, axis=0),
         ]
     )
-    norm_sums = after(norm_sums, kvq_pieces[1])
+    norm_sums = after(norm_sums, kvq_pieces[1:3])
     norm_sums = norm_sums + mirror(norm_sums)
     norm_sums = norm_sums.reshape(4, nz, ny, nb, rows)
 

time: 489 us -> 499 us (1.020)
  waiting for transfers between devices: 250 us -> 259 us
    ppermute x91, waiting for transfers between devices: 250 us -> 259 us  [swap(): return lax.ppermute(values, axis, [(i, i ^ k) for i in range(count)])]
    unnamed x134 -> x122, local copies, waits for them, and re-layouts: 14.9 us -> 16.8 us
  transfers between devices with their start and end apart: 91 -> 91, of which waited for: 46 -> 47; matrix products, arithmetic and copies ran while one was open for 4% -> 4% of each run, Pallas kernels for 8% -> 8%
where the time goes in v2:
time: 499 us; the launch traced here: 491 us
  waiting for transfers between devices  259 us (52%)
  starting transfers between devices  115 us (23%)
  Pallas kernels  65 us (13%)
  local copies, waits for them, and re-layouts  20.8 us (4%)
  matrix products  16.9 us (3%)
  other arithmetic  10.6 us (2%)
    ppermute x91, waiting for transfers between devices, swap(): return lax.ppermute(values, axis, [(i, i ^ k) for i in range(count)])  259 us
    ppermute x91, starting transfers between devices, swap(): return lax.ppermute(values, axis, [(i, i ^ k) for i in range(count)])  115 us
    pallas_call x32, Pallas kernels, call(): pl.pallas_call(kernel, grid=() if grid is None else grid, out_shape=shape...  45.3 us
    unnamed x122, local copies, waits for them, and re-layouts  16.8 us
    pallas_call x6, Pallas kernels, weight_grads(): pl.pallas_call(kernel, grid=(ny,), out_shape=shapes, in_specs=[SMEM] + [W...  15 us
  transfers between devices with their start and end apart: 91, of which 47 were waited for; matrix products, arithmetic and copies ran while one was open for 4% of the time, Pallas kernels for 8%

profile of v2, /device:TPU:0, one launch (start us, length us, event | category | flops | bytes accessed | tf_op | source)
XLA Modules:
  0.0 490.8 jit_solution(17623245863647889328)
XLA Ops:
  4.8 3.1 collective-permute-start
  7.9 2.6 collective-permute-start.1
  12.1 3.9 collective-permute-start.3
  21.3 11.0 %collective-permute-done.1 = bf16[144,768]{1,0:T(8,128)(2,1)S(1)} collective-permute-done((bf16[144,768]{1,0:T(8,128)(2,1)S(1)}, bf16[144,768]{1,0:T(8,128)(2,1)S(1)}, u32[]{:S(2)}, u32[]{:S(2)}) %collective-permute-start.1) | collective-permute-done | bytes 221216 | tf_op jit(solution)/shard_map/ppermute | solution.py:22
  32.3 6.9 %collective-permute-done.4 = bf16[2,128,768]{2,1,0:T(8,128)(2,1)S(1)} collective-permute-done((bf16[2,128,768]{2,1,0:T(8,128)(2,1)S(1)}, bf16[2,128,768]{2,1,0:T(8,128)(2,1)S(1)}, u32[]{:S(2)}, u32[]{:S(2)}) %collective-permute-start.4) | collective-permute-done | bytes 393248 | tf_op jit(solution)/shard_map/ppermute | solution.py:22
  40.9 2.7 collective-permute-start.7
  48.7 18.1 %collective-permute-done.8 = bf16[2,128,768]{2,1,0:T(8,128)(2,1)S(1)} collective-permute-done((bf16[2,128,768]{2,1,0:T(8,128)(2,1)S(1)}, bf16[2,128,768]{2,1,0:T(8,128)(2,1)S(1)}, u32[]{:S(2)}, u32[]{:S(2)}) %collective-permute-start.8) | collective-permute-done | bytes 393248 | tf_op jit(solution)/shard_map/ppermute | solution.py:22
  73.9 6.4 %collective-permute-done.12.refs_1_ = bf16[64,2048]{1,0:T(8,128)(2,1)S(1)} collective-permute-done((bf16[64,2048]{1,0:T(8,128)(2,1)S(1)}, bf16[64,2048]{1,0:T(8,128)(2,1)S(1)}, u32[]{:S(2)}, u32[]{:S(2)}) %collective-permute-start.12) | collective-permute-done | bytes 262176 | tf_op jit(solution)/shard_map/ppermute | solution.py:22
  80.3 4.6 collective-permute-done.13
  100.8 7.7 %collective-permute-done.17 = bf16[2,128,512]{2,1,0:T(8,128)(2,1)S(1)} collective-permute-done((bf16[2,128,512]{2,1,0:T(8,128)(2,1)S(1)}, bf16[2,128,512]{2,1,0:T(8,128)(2,1)S(1)}, u32[]{:S(2)}, u32[]{:S(2)}) %collective-permute-start.17) | collective-permute-done | bytes 262176 | tf_op jit(solution)/shard_map/ppermute | solution.py:22
  108.5 8.1 %collective-permute-done.18 = bf16[128,1536]{1,0:T(8,128)(2,1)S(1)} collective-permute-done((bf16[128,1536]{1,0:T(8,128)(2,1)S(1)}, bf16[128,1536]{1,0:T(8,128)(2,1)S(1)}, u32[]{:S(2)}, u32[]{:S(2)}) %collective-permute-start.18) | collective-permute-done | bytes 393248 | tf_op jit(solution)/shard_map/ppermute | solution.py:22
  118.3 2.5 collective-permute-start.21
  120.9 7.1 %retention_forward.1 = (bf16[2,4,64,512]{3,2,1,0:T(8,128)(2,1)S(1)}, f32[2,4,64,512]{3,2,1,0:T(8,128)S(1)}, f32[2,4,64,1]{3,2,1,0:T(8,128)S(1)}, bf16[4,256,512]...) custom-call(s32[4]{0:T(128)S(1)} %pad_add_fusion.where_ref, f32[8,128]{1,0:T(8,128)S(1)} %get-tuple-element.336.decay_ref, ...), custom_call_target="tpu_custom_call" | custom-call | tf_op jit(solution)/shard_map/retention_forward/pallas_call | solution.py:80
  128.0 4.6 collective-permute-done.21
  141.7 7.5 %collective-permute-done.25 = bf16[128,768]{1,0:T(8,128)(2,1)S(1)} collective-permute-done((bf16[128,768]{1,0:T(8,128)(2,1)S(1)}, bf16[128,768]{1,0:T(8,128)(2,1)S(1)}, u32[]{:S(2)}, u32[]{:S(2)}) %collective-permute-start.25) | collective-permute-done | bytes 196640 | tf_op jit(solution)/shard_map/ppermute | solution.py:22
  149.2 9.9 %collective-permute-done.26.refs_2_ = bf16[128,2048]{1,0:T(8,128)(2,1)S(1)} collective-permute-done((bf16[128,2048]{1,0:T(8,128)(2,1)S(1)}, bf16[128,2048]{1,0:T(8,128)(2,1)S(1)}, u32[]{:S(2)}, u32[]{:S(2)}) %collective-permute-start.26) | collective-permute-done | bytes 524320 | tf_op jit(solution)/shard_map/ppermute | solution.py:22
  162.5 13.4 %collective-permute-done.29.refs_2_ = bf16[4,128,512]{2,1,0:T(8,128)(2,1)S(1)} collective-permute-done((bf16[4,128,512]{2,1,0:T(8,128)(2,1)S(1)}, bf16[4,128,512]{2,1,0:T(8,128)(2,1)S(1)}, u32[]{:S(2)}, u32[]{:S(2)}) %collective-permute-start.29) | collective-permute-done | bytes 524320 | tf_op jit(solution)/shard_map/ppermute | solution.py:22
  180.8 6.9 %collective-permute-done.33.refs_4_ = bf16[64,2048]{1,0:T(8,128)(2,1)S(1)} collective-permute-done((bf16[64,2048]{1,0:T(8,128)(2,1)S(1)}, bf16[64,2048]{1,0:T(8,128)(2,1)S(1)}, u32[]{:S(2)}, u32[]{:S(2)}) %collective-permute-start.33) | collective-permute-done | bytes 262176 | tf_op jit(solution)/shard_map/ppermute | solution.py:22
  195.4 8.5 %collective-permute-done.35 = bf16[64,2048]{1,0:T(8,128)(2,1)S(1)} collective-permute-done((bf16[64,2048]{1,0:T(8,128)(2,1)S(1)}, bf16[64,2048]{1,0:T(8,128)(2,1)S(1)}, u32[]{:S(2)}, u32[]{:S(2)}) %collective-permute-start.35) | collective-permute-done | bytes 262176 | tf_op jit(solution)/shard_map/ppermute | solution.py:22
  205.1 6.9 %collective-permute-start.39 = (bf16[128,2048]{1,0:T(8,128)(2,1)S(1)}, bf16[128,2048]{1,0:T(8,128)(2,1)S(1)}, u32[]{:S(2)}, u32[]{:S(2)}) collective-permute-start(bf16[128,2048]{1,0:T(8,128)(2,1)S(1)} %constant_dynamic-update-slice_fusion.refs_0_), channel_id=1, source_target_pairs={{0,8},{8,0},{16,24},{24,16},{1,9},{9,1},{17,25},{25,17},{2,10},{10... | collective-permute-start | bytes 1572872 | tf_op jit(solution)/shard_map/ppermute | solution.py:22
  213.5 9.1 %collective-permute-done.39.refs_1_ = bf16[128,2048]{1,0:T(8,128)(2,1)S(1)} collective-permute-done((bf16[128,2048]{1,0:T(8,128)(2,1)S(1)}, bf16[128,2048]{1,0:T(8,128)(2,1)S(1)}, u32[]{:S(2)}, u32[]{:S(2)}) %collective-permute-start.39) | collective-permute-done | bytes 524320 | tf_op jit(solution)/shard_map/ppermute | solution.py:22
  227.8 4.1 collective-permute-done.43.refs_1_
  232.6 2.7 collective-permute-done.42.refs_3_
  240.1 2.6 far_messages.3
  245.6 2.9 weight_grads.6
  248.7 5.8 %collective-permute-done.44.got_ref = bf16[144,2048]{1,0:T(8,128)(2,1)S(1)} collective-permute-done((bf16[144,2048]{1,0:T(8,128)(2,1)S(1)}, bf16[144,2048]{1,0:T(8,128)(2,1)S(1)}, u32[]{:S(2)}, u32[]{:S(2)}) %collective-permute-start.44) | collective-permute-done | bytes 589856 | tf_op jit(solution)/shard_map/ppermute | solution.py:22
  260.2 3.1 weight_grads.7
  263.3 7.8 %collective-permute-done.45.got_ref = bf16[144,2048]{1,0:T(8,128)(2,1)S(1)} collective-permute-done((bf16[144,2048]{1,0:T(8,128)(2,1)S(1)}, bf16[144,2048]{1,0:T(8,128)(2,1)S(1)}, u32[]{:S(2)}, u32[]{:S(2)}) %collective-permute-start.45) | collective-permute-done | bytes 589856 | tf_op jit(solution)/shard_map/ppermute | solution.py:22
  278.1 11.3 %collective-permute-done.50 = bf16[512,512]{1,0:T(8,128)(2,1)S(1)} collective-permute-done((bf16[512,512]{1,0:T(8,128)(2,1)S(1)}, bf16[512,512]{1,0:T(8,128)(2,1)S(1)}, u32[]{:S(2)}, u32[]{:S(2)}) %collective-permute-start.50) | collective-permute-done | bytes 524320 | tf_op jit(solution)/shard_map/ppermute | solution.py:22
  297.3 6.7 %collective-permute-done.52 = bf16[512,512]{1,0:T(8,128)(2,1)S(1)} collective-permute-done((bf16[512,512]{1,0:T(8,128)(2,1)S(1)}, bf16[512,512]{1,0:T(8,128)(2,1)S(1)}, u32[]{:S(2)}, u32[]{:S(2)}) %collective-permute-start.52) | collective-permute-done | bytes 524320 | tf_op jit(solution)/shard_map/ppermute | solution.py:22
  304.1 9.3 %collective-permute-done.51 = bf16[64,2048]{1,0:T(8,128)(2,1)S(1)} collective-permute-done((bf16[64,2048]{1,0:T(8,128)(2,1)S(1)}, bf16[64,2048]{1,0:T(8,128)(2,1)S(1)}, u32[]{:S(2)}, u32[]{:S(2)}) %collective-permute-start.51) | collective-permute-done | bytes 262176 | tf_op jit(solution)/shard_map/ppermute | solution.py:22
  318.8 6.3 %collective-permute-done.57 = bf16[512,512]{1,0:T(8,128)(2,1)S(1)} collective-permute-done((bf16[512,512]{1,0:T(8,128)(2,1)S(1)}, bf16[512,512]{1,0:T(8,128)(2,1)S(1)}, u32[]{:S(2)}, u32[]{:S(2)}) %collective-permute-start.57) | collective-permute-done | bytes 524320 | tf_op jit(solution)/shard_map/ppermute | solution.py:22
  332.6 5.1 %collective-permute-done.59.refs_2_ = bf16[128,1024]{1,0:T(8,128)(2,1)} collective-permute-done((bf16[128,1024]{1,0:T(8,128)(2,1)}, bf16[128,1024]{1,0:T(8,128)(2,1)}, u32[]{:S(2)}, u32[]{:S(2)}) %collective-permute-start.59) | collective-permute-done | bytes 262176 | tf_op jit(solution)/shard_map/ppermute | solution.py:22
  353.7 8.4 %collective-permute-done.63.refs_1_ = bf16[128,512]{1,0:T(8,128)(2,1)S(1)} collective-permute-done((bf16[128,512]{1,0:T(8,128)(2,1)S(1)}, bf16[128,512]{1,0:T(8,128)(2,1)S(1)}, u32[]{:S(2)}, u32[]{:S(2)}) %collective-permute-start.63) | collective-permute-done | bytes 131104 | tf_op jit(solution)/shard_map/ppermute | solution.py:22
  362.2 6.7 %retention_backward.1 = (bf16[2,4,64,768]{3,2,1,0:T(8,128)(2,1)S(1)}, bf16[2,4,64,768]{3,2,1,0:T(8,128)(2,1)S(1)}) custom-call(s32[4]{0:T(128)S(1)} %pad_add_fusion.where_ref, f32[8,128]{1,0:T(8,128)S(1)} %get-tuple-element.336.decay_ref, bf16[2,4,64,256]{3,2,1,0:T(8,128)(2,1)S(1)} %copy-done.49, bf16[2,4,64,256]{3,2,1,0:T(8,128)(2,1)S(1)} %copy-done.51, ...), custom_call_target="tpu_custom_call" | custom-call | tf_op jit(solution)/shard_map/retention_backward/pallas_call | solution.py:80
  383.3 6.6 %collective-permute-done.69 = bf16[512,512]{1,0:T(8,128)(2,1)S(1)} collective-permute-done((bf16[512,512]{1,0:T(8,128)(2,1)S(1)}, bf16[512,512]{1,0:T(8,128)(2,1)S(1)}, u32[]{:S(2)}, u32[]{:S(2)}) %collective-permute-start.69) | collective-permute-done | bytes 524320 | tf_op jit(solution)/shard_map/ppermute | solution.py:22
  393.3 2.6 collective-permute-start.70
  405.6 8.6 %collective-permute-done.73 = bf16[64,2048]{1,0:T(8,128)(2,1)S(1)} collective-permute-done((bf16[64,2048]{1,0:T(8,128)(2,1)S(1)}, bf16[64,2048]{1,0:T(8,128)(2,1)S(1)}, u32[]{:S(2)}, u32[]{:S(2)}) %collective-permute-start.73) | collective-permute-done | bytes 262176 | tf_op jit(solution)/shard_map/ppermute | solution.py:22
  420.1 5.8 %collective-permute-done.76 = bf16[512,512]{1,0:T(8,128)(2,1)S(1)} collective-permute-done((bf16[512,512]{1,0:T(8,128)(2,1)S(1)}, bf16[512,512]{1,0:T(8,128)(2,1)S(1)}, u32[]{:S(2)}, u32[]{:S(2)}) %collective-permute-start.76) | collective-permute-done | bytes 524320 | tf_op jit(solution)/shard_map/ppermute | solution.py:22
  430.1 2.8 collective-permute-start.78
  434.5 2.7 collective-permute-done.80
  439.6 11.1 %collective-permute-done.78.refs_2_ = bf16[128,1024]{1,0:T(8,128)(2,1)S(1)} collective-permute-done((bf16[128,1024]{1,0:T(8,128)(2,1)S(1)}, bf16[128,1024]{1,0:T(8,128)(2,1)S(1)}, u32[]{:S(2)}, u32[]{:S(2)}) %collective-permute-start.78) | collective-permute-done | bytes 262176 | tf_op jit(solution)/shard_map/ppermute | solution.py:22
  450.7 3.8 collective-permute-start.82
  455.3 7.9 %collective-permute-done.82.refs_1_ = bf16[128,1024]{1,0:T(8,128)(2,1)S(1)} collective-permute-done((bf16[128,1024]{1,0:T(8,128)(2,1)S(1)}, bf16[128,1024]{1,0:T(8,128)(2,1)S(1)}, u32[]{:S(2)}, u32[]{:S(2)}) %collective-permute-start.82) | collective-permute-done | bytes 262176 | tf_op jit(solution)/shard_map/ppermute | solution.py:22
  463.2 4.5 collective-permute-done.83.refs_2_
  468.7 3.0 collective-permute-done.84
  473.0 3.2 collective-permute-start.86
  478.8 3.5 collective-permute-start.87
  (403 shorter events, 187.8 us)
Async XLA Ops:
  4.8 16.5 %collective-permute-start = (bf16[144,768]{1,0:T(8,128)(2,1)S(1)}, bf16[144,768]{1,0:T(8,128)(2,1)S(1)}, u32[]{:S(2)}, u32[]{:S(2)}) collective-permute-start(bf16[144,768]{1,0:T(8,128)(2,1)S(1)} %get-tuple-element.306), channel_id=1, source_target_pairs={{0,8},{8,0},{16,24},{24,16},{1,9},{9,1},{17,25},{25,17},{2,10},{10... | collective-permute-start | bytes 663560 | tf_op jit(solution)/shard_map/ppermute | solution.py:22
  7.9 24.4 %collective-permute-start.1 = (bf16[144,768]{1,0:T(8,128)(2,1)S(1)}, bf16[144,768]{1,0:T(8,128)(2,1)S(1)}, u32[]{:S(2)}, u32[]{:S(2)}) collective-permute-start(bf16[144,768]{1,0:T(8,128)(2,1)S(1)} %get-tuple-element.307), channel_id=1, source_target_pairs={{0,16},{8,24},{16,0},{24,8},{1,17},{9,25},{17,1},{25,9},{2,18},{10... | collective-permute-start | bytes 663560 | tf_op jit(solution)/shard_map/ppermute | solution.py:22
  10.5 21.8 %collective-permute-start.2 = (bf16[144,768]{1,0:T(8,128)(2,1)S(1)}, bf16[144,768]{1,0:T(8,128)(2,1)S(1)}, u32[]{:S(2)}, u32[]{:S(2)}) collective-permute-start(bf16[144,768]{1,0:T(8,128)(2,1)S(1)} %get-tuple-element.308), channel_id=1, source_target_pairs={{0,24},{8,16},{16,8},{24,0},{1,25},{9,17},{17,9},{25,1},{2,26},{10... | collective-permute-start | bytes 663560 | tf_op jit(solution)/shard_map/ppermute | solution.py:22
  12.1 20.2 %collective-permute-start.3 = (bf16[64,2048]{1,0:T(8,128)(2,1)S(1)}, bf16[64,2048]{1,0:T(8,128)(2,1)S(1)}, u32[]{:S(2)}, u32[]{:S(2)}) collective-permute-start(bf16[64,2048]{1,0:T(8,128)(2,1)S(1)} %get-tuple-element.304.refs_0_.in_ref), channel_id=1, source_target_pairs={{0,24},{8,16},{16,8},{24,0},{1,25},{9,17},{17,9},{25,1},{2,26},{10... | collective-permute-start | bytes 786440 | tf_op jit(solution)/shard_map/ppermute | solution.py:22
  18.6 20.5 %collective-permute-start.4 = (bf16[2,128,768]{2,1,0:T(8,128)(2,1)S(1)}, bf16[2,128,768]{2,1,0:T(8,128)(2,1)S(1)}, u32[]{:S(2)}, u32[]{:S(2)}) collective-permute-start(bf16[2,128,768]{2,1,0:T(8,128)(2,1)S(1)} %get-tuple-element.309), channel_id=1, source_target_pairs={{0,8},{8,0},{16,24},{24,16},{1,9},{9,1},{17,25},{25,17},{2,10},{10... | collective-permute-start | bytes 1179656 | tf_op jit(solution)/shard_map/ppermute | solution.py:22
  39.3 27.6 %collective-permute-start.5 = (bf16[4,144,768]{2,1,0:T(8,128)(2,1)S(1)}, bf16[4,144,768]{2,1,0:T(8,128)(2,1)S(1)}, u32[]{:S(2)}, u32[]{:S(2)}) collective-permute-start(bf16[4,144,768]{2,1,0:T(8,128)(2,1)S(1)} %pad_maximum_fusion.3.refs_0_), channel_id=1, source_target_pairs={{0,4},{4,0},{1,5},{5,1},{2,6},{6,2},{3,7},{7,3},{8,12},{12,8},{9,1... | collective-permute-start | bytes 2654216 | tf_op jit(solution)/shard_map/ppermute | solution.py:22
  40.8 26.0 %collective-permute-start.6 = (bf16[4,144,768]{2,1,0:T(8,128)(2,1)S(1)}, bf16[4,144,768]{2,1,0:T(8,128)(2,1)S(1)}, u32[]{:S(2)}, u32[]{:S(2)}) collective-permute-start(bf16[4,144,768]{2,1,0:T(8,128)(2,1)S(1)} %pad_maximum_fusion.3.refs_0_), channel_id=1, source_target_pairs={{0,2},{2,0},{1,3},{3,1},{4,6},{6,4},{5,7},{7,5},{8,10},{10,8},{9,1... | collective-permute-start | bytes 2654216 | tf_op jit(solution)/shard_map/ppermute | solution.py:22
  40.9 25.9 %collective-permute-start.7 = (bf16[128,2048]{1,0:T(8,128)(2,1)S(1)}, bf16[128,2048]{1,0:T(8,128)(2,1)S(1)}, u32[]{:S(2)}, u32[]{:S(2)}) collective-permute-start(bf16[128,2048]{1,0:T(8,128)(2,1)S(1)} %pad_maximum_fusion.7), channel_id=1, source_target_pairs={{0,8},{8,0},{16,24},{24,16},{1,9},{9,1},{17,25},{25,17},{2,10},{10... | collective-permute-start | bytes 1572872 | tf_op jit(solution)/shard_map/ppermute | solution.py:22
  43.7 23.1 %collective-permute-start.8 = (bf16[2,128,768]{2,1,0:T(8,128)(2,1)S(1)}, bf16[2,128,768]{2,1,0:T(8,128)(2,1)S(1)}, u32[]{:S(2)}, u32[]{:S(2)}) collective-permute-start(bf16[2,128,768]{2,1,0:T(8,128)(2,1)S(1)} %pad_maximum_fusion.10), channel_id=1, source_target_pairs={{0,24},{8,16},{16,8},{24,0},{1,25},{9,17},{17,9},{25,1},{2,26},{10... | collective-permute-start | bytes 1179656 | tf_op jit(solution)/shard_map/ppermute | solution.py:22
  66.8 21.6 %collective-permute-start.9 = (bf16[4,144,768]{2,1,0:T(8,128)(2,1)S(1)}, bf16[4,144,768]{2,1,0:T(8,128)(2,1)S(1)}, u32[]{:S(2)}, u32[]{:S(2)}) collective-permute-start(bf16[4,144,768]{2,1,0:T(8,128)(2,1)S(1)} %collective-permute-done.5.refs_2_), channel_id=1, source_target_pairs={{0,2},{2,0},{1,3},{3,1},{4,6},{6,4},{5,7},{7,5},{8,10},{10,8},{9,1... | collective-permute-start | bytes 2654216 | tf_op jit(solution)/shard_map/ppermute | solution.py:22
  67.0 20.0 %collective-permute-start.10 = (bf16[192,2048]{1,0:T(8,128)(2,1)S(1)}, bf16[192,2048]{1,0:T(8,128)(2,1)S(1)}, u32[]{:S(2)}, u32[]{:S(2)}) collective-permute-start(bf16[192,2048]{1,0:T(8,128)(2,1)S(1)} %pad_maximum_fusion.4), channel_id=1, source_target_pairs={{0,1},{1,0},{2,3},{3,2},{4,5},{5,4},{6,7},{7,6},{8,9},{9,8},{10,11... | collective-permute-start | bytes 2359304 | tf_op jit(solution)/shard_map/ppermute | solution.py:22
  68.7 19.7 %collective-permute-start.11 = (bf16[4,128,768]{2,1,0:T(8,128)(2,1)S(1)}, bf16[4,128,768]{2,1,0:T(8,128)(2,1)S(1)}, u32[]{:S(2)}, u32[]{:S(2)}) collective-permute-start(bf16[4,128,768]{2,1,0:T(8,128)(2,1)S(1)} %pad_maximum_fusion.5.refs_0_), channel_id=1, source_target_pairs={{0,4},{4,0},{1,5},{5,1},{2,6},{6,2},{3,7},{7,3},{8,12},{12,8},{9,1... | collective-permute-start | bytes 2359304 | tf_op jit(solution)/shard_map/ppermute | solution.py:22
  70.6 14.3 %collective-permute-start.13 = (bf16[2,128,512]{2,1,0:T(8,128)(2,1)S(1)}, bf16[2,128,512]{2,1,0:T(8,128)(2,1)S(1)}, u32[]{:S(2)}, u32[]{:S(2)}) collective-permute-start(bf16[2,128,512]{2,1,0:T(8,128)(2,1)S(1)} %get-tuple-element.329), channel_id=1, source_target_pairs={{0,24},{8,16},{16,8},{24,0},{1,25},{9,17},{17,9},{25,1},{2,26},{10... | collective-permute-start | bytes 786440 | tf_op jit(solution)/shard_map/ppermute | solution.py:22
  93.9 22.7 %collective-permute-start.14 = (bf16[2,4,64,768]{3,2,1,0:T(8,128)(2,1)S(1)}, bf16[2,4,64,768]{3,2,1,0:T(8,128)(2,1)S(1)}, u32[]{:S(2)}, u32[]{:S(2)}) collective-permute-start(bf16[2,4,64,768]{3,2,1,0:T(8,128)(2,1)S(1)} %pad_maximum_fusion.6.refs_0_.refs_4_), channel_id=1, source_target_pairs={{0,4},{4,0},{1,5},{5,1},{2,6},{6,2},{3,7},{7,3},{8,12},{12,8},{9,1... | collective-permute-start | bytes 2359304 | tf_op jit(solution)/shard_map/ppermute | solution.py:22
  94.5 14.0 %collective-permute-start.17 = (bf16[2,128,512]{2,1,0:T(8,128)(2,1)S(1)}, bf16[2,128,512]{2,1,0:T(8,128)(2,1)S(1)}, u32[]{:S(2)}, u32[]{:S(2)}) collective-permute-start(bf16[2,128,512]{2,1,0:T(8,128)(2,1)S(1)} %pad_maximum_fusion.11), channel_id=1, source_target_pairs={{0,8},{8,0},{16,24},{24,16},{1,9},{9,1},{17,25},{25,17},{2,10},{10... | collective-permute-start | bytes 786440 | tf_op jit(solution)/shard_map/ppermute | solution.py:22
  96.7 19.9 %collective-permute-start.18 = (bf16[128,1536]{1,0:T(8,128)(2,1)S(1)}, bf16[128,1536]{1,0:T(8,128)(2,1)S(1)}, u32[]{:S(2)}, u32[]{:S(2)}) collective-permute-start(bf16[128,1536]{1,0:T(8,128)(2,1)S(1)} %get-tuple-element.355), channel_id=1, source_target_pairs={{0,16},{8,24},{16,0},{24,8},{1,17},{9,25},{17,1},{25,9},{2,18},{10... | collective-permute-start | bytes 1179656 | tf_op jit(solution)/shard_map/ppermute | solution.py:22
  116.7 15.9 %collective-permute-start.19 = (bf16[4,128,512]{2,1,0:T(8,128)(2,1)S(1)}, bf16[4,128,512]{2,1,0:T(8,128)(2,1)S(1)}, u32[]{:S(2)}, u32[]{:S(2)}) collective-permute-start(bf16[4,128,512]{2,1,0:T(8,128)(2,1)S(1)} %pad_maximum_fusion.8.refs_0_), channel_id=1, source_target_pairs={{0,4},{4,0},{1,5},{5,1},{2,6},{6,2},{3,7},{7,3},{8,12},{12,8},{9,1... | collective-permute-start | bytes 1572872 | tf_op jit(solution)/shard_map/ppermute | solution.py:22
  118.3 14.3 %collective-permute-start.20 = (bf16[128,1536]{1,0:T(8,128)(2,1)S(1)}, bf16[128,1536]{1,0:T(8,128)(2,1)S(1)}, u32[]{:S(2)}, u32[]{:S(2)}) collective-permute-start(bf16[128,1536]{1,0:T(8,128)(2,1)S(1)} %get-tuple-element.364), channel_id=1, source_target_pairs={{0,8},{8,0},{16,24},{24,16},{1,9},{9,1},{17,25},{25,17},{2,10},{10... | collective-permute-start | bytes 1179656 | tf_op jit(solution)/shard_map/ppermute | solution.py:22
  118.3 14.3 %collective-permute-start.21 = (bf16[128,768]{1,0:T(8,128)(2,1)S(1)}, bf16[128,768]{1,0:T(8,128)(2,1)S(1)}, u32[]{:S(2)}, u32[]{:S(2)}) collective-permute-start(bf16[128,768]{1,0:T(8,128)(2,1)S(1)} %slice.219), channel_id=1, source_target_pairs={{0,24},{8,16},{16,8},{24,0},{1,25},{9,17},{17,9},{25,1},{2,26},{10... | collective-permute-start | bytes 589832 | tf_op jit(solution)/shard_map/ppermute | solution.py:22
  138.1 20.9 %collective-permute-start.24 = (bf16[144,2048]{1,0:T(8,128)(2,1)S(1)}, bf16[144,2048]{1,0:T(8,128)(2,1)S(1)}, u32[]{:S(2)}, u32[]{:S(2)}) collective-permute-start(bf16[144,2048]{1,0:T(8,128)(2,1)S(1)} %get-tuple-element.369), channel_id=1, source_target_pairs={{0,1},{1,0},{2,3},{3,2},{4,5},{5,4},{6,7},{7,6},{8,9},{9,8},{10,11... | collective-permute-start | bytes 1769480 | tf_op jit(solution)/shard_map/ppermute | solution.py:22
  141.4 17.7 %collective-permute-start.26 = (bf16[128,2048]{1,0:T(8,128)(2,1)S(1)}, bf16[128,2048]{1,0:T(8,128)(2,1)S(1)}, u32[]{:S(2)}, u32[]{:S(2)}) collective-permute-start(bf16[128,2048]{1,0:T(8,128)(2,1)S(1)} %pad_maximum_fusion.9), channel_id=1, source_target_pairs={{0,8},{8,0},{16,24},{24,16},{1,9},{9,1},{17,25},{25,17},{2,10},{10... | collective-permute-start | bytes 1572872 | tf_op jit(solution)/shard_map/ppermute | solution.py:22
  159.3 16.6 %collective-permute-start.30 = (bf16[4,128,1536]{2,1,0:T(8,128)(2,1)S(1)}, bf16[4,128,1536]{2,1,0:T(8,128)(2,1)S(1)}, u32[]{:S(2)}, u32[]{:S(2)}) collective-permute-start(bf16[4,128,1536]{2,1,0:T(8,128)(2,1)S(1)} %pad_maximum_fusion.1.refs_0_), channel_id=1, source_target_pairs={{0,2},{2,0},{1,3},{3,1},{4,6},{6,4},{5,7},{7,5},{8,10},{10,8},{9,1... | collective-permute-start | bytes 4718600 | tf_op jit(solution)/shard_map/ppermute | solution.py:22
  160.0 15.8 %collective-permute-start.27 = (bf16[144,2048]{1,0:T(8,128)(2,1)S(1)}, bf16[144,2048]{1,0:T(8,128)(2,1)S(1)}, u32[]{:S(2)}, u32[]{:S(2)}) collective-permute-start(bf16[144,2048]{1,0:T(8,128)(2,1)S(1)} %pass_message.2), channel_id=1, source_target_pairs={{0,8},{8,0},{16,24},{24,16},{1,9},{9,1},{17,25},{25,17},{2,10},{10... | collective-permute-start | bytes 1769480 | tf_op jit(solution)/shard_map/ppermute | solution.py:22
  160.4 15.6 %collective-permute-start.28 = (bf16[144,2048]{1,0:T(8,128)(2,1)S(1)}, bf16[144,2048]{1,0:T(8,128)(2,1)S(1)}, u32[]{:S(2)}, u32[]{:S(2)}) collective-permute-start(bf16[144,2048]{1,0:T(8,128)(2,1)S(1)} %get-tuple-element.378), channel_id=1, source_target_pairs={{0,1},{1,0},{2,3},{3,2},{4,5},{5,4},{6,7},{7,6},{8,9},{9,8},{10,11... | collective-permute-start | bytes 1769480 | tf_op jit(solution)/shard_map/ppermute | solution.py:22
  161.9 13.9 %collective-permute-start.29 = (bf16[4,128,512]{2,1,0:T(8,128)(2,1)S(1)}, bf16[4,128,512]{2,1,0:T(8,128)(2,1)S(1)}, u32[]{:S(2)}, u32[]{:S(2)}) collective-permute-start(bf16[4,128,512]{2,1,0:T(8,128)(2,1)S(1)} %slice.276), channel_id=1, source_target_pairs={{0,4},{4,0},{1,5},{5,1},{2,6},{6,2},{3,7},{7,3},{8,12},{12,8},{9,1... | collective-permute-start | bytes 1572872 | tf_op jit(solution)/shard_map/ppermute | solution.py:22
  176.7 13.5 %collective-permute-start.32 = (bf16[4,128,512]{2,1,0:T(8,128)(2,1)S(1)}, bf16[4,128,512]{2,1,0:T(8,128)(2,1)S(1)}, u32[]{:S(2)}, u32[]{:S(2)}) collective-permute-start(bf16[4,128,512]{2,1,0:T(8,128)(2,1)S(1)} %slice.226), channel_id=1, source_target_pairs={{0,4},{4,0},{1,5},{5,1},{2,6},{6,2},{3,7},{7,3},{8,12},{12,8},{9,1... | collective-permute-start | bytes 1572872 | tf_op jit(solution)/shard_map/ppermute | solution.py:22
  191.8 13.2 %collective-permute-start.37 = (bf16[128,2048]{1,0:T(8,128)(2,1)S(1)}, bf16[128,2048]{1,0:T(8,128)(2,1)S(1)}, u32[]{:S(2)}, u32[]{:S(2)}) collective-permute-start(bf16[128,2048]{1,0:T(8,128)(2,1)S(1)} %collective-permute-done.26.refs_2_), channel_id=1, source_target_pairs={{0,1},{1,0},{2,3},{3,2},{4,5},{5,4},{6,7},{7,6},{8,9},{9,8},{10,11... | collective-permute-start | bytes 1572872 | tf_op jit(solution)/shard_map/ppermute | solution.py:22
  205.1 17.5 %collective-permute-start.39 = (bf16[128,2048]{1,0:T(8,128)(2,1)S(1)}, bf16[128,2048]{1,0:T(8,128)(2,1)S(1)}, u32[]{:S(2)}, u32[]{:S(2)}) collective-permute-start(bf16[128,2048]{1,0:T(8,128)(2,1)S(1)} %constant_dynamic-update-slice_fusion.refs_0_), channel_id=1, source_target_pairs={{0,8},{8,0},{16,24},{24,16},{1,9},{9,1},{17,25},{25,17},{2,10},{10... | collective-permute-start | bytes 1572872 | tf_op jit(solution)/shard_map/ppermute | solution.py:22
  255.2 15.8 %collective-permute-start.45 = (bf16[144,2048]{1,0:T(8,128)(2,1)S(1)}, bf16[144,2048]{1,0:T(8,128)(2,1)S(1)}, u32[]{:S(2)}, u32[]{:S(2)}) collective-permute-start(bf16[144,2048]{1,0:T(8,128)(2,1)S(1)} %pass_message.3), channel_id=1, source_target_pairs={{0,8},{8,0},{16,24},{24,16},{1,9},{9,1},{17,25},{25,17},{2,10},{10... | collective-permute-start | bytes 1769480 | tf_op jit(solution)/shard_map/ppermute | solution.py:22
  256.1 15.5 %collective-permute-start.46 = (bf16[144,2048]{1,0:T(8,128)(2,1)S(1)}, bf16[144,2048]{1,0:T(8,128)(2,1)S(1)}, u32[]{:S(2)}, u32[]{:S(2)}) collective-permute-start(bf16[144,2048]{1,0:T(8,128)(2,1)S(1)} %get-tuple-element.441), channel_id=1, source_target_pairs={{0,1},{1,0},{2,3},{3,2},{4,5},{5,4},{6,7},{7,6},{8,9},{9,8},{10,11... | collective-permute-start | bytes 1769480 | tf_op jit(solution)/shard_map/ppermute | solution.py:22
  272.3 17.3 %collective-permute-start.48 = (bf16[80,2048]{1,0:T(8,128)(2,1)S(1)}, bf16[80,2048]{1,0:T(8,128)(2,1)S(1)}, u32[]{:S(2)}, u32[]{:S(2)}) collective-permute-start(bf16[80,2048]{1,0:T(8,128)(2,1)S(1)} %get-tuple-element.449), channel_id=1, source_target_pairs={{0,24},{8,16},{16,8},{24,0},{1,25},{9,17},{17,9},{25,1},{2,26},{10... | collective-permute-start | bytes 983048 | tf_op jit(solution)/shard_map/ppermute | solution.py:22
  274.4 15.2 %collective-permute-start.49 = (bf16[128,2048]{1,0:T(8,128)(2,1)S(1)}, bf16[128,2048]{1,0:T(8,128)(2,1)S(1)}, u32[]{:S(2)}, u32[]{:S(2)}) collective-permute-start(bf16[128,2048]{1,0:T(8,128)(2,1)S(1)} %get-tuple-element.450), channel_id=1, source_target_pairs={{0,1},{1,0},{2,3},{3,2},{4,5},{5,4},{6,7},{7,6},{8,9},{9,8},{10,11... | collective-permute-start | bytes 1572872 | tf_op jit(solution)/shard_map/ppermute | solution.py:22
  293.4 20.1 %collective-permute-start.53 = (bf16[128,2048]{1,0:T(8,128)(2,1)S(1)}, bf16[128,2048]{1,0:T(8,128)(2,1)S(1)}, u32[]{:S(2)}, u32[]{:S(2)}) collective-permute-start(bf16[128,2048]{1,0:T(8,128)(2,1)S(1)} %get-tuple-element.471), channel_id=1, source_target_pairs={{0,1},{1,0},{2,3},{3,2},{4,5},{5,4},{6,7},{7,6},{8,9},{9,8},{10,11... | collective-permute-start | bytes 1572872 | tf_op jit(solution)/shard_map/ppermute | solution.py:22
  295.2 18.2 %collective-permute-start.54 = (bf16[128,2048]{1,0:T(8,128)(2,1)S(1)}, bf16[128,2048]{1,0:T(8,128)(2,1)S(1)}, u32[]{:S(2)}, u32[]{:S(2)}) collective-permute-start(bf16[128,2048]{1,0:T(8,128)(2,1)S(1)} %add_convert_fusion.1), channel_id=1, source_target_pairs={{0,8},{8,0},{16,24},{24,16},{1,9},{9,1},{17,25},{25,17},{2,10},{10... | collective-permute-start | bytes 1572872 | tf_op jit(solution)/shard_map/ppermute | solution.py:22
  295.5 17.9 %collective-permute-start.51 = (bf16[64,2048]{1,0:T(8,128)(2,1)S(1)}, bf16[64,2048]{1,0:T(8,128)(2,1)S(1)}, u32[]{:S(2)}, u32[]{:S(2)}) collective-permute-start(bf16[64,2048]{1,0:T(8,128)(2,1)S(1)} %get-tuple-element.465), channel_id=1, source_target_pairs={{0,24},{8,16},{16,8},{24,0},{1,25},{9,17},{17,9},{25,1},{2,26},{10... | collective-permute-start | bytes 786440 | tf_op jit(solution)/shard_map/ppermute | solution.py:22
  347.1 15.0 %collective-permute-start.61 = (bf16[2,4,64,512]{3,2,1,0:T(8,128)(2,1)S(1)}, bf16[2,4,64,512]{3,2,1,0:T(8,128)(2,1)S(1)}, u32[]{:S(2)}, u32[]{:S(2)}) collective-permute-start(bf16[2,4,64,512]{3,2,1,0:T(8,128)(2,1)S(1)} %bitcast.121), channel_id=1, source_target_pairs={{0,4},{4,0},{1,5},{5,1},{2,6},{6,2},{3,7},{7,3},{8,12},{12,8},{9,1... | collective-permute-start | bytes 1572872 | tf_op jit(solution)/shard_map/ppermute | solution.py:22
  374.4 18.0 %collective-permute-start.68 = (bf16[1024,1024]{1,0:T(8,128)(2,1)S(1)}, bf16[1024,1024]{1,0:T(8,128)(2,1)S(1)}, u32[]{:S(2)}, u32[]{:S(2)}) collective-permute-start(bf16[1024,1024]{1,0:T(8,128)(2,1)S(1)} %weight_grads.10), channel_id=1, source_target_pairs={{0,2},{2,0},{1,3},{3,1},{4,6},{6,4},{5,7},{7,5},{8,10},{10,8},{9,1... | collective-permute-start | bytes 6291464 | tf_op jit(solution)/shard_map/ppermute | solution.py:22
  374.6 17.8 %collective-permute-start.65 = (bf16[128,2048]{1,0:T(8,128)(2,1)S(1)}, bf16[128,2048]{1,0:T(8,128)(2,1)S(1)}, u32[]{:S(2)}, u32[]{:S(2)}) collective-permute-start(bf16[128,2048]{1,0:T(8,128)(2,1)S(1)} %get-tuple-element.621), channel_id=1, source_target_pairs={{0,1},{1,0},{2,3},{3,2},{4,5},{5,4},{6,7},{7,6},{8,9},{9,8},{10,11... | collective-permute-start | bytes 1572872 | tf_op jit(solution)/shard_map/ppermute | solution.py:22
  375.8 14.1 %collective-permute-start.69 = (bf16[512,512]{1,0:T(8,128)(2,1)S(1)}, bf16[512,512]{1,0:T(8,128)(2,1)S(1)}, u32[]{:S(2)}, u32[]{:S(2)}) collective-permute-start(bf16[512,512]{1,0:T(8,128)(2,1)S(1)} %slice.257), channel_id=1, source_target_pairs={{0,4},{4,0},{1,5},{5,1},{2,6},{6,2},{3,7},{7,3},{8,12},{12,8},{9,1... | collective-permute-start | bytes 1572872 | tf_op jit(solution)/shard_map/ppermute | solution.py:22
  392.4 13.0 %collective-permute-start.72 = (bf16[512,512]{1,0:T(8,128)(2,1)S(1)}, bf16[512,512]{1,0:T(8,128)(2,1)S(1)}, u32[]{:S(2)}, u32[]{:S(2)}) collective-permute-start(bf16[512,512]{1,0:T(8,128)(2,1)S(1)} %slice.258), channel_id=1, source_target_pairs={{0,4},{4,0},{1,5},{5,1},{2,6},{6,2},{3,7},{7,3},{8,12},{12,8},{9,1... | collective-permute-start | bytes 1572872 | tf_op jit(solution)/shard_map/ppermute | solution.py:22
  393.3 20.8 %collective-permute-start.70 = (bf16[128,2048]{1,0:T(8,128)(2,1)S(1)}, bf16[128,2048]{1,0:T(8,128)(2,1)S(1)}, u32[]{:S(2)}, u32[]{:S(2)}) collective-permute-start(bf16[128,2048]{1,0:T(8,128)(2,1)S(1)} %add_convert_fusion), channel_id=1, source_target_pairs={{0,8},{8,0},{16,24},{24,16},{1,9},{9,1},{17,25},{25,17},{2,10},{10... | collective-permute-start | bytes 1572872 | tf_op jit(solution)/shard_map/ppermute | solution.py:22
  395.9 18.2 %collective-permute-start.71 = (bf16[128,2048]{1,0:T(8,128)(2,1)S(1)}, bf16[128,2048]{1,0:T(8,128)(2,1)S(1)}, u32[]{:S(2)}, u32[]{:S(2)}) collective-permute-start(bf16[128,2048]{1,0:T(8,128)(2,1)S(1)} %get-tuple-element.531), channel_id=1, source_target_pairs={{0,1},{1,0},{2,3},{3,2},{4,5},{5,4},{6,7},{7,6},{8,9},{9,8},{10,11... | collective-permute-start | bytes 1572872 | tf_op jit(solution)/shard_map/ppermute | solution.py:22
  399.4 14.7 %collective-permute-start.73 = (bf16[64,2048]{1,0:T(8,128)(2,1)S(1)}, bf16[64,2048]{1,0:T(8,128)(2,1)S(1)}, u32[]{:S(2)}, u32[]{:S(2)}) collective-permute-start(bf16[64,2048]{1,0:T(8,128)(2,1)S(1)} %copy-done.58), channel_id=1, source_target_pairs={{0,24},{8,16},{16,8},{24,0},{1,25},{9,17},{17,9},{25,1},{2,26},{10... | collective-permute-start | bytes 786440 | tf_op jit(solution)/shard_map/ppermute | solution.py:22
  428.2 22.5 %collective-permute-start.81 = (f32[64,2048]{1,0:T(8,128)S(1)}, f32[64,2048]{1,0:T(8,128)S(1)}, u32[]{:S(2)}, u32[]{:S(2)}) collective-permute-start(f32[64,2048]{1,0:T(8,128)S(1)} %fusion.21.own_ref), channel_id=1, source_target_pairs={{0,1},{1,0},{2,3},{3,2},{4,5},{5,4},{6,7},{7,6},{8,9},{9,8},{10,11... | collective-permute-start | bytes 1572872 | tf_op jit(solution)/shard_map/ppermute | solution.py:22
  430.1 20.6 %collective-permute-start.78 = (bf16[128,1024]{1,0:T(8,128)(2,1)S(1)}, bf16[128,1024]{1,0:T(8,128)(2,1)S(1)}, u32[]{:S(2)}, u32[]{:S(2)}) collective-permute-start(bf16[128,1024]{1,0:T(8,128)(2,1)S(1)} %get-tuple-element.565), channel_id=1, source_target_pairs={{0,16},{8,24},{16,0},{24,8},{1,17},{9,25},{17,1},{25,9},{2,18},{10... | collective-permute-start | bytes 786440 | tf_op jit(solution)/shard_map/ppermute | solution.py:22
  432.9 17.8 %collective-permute-start.79 = (bf16[128,1024]{1,0:T(8,128)(2,1)S(1)}, bf16[128,1024]{1,0:T(8,128)(2,1)S(1)}, u32[]{:S(2)}, u32[]{:S(2)}) collective-permute-start(bf16[128,1024]{1,0:T(8,128)(2,1)S(1)} %get-tuple-element.566), channel_id=1, source_target_pairs={{0,24},{8,16},{16,8},{24,0},{1,25},{9,17},{17,9},{25,1},{2,26},{10... | collective-permute-start | bytes 786440 | tf_op jit(solution)/shard_map/ppermute | solution.py:22
  454.5 13.2 %collective-permute-start.83 = (bf16[128,1024]{1,0:T(8,128)(2,1)S(1)}, bf16[128,1024]{1,0:T(8,128)(2,1)S(1)}, u32[]{:S(2)}, u32[]{:S(2)}) collective-permute-start(bf16[128,1024]{1,0:T(8,128)(2,1)S(1)} %get-tuple-element.578), channel_id=1, source_target_pairs={{0,16},{8,24},{16,0},{24,8},{1,17},{9,25},{17,1},{25,9},{2,18},{10... | collective-permute-start | bytes 786440 | tf_op jit(solution)/shard_map/ppermute | solution.py:22
  468.0 19.4 %collective-permute-start.90 = (bf16[128,1024]{1,0:T(8,128)(2,1)}, bf16[128,1024]{1,0:T(8,128)(2,1)}, u32[]{:S(2)}, u32[]{:S(2)}) collective-permute-start(bf16[128,1024]{1,0:T(8,128)(2,1)} %copy-done.53), channel_id=1, source_target_pairs={{0,24},{8,16},{16,8},{24,0},{1,25},{9,17},{17,9},{25,1},{2,26},{10... | collective-permute-start | bytes 786440 | tf_op jit(solution)/shard_map/ppermute | solution.py:22
  (103 other events, 1119.6 us)

commit v3 on v1

--- a/solution.py
+++ b/solution.py
@@ -923,7 +923,14 @@
     both_pieces, kvq_pieces, grad_in_other, grad_one = tie(
         both_pieces, kvq_pieces, grad_in_other, grad_one
     )
-    kvq_pieces = [trade(kvq_pieces, k) for k in range(nz)]
+    top = swap(kvq_pieces[1][:LOW], "row", 1)
+    rest = swap(kvq_pieces[1][LOW:], "row", 1)
+    kvq_pieces = [
+        kvq_pieces[0],
+        jnp.concatenate([top, rest]),
+        trade(kvq_pieces, 2),
+        trade(kvq_pieces, 3),
+    ]
     norm_sums = jnp.stack(
         [
             jnp.sum(grad_one * scaled_own, axis=0),
@@ -932,7 +939,7 @@
             jnp.sum(grad_two, axis=0),
         ]
     )
-    norm_sums = after(norm_sums, kvq_pieces[1])
+    norm_sums = after(norm_sums, top)
     norm_sums = norm_sums + mirror(norm_sums)
     norm_sums = norm_sums.reshape(4, nz, ny, nb, rows)
 

time: 489 us -> 504 us (1.031)
  waiting for transfers between devices: 250 us -> 265 us
    ppermute x91 -> x92, waiting for transfers between devices: 250 us -> 265 us  [swap(): return lax.ppermute(values, axis, [(i, i ^ k) for i in range(count)])]
    ppermute x91 -> x92, starting transfers between devices: 116 us -> 115 us  [swap(): return lax.ppermute(values, axis, [(i, i ^ k) for i in range(count)])]
    unnamed x134 -> x130, local copies, waits for them, and re-layouts: 14.9 us -> 14.7 us
  transfers between devices with their start and end apart: 91 -> 92, of which waited for: 46 -> 47; matrix products, arithmetic and copies ran while one was open for 4% -> 4% of each run, Pallas kernels for 8% -> 7%
where the time goes in v3:
time: 504 us; the launch traced here: 495 us
  waiting for transfers between devices  265 us (53%)
  starting transfers between devices  115 us (23%)
  Pallas kernels  64.4 us (13%)
  local copies, waits for them, and re-layouts  18.6 us (4%)
  matrix products  17.8 us (4%)
  other arithmetic  11.3 us (2%)
    ppermute x92, waiting for transfers between devices, swap(): return lax.ppermute(values, axis, [(i, i ^ k) for i in range(count)])  265 us
    ppermute x92, starting transfers between devices, swap(): return lax.ppermute(values, axis, [(i, i ^ k) for i in range(count)])  115 us
    pallas_call x32, Pallas kernels, call(): pl.pallas_call(kernel, grid=() if grid is None else grid, out_shape=shape...  42.8 us
    pallas_call x6, Pallas kernels, weight_grads(): pl.pallas_call(kernel, grid=(ny,), out_shape=shapes, in_specs=[SMEM] + [W...  16.9 us
    unnamed x130, local copies, waits for them, and re-layouts  14.7 us
    dot_general x5, matrix products, matmul(): return jnp.dot(values, weight, preferred_element_type=f32)  10.3 us
  transfers between devices with their start and end apart: 92, of which 47 were waited for; matrix products, arithmetic and copies ran while one was open for 4% of the time, Pallas kernels for 7%

profile of v3, /device:TPU:0, one launch (start us, length us, event | category | flops | bytes accessed | tf_op | source)
XLA Modules:
  0.0 495.4 jit_solution(17577636704912813405)
XLA Ops:
  4.8 3.1 collective-permute-start
  12.1 3.9 collective-permute-start.3
  21.3 10.9 %collective-permute-done.1 = bf16[144,768]{1,0:T(8,128)(2,1)S(1)} collective-permute-done((bf16[144,768]{1,0:T(8,128)(2,1)S(1)}, bf16[144,768]{1,0:T(8,128)(2,1)S(1)}, u32[]{:S(2)}, u32[]{:S(2)}) %collective-permute-start.1) | collective-permute-done | bytes 221216 | tf_op jit(solution)/shard_map/ppermute | solution.py:22
  32.3 6.9 %collective-permute-done.4 = bf16[2,128,768]{2,1,0:T(8,128)(2,1)S(1)} collective-permute-done((bf16[2,128,768]{2,1,0:T(8,128)(2,1)S(1)}, bf16[2,128,768]{2,1,0:T(8,128)(2,1)S(1)}, u32[]{:S(2)}, u32[]{:S(2)}) %collective-permute-start.4) | collective-permute-done | bytes 393248 | tf_op jit(solution)/shard_map/ppermute | solution.py:22
  40.9 2.7 collective-permute-start.7
  48.7 18.1 %collective-permute-done.8 = bf16[2,128,768]{2,1,0:T(8,128)(2,1)S(1)} collective-permute-done((bf16[2,128,768]{2,1,0:T(8,128)(2,1)S(1)}, bf16[2,128,768]{2,1,0:T(8,128)(2,1)S(1)}, u32[]{:S(2)}, u32[]{:S(2)}) %collective-permute-start.8) | collective-permute-done | bytes 393248 | tf_op jit(solution)/shard_map/ppermute | solution.py:22
  73.9 6.4 %collective-permute-done.12.refs_1_ = bf16[64,2048]{1,0:T(8,128)(2,1)S(1)} collective-permute-done((bf16[64,2048]{1,0:T(8,128)(2,1)S(1)}, bf16[64,2048]{1,0:T(8,128)(2,1)S(1)}, u32[]{:S(2)}, u32[]{:S(2)}) %collective-permute-start.12) | collective-permute-done | bytes 262176 | tf_op jit(solution)/shard_map/ppermute | solution.py:22
  80.3 4.6 collective-permute-done.13
  100.7 7.7 %collective-permute-done.17 = bf16[2,128,512]{2,1,0:T(8,128)(2,1)S(1)} collective-permute-done((bf16[2,128,512]{2,1,0:T(8,128)(2,1)S(1)}, bf16[2,128,512]{2,1,0:T(8,128)(2,1)S(1)}, u32[]{:S(2)}, u32[]{:S(2)}) %collective-permute-start.17) | collective-permute-done | bytes 262176 | tf_op jit(solution)/shard_map/ppermute | solution.py:22
  108.5 8.1 %collective-permute-done.18 = bf16[128,1536]{1,0:T(8,128)(2,1)S(1)} collective-permute-done((bf16[128,1536]{1,0:T(8,128)(2,1)S(1)}, bf16[128,1536]{1,0:T(8,128)(2,1)S(1)}, u32[]{:S(2)}, u32[]{:S(2)}) %collective-permute-start.18) | collective-permute-done | bytes 393248 | tf_op jit(solution)/shard_map/ppermute | solution.py:22
  121.0 7.1 %retention_forward.1 = (bf16[2,4,64,512]{3,2,1,0:T(8,128)(2,1)S(1)}, f32[2,4,64,512]{3,2,1,0:T(8,128)S(1)}, f32[2,4,64,1]{3,2,1,0:T(8,128)S(1)}, bf16[4,256,512]...) custom-call(s32[4]{0:T(128)S(1)} %pad_add_fusion.where_ref, f32[8,128]{1,0:T(8,128)S(1)} %get-tuple-element.334.decay_ref, ...), custom_call_target="tpu_custom_call" | custom-call | tf_op jit(solution)/shard_map/retention_forward/pallas_call | solution.py:80
  129.8 5.8 %collective-permute-done.21 = bf16[128,768]{1,0:T(8,128)(2,1)S(1)} collective-permute-done((bf16[128,768]{1,0:T(8,128)(2,1)S(1)}, bf16[128,768]{1,0:T(8,128)(2,1)S(1)}, u32[]{:S(2)}, u32[]{:S(2)}) %collective-permute-start.21) | collective-permute-done | bytes 196640 | tf_op jit(solution)/shard_map/ppermute | solution.py:22
  144.4 7.6 %collective-permute-done.25 = bf16[128,768]{1,0:T(8,128)(2,1)S(1)} collective-permute-done((bf16[128,768]{1,0:T(8,128)(2,1)S(1)}, bf16[128,768]{1,0:T(8,128)(2,1)S(1)}, u32[]{:S(2)}, u32[]{:S(2)}) %collective-permute-start.25) | collective-permute-done | bytes 196640 | tf_op jit(solution)/shard_map/ppermute | solution.py:22
  152.0 7.0 %collective-permute-done.26 = bf16[128,1536]{1,0:T(8,128)(2,1)S(1)} collective-permute-done((bf16[128,1536]{1,0:T(8,128)(2,1)S(1)}, bf16[128,1536]{1,0:T(8,128)(2,1)S(1)}, u32[]{:S(2)}, u32[]{:S(2)}) %collective-permute-start.26) | collective-permute-done | bytes 393248 | tf_op jit(solution)/shard_map/ppermute | solution.py:22
  162.5 13.3 %collective-permute-done.29.refs_2_ = bf16[4,128,512]{2,1,0:T(8,128)(2,1)S(1)} collective-permute-done((bf16[4,128,512]{2,1,0:T(8,128)(2,1)S(1)}, bf16[4,128,512]{2,1,0:T(8,128)(2,1)S(1)}, u32[]{:S(2)}, u32[]{:S(2)}) %collective-permute-start.29) | collective-permute-done | bytes 524320 | tf_op jit(solution)/shard_map/ppermute | solution.py:22
  180.8 6.9 %collective-permute-done.33.refs_4_ = bf16[64,2048]{1,0:T(8,128)(2,1)S(1)} collective-permute-done((bf16[64,2048]{1,0:T(8,128)(2,1)S(1)}, bf16[64,2048]{1,0:T(8,128)(2,1)S(1)}, u32[]{:S(2)}, u32[]{:S(2)}) %collective-permute-start.33) | collective-permute-done | bytes 262176 | tf_op jit(solution)/shard_map/ppermute | solution.py:22
  195.4 8.5 %collective-permute-done.35 = bf16[64,2048]{1,0:T(8,128)(2,1)S(1)} collective-permute-done((bf16[64,2048]{1,0:T(8,128)(2,1)S(1)}, bf16[64,2048]{1,0:T(8,128)(2,1)S(1)}, u32[]{:S(2)}, u32[]{:S(2)}) %collective-permute-start.35) | collective-permute-done | bytes 262176 | tf_op jit(solution)/shard_map/ppermute | solution.py:22
  205.0 6.9 %collective-permute-start.39 = (bf16[128,2048]{1,0:T(8,128)(2,1)S(1)}, bf16[128,2048]{1,0:T(8,128)(2,1)S(1)}, u32[]{:S(2)}, u32[]{:S(2)}) collective-permute-start(bf16[128,2048]{1,0:T(8,128)(2,1)S(1)} %constant_dynamic-update-slice_fusion.refs_0_), channel_id=1, source_target_pairs={{0,8},{8,0},{16,24},{24,16},{1,9},{9,1},{17,25},{25,17},{2,10},{10... | collective-permute-start | bytes 1572872 | tf_op jit(solution)/shard_map/ppermute | solution.py:22
  213.4 9.1 %collective-permute-done.39.refs_1_ = bf16[128,2048]{1,0:T(8,128)(2,1)S(1)} collective-permute-done((bf16[128,2048]{1,0:T(8,128)(2,1)S(1)}, bf16[128,2048]{1,0:T(8,128)(2,1)S(1)}, u32[]{:S(2)}, u32[]{:S(2)}) %collective-permute-start.39) | collective-permute-done | bytes 524320 | tf_op jit(solution)/shard_map/ppermute | solution.py:22
  227.7 4.1 collective-permute-done.43.refs_1_
  232.6 2.6 collective-permute-done.42.refs_3_
  240.1 2.6 far_messages.3
  245.6 2.7 weight_grads.6
  248.5 6.0 %collective-permute-done.44.got_ref = bf16[144,2048]{1,0:T(8,128)(2,1)S(1)} collective-permute-done((bf16[144,2048]{1,0:T(8,128)(2,1)S(1)}, bf16[144,2048]{1,0:T(8,128)(2,1)S(1)}, u32[]{:S(2)}, u32[]{:S(2)}) %collective-permute-start.44) | collective-permute-done | bytes 589856 | tf_op jit(solution)/shard_map/ppermute | solution.py:22
  260.1 3.3 weight_grads.7
  263.4 7.6 %collective-permute-done.45.got_ref = bf16[144,2048]{1,0:T(8,128)(2,1)S(1)} collective-permute-done((bf16[144,2048]{1,0:T(8,128)(2,1)S(1)}, bf16[144,2048]{1,0:T(8,128)(2,1)S(1)}, u32[]{:S(2)}, u32[]{:S(2)}) %collective-permute-start.45) | collective-permute-done | bytes 589856 | tf_op jit(solution)/shard_map/ppermute | solution.py:22
  278.1 11.3 %collective-permute-done.50 = bf16[512,512]{1,0:T(8,128)(2,1)S(1)} collective-permute-done((bf16[512,512]{1,0:T(8,128)(2,1)S(1)}, bf16[512,512]{1,0:T(8,128)(2,1)S(1)}, u32[]{:S(2)}, u32[]{:S(2)}) %collective-permute-start.50) | collective-permute-done | bytes 524320 | tf_op jit(solution)/shard_map/ppermute | solution.py:22
  297.2 6.7 %collective-permute-done.52 = bf16[512,512]{1,0:T(8,128)(2,1)S(1)} collective-permute-done((bf16[512,512]{1,0:T(8,128)(2,1)S(1)}, bf16[512,512]{1,0:T(8,128)(2,1)S(1)}, u32[]{:S(2)}, u32[]{:S(2)}) %collective-permute-start.52) | collective-permute-done | bytes 524320 | tf_op jit(solution)/shard_map/ppermute | solution.py:22
  304.1 9.3 %collective-permute-done.51 = bf16[64,2048]{1,0:T(8,128)(2,1)S(1)} collective-permute-done((bf16[64,2048]{1,0:T(8,128)(2,1)S(1)}, bf16[64,2048]{1,0:T(8,128)(2,1)S(1)}, u32[]{:S(2)}, u32[]{:S(2)}) %collective-permute-start.51) | collective-permute-done | bytes 262176 | tf_op jit(solution)/shard_map/ppermute | solution.py:22
  317.4 7.5 %collective-permute-done.57 = bf16[512,512]{1,0:T(8,128)(2,1)S(1)} collective-permute-done((bf16[512,512]{1,0:T(8,128)(2,1)S(1)}, bf16[512,512]{1,0:T(8,128)(2,1)S(1)}, u32[]{:S(2)}, u32[]{:S(2)}) %collective-permute-start.57) | collective-permute-done | bytes 524320 | tf_op jit(solution)/shard_map/ppermute | solution.py:22
  329.3 6.9 %collective-permute-done.59.refs_2_ = bf16[128,1024]{1,0:T(8,128)(2,1)S(1)} collective-permute-done((bf16[128,1024]{1,0:T(8,128)(2,1)S(1)}, bf16[128,1024]{1,0:T(8,128)(2,1)S(1)}, u32[]{:S(2)}, u32[]{:S(2)}) %collective-permute-start.59) | collective-permute-done | bytes 262176 | tf_op jit(solution)/shard_map/ppermute | solution.py:22
  337.0 2.6 fusion.34
  339.6 3.1 weight_grads.8
  350.6 3.2 weight_grads.9
  353.8 6.7 %collective-permute-done.63.refs_1_ = bf16[128,512]{1,0:T(8,128)(2,1)S(1)} collective-permute-done((bf16[128,512]{1,0:T(8,128)(2,1)}, bf16[128,512]{1,0:T(8,128)(2,1)S(1)}, u32[]{:S(2)}, u32[]{:S(2)}) %collective-permute-start.63) | collective-permute-done | bytes 131104 | tf_op jit(solution)/shard_map/ppermute | solution.py:22
  360.6 6.8 %retention_backward.1 = (bf16[2,4,64,768]{3,2,1,0:T(8,128)(2,1)S(1)}, bf16[2,4,64,768]{3,2,1,0:T(8,128)(2,1)S(1)}) custom-call(s32[4]{0:T(128)S(1)} %pad_add_fusion.where_ref, f32[8,128]{1,0:T(8,128)S(1)} %get-tuple-element.334.decay_ref, bf16[2,4,64,256]{3,2,1,0:T(8,128)(2,1)S(1)} %copy-done.44, bf16[2,4,64,256]{3,2,1,0:T(8,128)(2,1)S(1)} %copy-done.46, ...), custom_call_target="tpu_custom_call" | custom-call | tf_op jit(solution)/shard_map/retention_backward/pallas_call | solution.py:80
  382.5 5.9 %collective-permute-done.69 = bf16[512,512]{1,0:T(8,128)(2,1)S(1)} collective-permute-done((bf16[512,512]{1,0:T(8,128)(2,1)S(1)}, bf16[512,512]{1,0:T(8,128)(2,1)S(1)}, u32[]{:S(2)}, u32[]{:S(2)}) %collective-permute-start.69) | collective-permute-done | bytes 524320 | tf_op jit(solution)/shard_map/ppermute | solution.py:22
  388.5 3.0 collective-permute-done.66.refs_2_
  392.4 2.6 collective-permute-start.70
  404.4 8.8 %collective-permute-done.73 = bf16[64,2048]{1,0:T(8,128)(2,1)S(1)} collective-permute-done((bf16[64,2048]{1,0:T(8,128)(2,1)S(1)}, bf16[64,2048]{1,0:T(8,128)(2,1)S(1)}, u32[]{:S(2)}, u32[]{:S(2)}) %collective-permute-start.73) | collective-permute-done | bytes 262176 | tf_op jit(solution)/shard_map/ppermute | solution.py:22
  419.1 5.9 %collective-permute-done.76 = bf16[512,512]{1,0:T(8,128)(2,1)S(1)} collective-permute-done((bf16[512,512]{1,0:T(8,128)(2,1)S(1)}, bf16[512,512]{1,0:T(8,128)(2,1)S(1)}, u32[]{:S(2)}, u32[]{:S(2)}) %collective-permute-start.76) | collective-permute-done | bytes 524320 | tf_op jit(solution)/shard_map/ppermute | solution.py:22
  428.1 3.5 collective-permute-start.78
  432.5 3.8 collective-permute-done.80
  437.8 10.8 %collective-permute-done.78.refs_2_ = bf16[128,1024]{1,0:T(8,128)(2,1)S(1)} collective-permute-done((bf16[128,1024]{1,0:T(8,128)(2,1)S(1)}, bf16[128,1024]{1,0:T(8,128)(2,1)S(1)}, u32[]{:S(2)}, u32[]{:S(2)}) %collective-permute-start.78) | collective-permute-done | bytes 262176 | tf_op jit(solution)/shard_map/ppermute | solution.py:22
  449.3 3.4 collective-permute-start.82
  454.9 3.6 collective-permute-done.83
  460.7 2.9 collective-permute-done.85
  480.5 12.5 %collective-permute-done.90.refs_2_ = bf16[128,1024]{1,0:T(8,128)(2,1)S(1)} collective-permute-done((bf16[128,1024]{1,0:T(8,128)(2,1)S(1)}, bf16[128,1024]{1,0:T(8,128)(2,1)S(1)}, u32[]{:S(2)}, u32[]{:S(2)}) %collective-permute-start.90) | collective-permute-done | bytes 262176 | tf_op jit(solution)/shard_map/ppermute | solution.py:22
  (416 shorter events, 188.5 us)
Async XLA Ops:
  4.8 16.5 %collective-permute-start = (bf16[144,768]{1,0:T(8,128)(2,1)S(1)}, bf16[144,768]{1,0:T(8,128)(2,1)S(1)}, u32[]{:S(2)}, u32[]{:S(2)}) collective-permute-start(bf16[144,768]{1,0:T(8,128)(2,1)S(1)} %get-tuple-element.304), channel_id=1, source_target_pairs={{0,8},{8,0},{16,24},{24,16},{1,9},{9,1},{17,25},{25,17},{2,10},{10... | collective-permute-start | bytes 663560 | tf_op jit(solution)/shard_map/ppermute | solution.py:22
  7.9 24.4 %collective-permute-start.1 = (bf16[144,768]{1,0:T(8,128)(2,1)S(1)}, bf16[144,768]{1,0:T(8,128)(2,1)S(1)}, u32[]{:S(2)}, u32[]{:S(2)}) collective-permute-start(bf16[144,768]{1,0:T(8,128)(2,1)S(1)} %get-tuple-element.305), channel_id=1, source_target_pairs={{0,16},{8,24},{16,0},{24,8},{1,17},{9,25},{17,1},{25,9},{2,18},{10... | collective-permute-start | bytes 663560 | tf_op jit(solution)/shard_map/ppermute | solution.py:22
  10.5 21.8 %collective-permute-start.2 = (bf16[144,768]{1,0:T(8,128)(2,1)S(1)}, bf16[144,768]{1,0:T(8,128)(2,1)S(1)}, u32[]{:S(2)}, u32[]{:S(2)}) collective-permute-start(bf16[144,768]{1,0:T(8,128)(2,1)S(1)} %get-tuple-element.306), channel_id=1, source_target_pairs={{0,24},{8,16},{16,8},{24,0},{1,25},{9,17},{17,9},{25,1},{2,26},{10... | collective-permute-start | bytes 663560 | tf_op jit(solution)/shard_map/ppermute | solution.py:22
  12.1 20.2 %collective-permute-start.3 = (bf16[64,2048]{1,0:T(8,128)(2,1)S(1)}, bf16[64,2048]{1,0:T(8,128)(2,1)S(1)}, u32[]{:S(2)}, u32[]{:S(2)}) collective-permute-start(bf16[64,2048]{1,0:T(8,128)(2,1)S(1)} %get-tuple-element.302.refs_0_.in_ref), channel_id=1, source_target_pairs={{0,24},{8,16},{16,8},{24,0},{1,25},{9,17},{17,9},{25,1},{2,26},{10... | collective-permute-start | bytes 786440 | tf_op jit(solution)/shard_map/ppermute | solution.py:22
  18.6 20.5 %collective-permute-start.4 = (bf16[2,128,768]{2,1,0:T(8,128)(2,1)S(1)}, bf16[2,128,768]{2,1,0:T(8,128)(2,1)S(1)}, u32[]{:S(2)}, u32[]{:S(2)}) collective-permute-start(bf16[2,128,768]{2,1,0:T(8,128)(2,1)S(1)} %get-tuple-element.307), channel_id=1, source_target_pairs={{0,8},{8,0},{16,24},{24,16},{1,9},{9,1},{17,25},{25,17},{2,10},{10... | collective-permute-start | bytes 1179656 | tf_op jit(solution)/shard_map/ppermute | solution.py:22
  39.3 27.6 %collective-permute-start.5 = (bf16[4,144,768]{2,1,0:T(8,128)(2,1)S(1)}, bf16[4,144,768]{2,1,0:T(8,128)(2,1)S(1)}, u32[]{:S(2)}, u32[]{:S(2)}) collective-permute-start(bf16[4,144,768]{2,1,0:T(8,128)(2,1)S(1)} %pad_maximum_fusion.3.refs_0_), channel_id=1, source_target_pairs={{0,4},{4,0},{1,5},{5,1},{2,6},{6,2},{3,7},{7,3},{8,12},{12,8},{9,1... | collective-permute-start | bytes 2654216 | tf_op jit(solution)/shard_map/ppermute | solution.py:22
  40.8 26.0 %collective-permute-start.6 = (bf16[4,144,768]{2,1,0:T(8,128)(2,1)S(1)}, bf16[4,144,768]{2,1,0:T(8,128)(2,1)S(1)}, u32[]{:S(2)}, u32[]{:S(2)}) collective-permute-start(bf16[4,144,768]{2,1,0:T(8,128)(2,1)S(1)} %pad_maximum_fusion.3.refs_0_), channel_id=1, source_target_pairs={{0,2},{2,0},{1,3},{3,1},{4,6},{6,4},{5,7},{7,5},{8,10},{10,8},{9,1... | collective-permute-start | bytes 2654216 | tf_op jit(solution)/shard_map/ppermute | solution.py:22
  40.9 25.9 %collective-permute-start.7 = (bf16[128,2048]{1,0:T(8,128)(2,1)S(1)}, bf16[128,2048]{1,0:T(8,128)(2,1)S(1)}, u32[]{:S(2)}, u32[]{:S(2)}) collective-permute-start(bf16[128,2048]{1,0:T(8,128)(2,1)S(1)} %pad_maximum_fusion.7), channel_id=1, source_target_pairs={{0,8},{8,0},{16,24},{24,16},{1,9},{9,1},{17,25},{25,17},{2,10},{10... | collective-permute-start | bytes 1572872 | tf_op jit(solution)/shard_map/ppermute | solution.py:22
  43.7 23.1 %collective-permute-start.8 = (bf16[2,128,768]{2,1,0:T(8,128)(2,1)S(1)}, bf16[2,128,768]{2,1,0:T(8,128)(2,1)S(1)}, u32[]{:S(2)}, u32[]{:S(2)}) collective-permute-start(bf16[2,128,768]{2,1,0:T(8,128)(2,1)S(1)} %pad_maximum_fusion.10), channel_id=1, source_target_pairs={{0,24},{8,16},{16,8},{24,0},{1,25},{9,17},{17,9},{25,1},{2,26},{10... | collective-permute-start | bytes 1179656 | tf_op jit(solution)/shard_map/ppermute | solution.py:22
  66.8 21.6 %collective-permute-start.9 = (bf16[4,144,768]{2,1,0:T(8,128)(2,1)S(1)}, bf16[4,144,768]{2,1,0:T(8,128)(2,1)S(1)}, u32[]{:S(2)}, u32[]{:S(2)}) collective-permute-start(bf16[4,144,768]{2,1,0:T(8,128)(2,1)S(1)} %collective-permute-done.5.refs_2_), channel_id=1, source_target_pairs={{0,2},{2,0},{1,3},{3,1},{4,6},{6,4},{5,7},{7,5},{8,10},{10,8},{9,1... | collective-permute-start | bytes 2654216 | tf_op jit(solution)/shard_map/ppermute | solution.py:22
  67.0 20.0 %collective-permute-start.10 = (bf16[192,2048]{1,0:T(8,128)(2,1)S(1)}, bf16[192,2048]{1,0:T(8,128)(2,1)S(1)}, u32[]{:S(2)}, u32[]{:S(2)}) collective-permute-start(bf16[192,2048]{1,0:T(8,128)(2,1)S(1)} %pad_maximum_fusion.4), channel_id=1, source_target_pairs={{0,1},{1,0},{2,3},{3,2},{4,5},{5,4},{6,7},{7,6},{8,9},{9,8},{10,11... | collective-permute-start | bytes 2359304 | tf_op jit(solution)/shard_map/ppermute | solution.py:22
  68.7 19.7 %collective-permute-start.11 = (bf16[4,128,768]{2,1,0:T(8,128)(2,1)S(1)}, bf16[4,128,768]{2,1,0:T(8,128)(2,1)S(1)}, u32[]{:S(2)}, u32[]{:S(2)}) collective-permute-start(bf16[4,128,768]{2,1,0:T(8,128)(2,1)S(1)} %pad_maximum_fusion.5.refs_0_), channel_id=1, source_target_pairs={{0,4},{4,0},{1,5},{5,1},{2,6},{6,2},{3,7},{7,3},{8,12},{12,8},{9,1... | collective-permute-start | bytes 2359304 | tf_op jit(solution)/shard_map/ppermute | solution.py:22
  70.6 14.3 %collective-permute-start.13 = (bf16[2,128,512]{2,1,0:T(8,128)(2,1)S(1)}, bf16[2,128,512]{2,1,0:T(8,128)(2,1)S(1)}, u32[]{:S(2)}, u32[]{:S(2)}) collective-permute-start(bf16[2,128,512]{2,1,0:T(8,128)(2,1)S(1)} %get-tuple-element.327), channel_id=1, source_target_pairs={{0,24},{8,16},{16,8},{24,0},{1,25},{9,17},{17,9},{25,1},{2,26},{10... | collective-permute-start | bytes 786440 | tf_op jit(solution)/shard_map/ppermute | solution.py:22
  93.9 22.7 %collective-permute-start.14 = (bf16[2,4,64,768]{3,2,1,0:T(8,128)(2,1)S(1)}, bf16[2,4,64,768]{3,2,1,0:T(8,128)(2,1)S(1)}, u32[]{:S(2)}, u32[]{:S(2)}) collective-permute-start(bf16[2,4,64,768]{3,2,1,0:T(8,128)(2,1)S(1)} %pad_maximum_fusion.6.refs_0_.refs_4_), channel_id=1, source_target_pairs={{0,4},{4,0},{1,5},{5,1},{2,6},{6,2},{3,7},{7,3},{8,12},{12,8},{9,1... | collective-permute-start | bytes 2359304 | tf_op jit(solution)/shard_map/ppermute | solution.py:22
  94.5 14.0 %collective-permute-start.17 = (bf16[2,128,512]{2,1,0:T(8,128)(2,1)S(1)}, bf16[2,128,512]{2,1,0:T(8,128)(2,1)S(1)}, u32[]{:S(2)}, u32[]{:S(2)}) collective-permute-start(bf16[2,128,512]{2,1,0:T(8,128)(2,1)S(1)} %pad_maximum_fusion.11), channel_id=1, source_target_pairs={{0,8},{8,0},{16,24},{24,16},{1,9},{9,1},{17,25},{25,17},{2,10},{10... | collective-permute-start | bytes 786440 | tf_op jit(solution)/shard_map/ppermute | solution.py:22
  96.7 19.9 %collective-permute-start.18 = (bf16[128,1536]{1,0:T(8,128)(2,1)S(1)}, bf16[128,1536]{1,0:T(8,128)(2,1)S(1)}, u32[]{:S(2)}, u32[]{:S(2)}) collective-permute-start(bf16[128,1536]{1,0:T(8,128)(2,1)S(1)} %get-tuple-element.353), channel_id=1, source_target_pairs={{0,16},{8,24},{16,0},{24,8},{1,17},{9,25},{17,1},{25,9},{2,18},{10... | collective-permute-start | bytes 1179656 | tf_op jit(solution)/shard_map/ppermute | solution.py:22
  116.7 18.9 %collective-permute-start.19 = (bf16[4,128,512]{2,1,0:T(8,128)(2,1)S(1)}, bf16[4,128,512]{2,1,0:T(8,128)(2,1)S(1)}, u32[]{:S(2)}, u32[]{:S(2)}) collective-permute-start(bf16[4,128,512]{2,1,0:T(8,128)(2,1)S(1)} %pad_maximum_fusion.8.refs_0_), channel_id=1, source_target_pairs={{0,4},{4,0},{1,5},{5,1},{2,6},{6,2},{3,7},{7,3},{8,12},{12,8},{9,1... | collective-permute-start | bytes 1572872 | tf_op jit(solution)/shard_map/ppermute | solution.py:22
  118.3 17.2 %collective-permute-start.20 = (bf16[128,2048]{1,0:T(8,128)(2,1)S(1)}, bf16[128,2048]{1,0:T(8,128)(2,1)S(1)}, u32[]{:S(2)}, u32[]{:S(2)}) collective-permute-start(bf16[128,2048]{1,0:T(8,128)(2,1)S(1)} %pad_maximum_fusion.9), channel_id=1, source_target_pairs={{0,8},{8,0},{16,24},{24,16},{1,9},{9,1},{17,25},{25,17},{2,10},{10... | collective-permute-start | bytes 1572872 | tf_op jit(solution)/shard_map/ppermute | solution.py:22
  118.4 17.1 %collective-permute-start.21 = (bf16[128,768]{1,0:T(8,128)(2,1)S(1)}, bf16[128,768]{1,0:T(8,128)(2,1)S(1)}, u32[]{:S(2)}, u32[]{:S(2)}) collective-permute-start(bf16[128,768]{1,0:T(8,128)(2,1)S(1)} %slice.225), channel_id=1, source_target_pairs={{0,24},{8,16},{16,8},{24,0},{1,25},{9,17},{17,9},{25,1},{2,26},{10... | collective-permute-start | bytes 589832 | tf_op jit(solution)/shard_map/ppermute | solution.py:22
  141.0 18.0 %collective-permute-start.24 = (bf16[144,2048]{1,0:T(8,128)(2,1)S(1)}, bf16[144,2048]{1,0:T(8,128)(2,1)S(1)}, u32[]{:S(2)}, u32[]{:S(2)}) collective-permute-start(bf16[144,2048]{1,0:T(8,128)(2,1)S(1)} %get-tuple-element.368), channel_id=1, source_target_pairs={{0,1},{1,0},{2,3},{3,2},{4,5},{5,4},{6,7},{7,6},{8,9},{9,8},{10,11... | collective-permute-start | bytes 1769480 | tf_op jit(solution)/shard_map/ppermute | solution.py:22
  144.1 14.8 %collective-permute-start.26 = (bf16[128,1536]{1,0:T(8,128)(2,1)S(1)}, bf16[128,1536]{1,0:T(8,128)(2,1)S(1)}, u32[]{:S(2)}, u32[]{:S(2)}) collective-permute-start(bf16[128,1536]{1,0:T(8,128)(2,1)S(1)} %get-tuple-element.373), channel_id=1, source_target_pairs={{0,8},{8,0},{16,24},{24,16},{1,9},{9,1},{17,25},{25,17},{2,10},{10... | collective-permute-start | bytes 1179656 | tf_op jit(solution)/shard_map/ppermute | solution.py:22
  159.2 16.7 %collective-permute-start.30 = (bf16[4,128,1536]{2,1,0:T(8,128)(2,1)S(1)}, bf16[4,128,1536]{2,1,0:T(8,128)(2,1)S(1)}, u32[]{:S(2)}, u32[]{:S(2)}) collective-permute-start(bf16[4,128,1536]{2,1,0:T(8,128)(2,1)S(1)} %pad_maximum_fusion.1.refs_0_), channel_id=1, source_target_pairs={{0,2},{2,0},{1,3},{3,1},{4,6},{6,4},{5,7},{7,5},{8,10},{10,8},{9,1... | collective-permute-start | bytes 4718600 | tf_op jit(solution)/shard_map/ppermute | solution.py:22
  160.0 15.8 %collective-permute-start.27 = (bf16[144,2048]{1,0:T(8,128)(2,1)S(1)}, bf16[144,2048]{1,0:T(8,128)(2,1)S(1)}, u32[]{:S(2)}, u32[]{:S(2)}) collective-permute-start(bf16[144,2048]{1,0:T(8,128)(2,1)S(1)} %pass_message.2), channel_id=1, source_target_pairs={{0,8},{8,0},{16,24},{24,16},{1,9},{9,1},{17,25},{25,17},{2,10},{10... | collective-permute-start | bytes 1769480 | tf_op jit(solution)/shard_map/ppermute | solution.py:22
  160.4 15.4 %collective-permute-start.28 = (bf16[144,2048]{1,0:T(8,128)(2,1)S(1)}, bf16[144,2048]{1,0:T(8,128)(2,1)S(1)}, u32[]{:S(2)}, u32[]{:S(2)}) collective-permute-start(bf16[144,2048]{1,0:T(8,128)(2,1)S(1)} %get-tuple-element.377), channel_id=1, source_target_pairs={{0,1},{1,0},{2,3},{3,2},{4,5},{5,4},{6,7},{7,6},{8,9},{9,8},{10,11... | collective-permute-start | bytes 1769480 | tf_op jit(solution)/shard_map/ppermute | solution.py:22
  161.9 13.8 %collective-permute-start.29 = (bf16[4,128,512]{2,1,0:T(8,128)(2,1)S(1)}, bf16[4,128,512]{2,1,0:T(8,128)(2,1)S(1)}, u32[]{:S(2)}, u32[]{:S(2)}) collective-permute-start(bf16[4,128,512]{2,1,0:T(8,128)(2,1)S(1)} %slice.284), channel_id=1, source_target_pairs={{0,4},{4,0},{1,5},{5,1},{2,6},{6,2},{3,7},{7,3},{8,12},{12,8},{9,1... | collective-permute-start | bytes 1572872 | tf_op jit(solution)/shard_map/ppermute | solution.py:22
  176.7 13.5 %collective-permute-start.32 = (bf16[4,128,512]{2,1,0:T(8,128)(2,1)S(1)}, bf16[4,128,512]{2,1,0:T(8,128)(2,1)S(1)}, u32[]{:S(2)}, u32[]{:S(2)}) collective-permute-start(bf16[4,128,512]{2,1,0:T(8,128)(2,1)S(1)} %slice.232), channel_id=1, source_target_pairs={{0,4},{4,0},{1,5},{5,1},{2,6},{6,2},{3,7},{7,3},{8,12},{12,8},{9,1... | collective-permute-start | bytes 1572872 | tf_op jit(solution)/shard_map/ppermute | solution.py:22
  191.8 13.2 %collective-permute-start.37 = (bf16[128,2048]{1,0:T(8,128)(2,1)S(1)}, bf16[128,2048]{1,0:T(8,128)(2,1)S(1)}, u32[]{:S(2)}, u32[]{:S(2)}) collective-permute-start(bf16[128,2048]{1,0:T(8,128)(2,1)S(1)} %collective-permute-done.20.refs_2_), channel_id=1, source_target_pairs={{0,1},{1,0},{2,3},{3,2},{4,5},{5,4},{6,7},{7,6},{8,9},{9,8},{10,11... | collective-permute-start | bytes 1572872 | tf_op jit(solution)/shard_map/ppermute | solution.py:22
  205.0 17.5 %collective-permute-start.39 = (bf16[128,2048]{1,0:T(8,128)(2,1)S(1)}, bf16[128,2048]{1,0:T(8,128)(2,1)S(1)}, u32[]{:S(2)}, u32[]{:S(2)}) collective-permute-start(bf16[128,2048]{1,0:T(8,128)(2,1)S(1)} %constant_dynamic-update-slice_fusion.refs_0_), channel_id=1, source_target_pairs={{0,8},{8,0},{16,24},{24,16},{1,9},{9,1},{17,25},{25,17},{2,10},{10... | collective-permute-start | bytes 1572872 | tf_op jit(solution)/shard_map/ppermute | solution.py:22
  255.2 15.8 %collective-permute-start.45 = (bf16[144,2048]{1,0:T(8,128)(2,1)S(1)}, bf16[144,2048]{1,0:T(8,128)(2,1)S(1)}, u32[]{:S(2)}, u32[]{:S(2)}) collective-permute-start(bf16[144,2048]{1,0:T(8,128)(2,1)S(1)} %pass_message.3), channel_id=1, source_target_pairs={{0,8},{8,0},{16,24},{24,16},{1,9},{9,1},{17,25},{25,17},{2,10},{10... | collective-permute-start | bytes 1769480 | tf_op jit(solution)/shard_map/ppermute | solution.py:22
  256.0 15.5 %collective-permute-start.46 = (bf16[144,2048]{1,0:T(8,128)(2,1)S(1)}, bf16[144,2048]{1,0:T(8,128)(2,1)S(1)}, u32[]{:S(2)}, u32[]{:S(2)}) collective-permute-start(bf16[144,2048]{1,0:T(8,128)(2,1)S(1)} %get-tuple-element.439), channel_id=1, source_target_pairs={{0,1},{1,0},{2,3},{3,2},{4,5},{5,4},{6,7},{7,6},{8,9},{9,8},{10,11... | collective-permute-start | bytes 1769480 | tf_op jit(solution)/shard_map/ppermute | solution.py:22
  272.2 17.4 %collective-permute-start.48 = (bf16[80,2048]{1,0:T(8,128)(2,1)S(1)}, bf16[80,2048]{1,0:T(8,128)(2,1)S(1)}, u32[]{:S(2)}, u32[]{:S(2)}) collective-permute-start(bf16[80,2048]{1,0:T(8,128)(2,1)S(1)} %get-tuple-element.447), channel_id=1, source_target_pairs={{0,24},{8,16},{16,8},{24,0},{1,25},{9,17},{17,9},{25,1},{2,26},{10... | collective-permute-start | bytes 983048 | tf_op jit(solution)/shard_map/ppermute | solution.py:22
  274.4 15.2 %collective-permute-start.49 = (bf16[128,2048]{1,0:T(8,128)(2,1)S(1)}, bf16[128,2048]{1,0:T(8,128)(2,1)S(1)}, u32[]{:S(2)}, u32[]{:S(2)}) collective-permute-start(bf16[128,2048]{1,0:T(8,128)(2,1)S(1)} %get-tuple-element.448), channel_id=1, source_target_pairs={{0,1},{1,0},{2,3},{3,2},{4,5},{5,4},{6,7},{7,6},{8,9},{9,8},{10,11... | collective-permute-start | bytes 1572872 | tf_op jit(solution)/shard_map/ppermute | solution.py:22
  293.3 20.1 %collective-permute-start.53 = (bf16[128,2048]{1,0:T(8,128)(2,1)S(1)}, bf16[128,2048]{1,0:T(8,128)(2,1)S(1)}, u32[]{:S(2)}, u32[]{:S(2)}) collective-permute-start(bf16[128,2048]{1,0:T(8,128)(2,1)S(1)} %get-tuple-element.469), channel_id=1, source_target_pairs={{0,1},{1,0},{2,3},{3,2},{4,5},{5,4},{6,7},{7,6},{8,9},{9,8},{10,11... | collective-permute-start | bytes 1572872 | tf_op jit(solution)/shard_map/ppermute | solution.py:22
  295.2 18.2 %collective-permute-start.54 = (bf16[128,2048]{1,0:T(8,128)(2,1)S(1)}, bf16[128,2048]{1,0:T(8,128)(2,1)S(1)}, u32[]{:S(2)}, u32[]{:S(2)}) collective-permute-start(bf16[128,2048]{1,0:T(8,128)(2,1)S(1)} %add_convert_fusion.1), channel_id=1, source_target_pairs={{0,8},{8,0},{16,24},{24,16},{1,9},{9,1},{17,25},{25,17},{2,10},{10... | collective-permute-start | bytes 1572872 | tf_op jit(solution)/shard_map/ppermute | solution.py:22
  295.5 17.9 %collective-permute-start.51 = (bf16[64,2048]{1,0:T(8,128)(2,1)S(1)}, bf16[64,2048]{1,0:T(8,128)(2,1)S(1)}, u32[]{:S(2)}, u32[]{:S(2)}) collective-permute-start(bf16[64,2048]{1,0:T(8,128)(2,1)S(1)} %get-tuple-element.463), channel_id=1, source_target_pairs={{0,24},{8,16},{16,8},{24,0},{1,25},{9,17},{17,9},{25,1},{2,26},{10... | collective-permute-start | bytes 786440 | tf_op jit(solution)/shard_map/ppermute | solution.py:22
  345.9 14.6 %collective-permute-start.61 = (bf16[2,4,64,512]{3,2,1,0:T(8,128)(2,1)S(1)}, bf16[2,4,64,512]{3,2,1,0:T(8,128)(2,1)S(1)}, u32[]{:S(2)}, u32[]{:S(2)}) collective-permute-start(bf16[2,4,64,512]{3,2,1,0:T(8,128)(2,1)S(1)} %bitcast.121), channel_id=1, source_target_pairs={{0,4},{4,0},{1,5},{5,1},{2,6},{6,2},{3,7},{7,3},{8,12},{12,8},{9,1... | collective-permute-start | bytes 1572872 | tf_op jit(solution)/shard_map/ppermute | solution.py:22
  347.5 13.0 %collective-permute-start.62 = (bf16[128,1024]{1,0:T(8,128)(2,1)}, bf16[128,1024]{1,0:T(8,128)(2,1)S(1)}, u32[]{:S(2)}, u32[]{:S(2)}) collective-permute-start(bf16[128,1024]{1,0:T(8,128)(2,1)} %copy-done.54), channel_id=1, source_target_pairs={{0,24},{8,16},{16,8},{24,0},{1,25},{9,17},{17,9},{25,1},{2,26},{10... | collective-permute-start | bytes 786440 | tf_op jit(solution)/shard_map/ppermute | solution.py:22
  372.8 18.7 %collective-permute-start.68 = (bf16[1024,1024]{1,0:T(8,128)(2,1)S(1)}, bf16[1024,1024]{1,0:T(8,128)(2,1)S(1)}, u32[]{:S(2)}, u32[]{:S(2)}) collective-permute-start(bf16[1024,1024]{1,0:T(8,128)(2,1)S(1)} %weight_grads.10), channel_id=1, source_target_pairs={{0,2},{2,0},{1,3},{3,1},{4,6},{6,4},{5,7},{7,5},{8,10},{10,8},{9,1... | collective-permute-start | bytes 6291464 | tf_op jit(solution)/shard_map/ppermute | solution.py:22
  373.0 18.5 %collective-permute-start.65 = (bf16[128,2048]{1,0:T(8,128)(2,1)S(1)}, bf16[128,2048]{1,0:T(8,128)(2,1)S(1)}, u32[]{:S(2)}, u32[]{:S(2)}) collective-permute-start(bf16[128,2048]{1,0:T(8,128)(2,1)S(1)} %get-tuple-element.617), channel_id=1, source_target_pairs={{0,1},{1,0},{2,3},{3,2},{4,5},{5,4},{6,7},{7,6},{8,9},{9,8},{10,11... | collective-permute-start | bytes 1572872 | tf_op jit(solution)/shard_map/ppermute | solution.py:22
  374.2 14.1 %collective-permute-start.69 = (bf16[512,512]{1,0:T(8,128)(2,1)S(1)}, bf16[512,512]{1,0:T(8,128)(2,1)S(1)}, u32[]{:S(2)}, u32[]{:S(2)}) collective-permute-start(bf16[512,512]{1,0:T(8,128)(2,1)S(1)} %slice.263), channel_id=1, source_target_pairs={{0,4},{4,0},{1,5},{5,1},{2,6},{6,2},{3,7},{7,3},{8,12},{12,8},{9,1... | collective-permute-start | bytes 1572872 | tf_op jit(solution)/shard_map/ppermute | solution.py:22
  392.4 20.8 %collective-permute-start.70 = (bf16[128,2048]{1,0:T(8,128)(2,1)S(1)}, bf16[128,2048]{1,0:T(8,128)(2,1)S(1)}, u32[]{:S(2)}, u32[]{:S(2)}) collective-permute-start(bf16[128,2048]{1,0:T(8,128)(2,1)S(1)} %add_convert_fusion), channel_id=1, source_target_pairs={{0,8},{8,0},{16,24},{24,16},{1,9},{9,1},{17,25},{25,17},{2,10},{10... | collective-permute-start | bytes 1572872 | tf_op jit(solution)/shard_map/ppermute | solution.py:22
  395.0 18.2 %collective-permute-start.71 = (bf16[128,2048]{1,0:T(8,128)(2,1)S(1)}, bf16[128,2048]{1,0:T(8,128)(2,1)S(1)}, u32[]{:S(2)}, u32[]{:S(2)}) collective-permute-start(bf16[128,2048]{1,0:T(8,128)(2,1)S(1)} %get-tuple-element.527), channel_id=1, source_target_pairs={{0,1},{1,0},{2,3},{3,2},{4,5},{5,4},{6,7},{7,6},{8,9},{9,8},{10,11... | collective-permute-start | bytes 1572872 | tf_op jit(solution)/shard_map/ppermute | solution.py:22
  398.1 15.1 %collective-permute-start.73 = (bf16[64,2048]{1,0:T(8,128)(2,1)S(1)}, bf16[64,2048]{1,0:T(8,128)(2,1)S(1)}, u32[]{:S(2)}, u32[]{:S(2)}) collective-permute-start(bf16[64,2048]{1,0:T(8,128)(2,1)S(1)} %copy-done.62), channel_id=1, source_target_pairs={{0,24},{8,16},{16,8},{24,0},{1,25},{9,17},{17,9},{25,1},{2,26},{10... | collective-permute-start | bytes 786440 | tf_op jit(solution)/shard_map/ppermute | solution.py:22
  427.0 21.7 %collective-permute-start.81 = (f32[64,2048]{1,0:T(8,128)S(1)}, f32[64,2048]{1,0:T(8,128)S(1)}, u32[]{:S(2)}, u32[]{:S(2)}) collective-permute-start(f32[64,2048]{1,0:T(8,128)S(1)} %fusion.21.own_ref), channel_id=1, source_target_pairs={{0,1},{1,0},{2,3},{3,2},{4,5},{5,4},{6,7},{7,6},{8,9},{9,8},{10,11... | collective-permute-start | bytes 1572872 | tf_op jit(solution)/shard_map/ppermute | solution.py:22
  428.1 20.5 %collective-permute-start.78 = (bf16[128,1024]{1,0:T(8,128)(2,1)S(1)}, bf16[128,1024]{1,0:T(8,128)(2,1)S(1)}, u32[]{:S(2)}, u32[]{:S(2)}) collective-permute-start(bf16[128,1024]{1,0:T(8,128)(2,1)S(1)} %get-tuple-element.561), channel_id=1, source_target_pairs={{0,16},{8,24},{16,0},{24,8},{1,17},{9,25},{17,1},{25,9},{2,18},{10... | collective-permute-start | bytes 786440 | tf_op jit(solution)/shard_map/ppermute | solution.py:22
  431.7 16.9 %collective-permute-start.79 = (bf16[128,1024]{1,0:T(8,128)(2,1)S(1)}, bf16[128,1024]{1,0:T(8,128)(2,1)S(1)}, u32[]{:S(2)}, u32[]{:S(2)}) collective-permute-start(bf16[128,1024]{1,0:T(8,128)(2,1)S(1)} %get-tuple-element.562), channel_id=1, source_target_pairs={{0,24},{8,16},{16,8},{24,0},{1,25},{9,17},{17,9},{25,1},{2,26},{10... | collective-permute-start | bytes 786440 | tf_op jit(solution)/shard_map/ppermute | solution.py:22
  472.2 20.8 %collective-permute-start.90 = (bf16[128,1024]{1,0:T(8,128)(2,1)S(1)}, bf16[128,1024]{1,0:T(8,128)(2,1)S(1)}, u32[]{:S(2)}, u32[]{:S(2)}) collective-permute-start(bf16[128,1024]{1,0:T(8,128)(2,1)S(1)} %copy-done.53), channel_id=1, source_target_pairs={{0,16},{8,24},{16,0},{24,8},{1,17},{9,25},{17,1},{25,9},{2,18},{10... | collective-permute-start | bytes 786440 | tf_op jit(solution)/shard_map/ppermute | solution.py:22
  476.2 16.8 %collective-permute-start.91 = (bf16[128,1024]{1,0:T(8,128)(2,1)S(1)}, bf16[128,1024]{1,0:T(8,128)(2,1)S(1)}, u32[]{:S(2)}, u32[]{:S(2)}) collective-permute-start(bf16[128,1024]{1,0:T(8,128)(2,1)S(1)} %copy-done.51), channel_id=1, source_target_pairs={{0,24},{8,16},{16,8},{24,0},{1,25},{9,17},{17,9},{25,1},{2,26},{10... | collective-permute-start | bytes 786440 | tf_op jit(solution)/shard_map/ppermute | solution.py:22
  (108 other events, 1500.8 us)
